TPU v7x, 128 devices: a whole 4x4x4 slice. The times are simulated.
128 devices in a mesh: dp: 8 (over z, core), tensor: 16 (over y, x).
Axes of the slice: x: 4, y: 4, z: 4, core: 2. Of those that a mesh axis runs over, the one named last changes fastest.
Arguments:
- tokens: bfloat16 [2048, 4096], P('dp', 'tensor'), may hold values from -6 to 6
- gate_pre: bfloat16 [2048, 14336], P('dp', 'tensor'), may hold values from -8 to 8
- up_act: bfloat16 [2048, 14336], P('dp', 'tensor'), may hold values from -6 to 6
- grad_hidden: bfloat16 [2048, 14336], P('dp', 'tensor'), may hold values from -1 to 1
- gate_weight: bfloat16 [4096, 14336], P(None, 'tensor'), may hold values from -0.09375 to 0.09375
- up_weight: bfloat16 [4096, 14336], P(None, 'tensor'), may hold values from -0.09375 to 0.09375
- q_init: float32 [14336, 64], P('tensor'), may hold values from -6 to 6
Outputs:
- grad_input: bfloat16 [2048, 4096], P('dp')
- gate_q: float32 [14336, 64], P('tensor')
- gate_error: bfloat16 [32768, 14336], P('dp', 'tensor')
All inputs are finite; a program needn't handle non-finite values.
Results may differ from a plain program's by a relative error of at most 0.0075.
Values may be sent and summed in bfloat16 or wider, within the bound.
No kernel may reach another device: no remote copies, remote signals or barrier semaphores. Data moves between devices by JAX's collectives and lax.ppermute only.
A program may use at most 128 MiB of HBM per device.

v0:
```python
import jax
import jax.numpy as jnp
from jax import lax
from jax.sharding import PartitionSpec as P


def gram_schmidt(factor):
    highest = lax.Precision.HIGHEST

    def column_step(column_id, orthonormal):
        column = lax.dynamic_slice_in_dim(factor, column_id, 1, 1)
        weights_col = jnp.dot(orthonormal.T, column, precision=highest)
        vector = column - jnp.dot(orthonormal, weights_col, precision=highest)
        vector = vector / jnp.sqrt(jnp.sum(vector * vector))
        return lax.dynamic_update_slice_in_dim(orthonormal, vector, column_id, 1)

    return lax.fori_loop(0, factor.shape[1], column_step, jnp.zeros_like(factor))


def local(tokens, gate_pre, up_act, grad_hidden, gate_weight, up_weight, q_init):
    highest = lax.Precision.HIGHEST
    preact = gate_pre.astype(jnp.float32)
    sigmoid_gate = jax.nn.sigmoid(preact)
    cotangent = grad_hidden.astype(jnp.float32)
    grad_up = (cotangent * preact * sigmoid_gate).astype(jnp.bfloat16)
    grad_gate = (
        cotangent
        * up_act.astype(jnp.float32)
        * sigmoid_gate
        * (1.0 + preact * (1.0 - sigmoid_gate))
    ).astype(jnp.bfloat16)
    contract_last = (((1,), (1,)), ((), ()))
    partial_input = lax.dot_general(
        grad_gate, gate_weight, contract_last, preferred_element_type=jnp.float32
    )
    partial_input = partial_input + lax.dot_general(
        grad_up, up_weight, contract_last, preferred_element_type=jnp.float32
    )
    grad_input = lax.psum(partial_input, "tensor").astype(jnp.bfloat16)
    gradient = lax.dot_general(
        lax.all_gather(tokens, "tensor", axis=1, tiled=True),
        grad_gate,
        (((0,), (0,)), ((), ())),
        preferred_element_type=jnp.float32,
    )
    left_sum = lax.psum(
        jnp.dot(gradient, q_init, precision=highest).astype(jnp.bfloat16), "dp"
    ).astype(jnp.float32)
    orthonormal = gram_schmidt(left_sum)
    right_local = lax.dot_general(
        gradient, orthonormal, (((0,), (0,)), ((), ())), precision=highest
    )
    right_mean = lax.psum(right_local, "dp") / lax.axis_size("dp")
    residual = (gradient - jnp.dot(orthonormal, right_mean.T, precision=highest)).astype(
        jnp.bfloat16
    )
    return (grad_input, right_mean, residual)


def solution(mesh):
    return jax.shard_map(
        local,
        mesh=mesh,
        in_specs=(
            P("dp", "tensor"),
            P("dp", "tensor"),
            P("dp", "tensor"),
            P("dp", "tensor"),
            P(None, "tensor"),
            P(None, "tensor"),
            P("tensor", None),
        ),
        out_specs=(P("dp", None), P("tensor", None), P("dp", "tensor")),
        check_vma=False,
    )
```

profile of v0, /device:TPU:0, one launch (start us, length us, event | category | flops | bytes accessed | tf_op | source)
XLA Modules:
  0.0 507.6 jit_solution(8292397436021914570)
XLA Ops:
  8.0 8.1 %fusion.18 = f32[256,4096]{1,0:T(8,128)} fusion(bf16[4096,896]{1,0:T(8,128)(2,1)} %param.13, bf16[256,896]{1,0:T(8,128)(2,1)} %param.12, bf16[256,896]{1,0:T(8,128)(2,1)} %param.10, bf16[256,896]{1,0:T(8,128)(2,1)} %param.11), kind=kOutput, calls=%fused_computation.28 | convolution fusion | flops 1882030080 | bytes 12910592 | tf_op jit(solution)/shard_map/dot_general | solution.py:33
  16.1 44.0 %all-gather.2.cloned.1.call-done = bf16[256,4096]{1,0:T(8,128)(2,1)} async-done(((bf16[256,256]{1,0:T(8,128)(2,1)}), bf16[256,4096]{1,0:T(8,128)(2,1)}) %all-gather.2.cloned.1.call-update) | async-done | bytes 2097168 | tf_op jit(solution)/shard_map/all_gather | solution.py:41
  60.1 4.0 fusion.16
  64.2 5.2 %copy-done.1 = f32[896,4096]{1,0:T(8,128)} copy-done((f32[896,4096]{1,0:T(8,128)}, f32[896,4096]{1,0:T(8,128)S(1)}, u32[]{:S(2)}) %copy-start.1) | copy-done | bytes 14680088
  69.4 10.6 %convolution_convert_fusion = bf16[4096,64]{0,1:T(8,128)(2,1)} fusion(f32[896,4096]{1,0:T(8,128)S(1)} %fusion.16, f32[896,64]{0,1:T(8,128)S(1)} %copy-done), kind=kOutput, calls=%fused_computation.10 | convolution fusion | flops 2818834432 | bytes 15433728 | tf_op jit(solution)/shard_map/dot_general | solution.py:47
  80.1 8.7 %convolution_add_fusion = f32[256,4096]{1,0:T(8,128)} fusion(f32[256,4096]{1,0:T(8,128)} %fusion.18, bf16[4096,896]{1,0:T(8,128)(2,1)} %param.14, bf16[256,896]{1,0:T(8,128)(2,1)S(1)} %copy-done.3, bf16[256,896]{1,0:T(8,128)(2,1)S(1)} %copy-done.2), kind=kOutput, calls=%fused_computation.9 | convolution fusion | flops 1881931776 | bytes 16646144 | tf_op jit(solution)/shard_map/dot_general | solution.py:36
  88.7 51.7 %all-reduce.4.cloned.1.call-done = bf16[4096,64]{0,1:T(8,128)(2,1)} async-done(((bf16[4096,64]{0,1:T(8,128)(2,1)}), bf16[4096,64]{0,1:T(8,128)(2,1)}) %all-reduce.4.cloned.1.call-update) | async-done | bytes 524304 | tf_op jit(solution)/shard_map/psum | solution.py:46
  141.7 209.6 %while.13 = (s32[]{:T(128)}, f32[4096,64]{0,1:T(8,128)S(1)}, f32[4096,64]{0,1:T(8,128)S(1)}, s32[]{:T(128)}, s32[]{:T(128)}) while((s32[]{:T(128)}, f32[4096,64]{0,1:T(8,128)S(1)}, f32[4096,64]{0,1:T(8,128)S(1)}, s32[]{:T(128)}, s32[]{:T(128)}) %tuple.38), condition=%wide.region_4.0_spmd, body=%wide.region_2.0_spmd.sunk | while | flops 6307841 | bytes 2212441 | solution.py:17
  142.6 1.2 multiply_reduce_fusion.2
  145.9 1.2 multiply_reduce_fusion.2
  149.1 1.2 multiply_reduce_fusion.2
  159.0 1.2 multiply_reduce_fusion.2
  162.2 1.2 multiply_reduce_fusion.2
  165.5 1.2 multiply_reduce_fusion.2
  168.8 1.2 multiply_reduce_fusion.2
  172.1 1.2 multiply_reduce_fusion.2
  178.6 1.2 multiply_reduce_fusion.2
  181.9 1.2 multiply_reduce_fusion.2
  185.2 1.2 multiply_reduce_fusion.2
  188.4 1.2 multiply_reduce_fusion.2
  191.7 1.2 multiply_reduce_fusion.2
  201.5 1.2 multiply_reduce_fusion.2
  204.8 1.2 multiply_reduce_fusion.2
  208.1 1.2 multiply_reduce_fusion.2
  211.4 1.2 multiply_reduce_fusion.2
  221.2 1.2 multiply_reduce_fusion.2
  224.5 1.2 multiply_reduce_fusion.2
  227.7 1.2 multiply_reduce_fusion.2
  231.0 1.2 multiply_reduce_fusion.2
  234.3 1.2 multiply_reduce_fusion.2
  240.8 1.2 multiply_reduce_fusion.2
  244.1 1.2 multiply_reduce_fusion.2
  247.4 1.2 multiply_reduce_fusion.2
  250.7 1.2 multiply_reduce_fusion.2
  253.9 1.2 multiply_reduce_fusion.2
  263.8 1.2 multiply_reduce_fusion.2
  267.0 1.2 multiply_reduce_fusion.2
  270.3 1.2 multiply_reduce_fusion.2
  273.6 1.2 multiply_reduce_fusion.2
  283.4 1.2 multiply_reduce_fusion.2
  286.7 1.2 multiply_reduce_fusion.2
  290.0 1.2 multiply_reduce_fusion.2
  293.3 1.2 multiply_reduce_fusion.2
  296.5 1.2 multiply_reduce_fusion.2
  351.3 18.0 %fusion.20 = f32[896,64]{0,1:T(8,128)} fusion(f32[896,4096]{1,0:T(8,128)} %copy-done.1, f32[4096,64]{0,1:T(8,128)S(1)} %get-tuple-element.67), kind=kOutput, calls=%fused_computation.29 | convolution fusion | flops 2818572288 | bytes 15958016 | tf_op jit(solution)/shard_map/dot_general | solution.py:50
  369.4 103.9 %all-reduce.7 = bf16[256,4096]{1,0:T(8,128)(2,1)} all-reduce(f32[256,4096]{1,0:T(8,128)} %convolution_add_fusion), channel_id=1, replica_groups=mesh['dp'=8,'tensor'=16] {'tensor'}, use_global_device_ids=true, to_apply=%region_0.0 | all-reduce | flops 1048576 | bytes 6291456 | tf_op jit(solution)/shard_map/psum | solution.py:39
  474.2 16.0 %fusion.3 = bf16[4096,896]{0,1:T(8,128)(2,1)} fusion(f32[896,4096]{1,0:T(8,128)} %copy-done.1, f32[4096,64]{0,1:T(8,128)S(1)} %get-tuple-element.67, f32[896,64]{0,1:T(8,128)S(1)} %broadcast_multiply_fusion), kind=kOutput, calls=%fused_computation.8 | convolution fusion | flops 2825912320 | bytes 23298048 | tf_op jit(solution)/shard_map/dot_general | solution.py:54
  490.2 10.8 %copy.14 = bf16[4096,896]{1,0:T(8,128)(2,1)} copy(bf16[4096,896]{0,1:T(8,128)(2,1)} %fusion.3) | data formatting | bytes 14680064
  (241 shorter events, 122.1 us)
Async XLA Ops:
  7.2 62.2 %copy-start = (f32[896,64]{0,1:T(8,128)S(1)}, f32[896,64]{0,1:T(8,128)}, u32[]{:S(2)}) copy-start(f32[896,64]{0,1:T(8,128)} %param.15) | copy-start | bytes 688132
  7.2 53.0 %all-gather.2.cloned.1.call-start = ((), (), s32[]{:S(2)}) async-start(), calls=%async_computation | async-start | bytes 2228224 | tf_op jit(solution)/shard_map/all_gather | solution.py:41
  7.9 52.2 %copy-start.2 = (bf16[256,896]{1,0:T(8,128)(2,1)S(1)}, bf16[256,896]{1,0:T(8,128)(2,1)}, u32[]{:S(2)}) copy-start(bf16[256,896]{1,0:T(8,128)(2,1)} %param.12) | copy-start | bytes 1376260
  7.9 52.2 %copy-start.3 = (bf16[256,896]{1,0:T(8,128)(2,1)S(1)}, bf16[256,896]{1,0:T(8,128)(2,1)}, u32[]{:S(2)}) copy-start(bf16[256,896]{1,0:T(8,128)(2,1)} %param.10) | copy-start | bytes 1376260
  7.9 52.2 %copy-start.5 = (bf16[256,896]{1,0:T(8,128)(2,1)S(1)}, bf16[256,896]{1,0:T(8,128)(2,1)}, u32[]{:S(2)}) copy-start(bf16[256,896]{1,0:T(8,128)(2,1)} %param.11) | copy-start | bytes 1376260
  7.9 132.5 %all-reduce.4.cloned.1.call-start = ((), (), s32[]{:S(2)}) async-start(), calls=%async_computation.1 | async-start | bytes 1048576 | tf_op jit(solution)/shard_map/psum | solution.py:46
  64.2 5.2 %copy-start.1 = (f32[896,4096]{1,0:T(8,128)}, f32[896,4096]{1,0:T(8,128)S(1)}, u32[]{:S(2)}) copy-start(f32[896,4096]{1,0:T(8,128)S(1)} %fusion.16) | copy-start | bytes 44040196
  80.0 393.3 %all-reduce.6.cloned.1.call-start = ((), (), s32[]{:S(2)}) async-start(), calls=%async_computation.2 | async-start | bytes 458752 | tf_op jit(solution)/shard_map/psum | solution.py:53
  474.2 16.0 %copy-start.4 = (f32[896,64]{0,1:T(8,128)}, f32[896,64]{0,1:T(8,128)S(1)}, u32[]{:S(2)}) copy-start(f32[896,64]{0,1:T(8,128)S(1)} %broadcast_multiply_fusion) | copy-start | bytes 688132
Sparse Core Ops, SparseCore 0:
  10.1 49.9 all-gather.1
  80.1 60.3 all-reduce.3
  369.5 57.9 all-reduce.5
where the time goes:
time: 509 us; the launch traced here: 508 us
  matrix products  202 us (40%)
  blocking collectives  104 us (20%)
  waiting for transfers between devices  96.5 us (19%)
  loops' own time  46.3 us (9%)
  local copies, waits for them, and re-layouts  41.2 us (8%)
  between operations  13.8 us (3%)
    psum x1, blocking collectives, local(): grad_input = lax.psum(partial_input, 'tensor').astype(jnp.bfloat16)  104 us
    dot_general x64, matrix products, column_step(): vector = column - jnp.dot(orthonormal, weights_col, precision=highest)  78.6 us
    dot_general x64, matrix products, column_step(): weights_col = jnp.dot(orthonormal.T, column, precision=highest)  58.4 us
    psum x1, waiting for transfers between devices, local(): lax.psum(jnp.dot(gradient, q_init, precision=highest).astype(jnp.bfloat16...  51.7 us
    another operation x1, loops' own time, gram_schmidt(): lax.fori_loop(0, factor.shape[1], column_step, jnp.zeros_like(factor))  46.3 us
    all_gather x1, waiting for transfers between devices, local(): lax.all_gather(tokens, 'tensor', axis=1, tiled=True)  44 us
    dynamic_update_slice x64, local copies, waits for them, and re-layouts, column_step(): return lax.dynamic_update_slice_in_dim(orthonormal, vector, column_id, 1)  25.1 us
    dot_general x1, matrix products, local(): lax.dot_general(gradient, orthonormal, (((0,), (0,)), ((), ())), precisio...  18 us
  transfers between devices with their start and end apart: 3, of which 2 were waited for; matrix products, arithmetic and copies ran while one was open for 3% of the time, Pallas kernels for 0%

commit v1 on v0

v1 whole, which is shorter than its diff:
```python
import jax
import jax.numpy as jnp
from jax import lax
from jax.experimental import pallas as pl
from jax.experimental.pallas import tpu as pltpu
from jax.sharding import PartitionSpec as P

F32 = jnp.float32
BF16 = jnp.bfloat16
SIDE = 4
MIB = 1024 * 1024


def mm(a, b, ca, cb):
    return lax.dot_general(a, b, (((ca,), (cb,)), ((), ())), preferred_element_type=F32)


def mm_exact(a, b, ca, cb):
    return lax.dot_general(
        a, b, (((ca,), (cb,)), ((), ())),
        precision=lax.Precision.HIGHEST, preferred_element_type=F32,
    )


def split_hi_lo(a):
    hi = a.astype(BF16)
    return hi, (a - hi.astype(F32)).astype(BF16)


def vmem():
    return pl.BlockSpec(memory_space=pltpu.VMEM)


def smem():
    return pl.BlockSpec(memory_space=pltpu.SMEM)


def call(kernel, outs, n_in, flops, nbytes, scratch=(), mib=32, scalars=1):
    return pl.pallas_call(
        kernel,
        out_shape=outs,
        in_specs=[smem()] * scalars + [vmem()] * n_in,
        out_specs=jax.tree.map(lambda _: vmem(), outs),
        scratch_shapes=list(scratch),
        compiler_params=pltpu.CompilerParams(vmem_limit_bytes=mib * MIB),
        cost_estimate=pl.CostEstimate(flops=flops, bytes_accessed=nbytes, transcendentals=0),
    )


def shape(*dims, dtype=BF16):
    return jax.ShapeDtypeStruct(dims, dtype)


def gates_kernel(pos, gate_pre, up_act, grad_hidden, q_t, gate, rel, z_t):
    x, y = pos[0], pos[1]
    width = gate_pre.shape[1]
    rows = gate_pre.shape[0] // (SIDE * SIDE)
    for k in range(SIDE):
        for j in range(SIDE):
            src = ((x + k) % SIDE) * SIDE + (y + j) % SIDE
            src = pl.ds(pl.multiple_of(src * rows, rows), rows)
            dst = pl.ds((k * SIDE + j) * rows, rows)
            pre = gate_pre[src, :].astype(F32)
            cot = grad_hidden[src, :].astype(F32)
            sig = 1.0 / (1.0 + jnp.exp(-pre))
            rel[dst, width:] = (cot * pre * sig).astype(BF16)
            grad_gate = (
                cot * up_act[src, :].astype(F32) * sig * (1.0 + pre * (1.0 - sig))
            ).astype(BF16)
            rel[dst, :width] = grad_gate
            gate[src, :] = grad_gate
    q_hi, q_lo = split_hi_lo(q_t[...])
    z = mm(jnp.concatenate([q_hi, q_lo], 0), gate[...], 1, 1)
    r = q_t.shape[0]
    z_hi, z_lo = split_hi_lo(z[:r] + z[r:])
    z_t[:r] = z_hi
    z_t[r:] = z_lo


def partial_kernel(rel, gate_weight, up_weight, *outs):
    width = gate_weight.shape[1]
    acc = mm(rel[:, :width], gate_weight[...], 1, 1)
    acc = acc + mm(rel[:, width:], up_weight[...], 1, 1)
    rows = acc.shape[0] // SIDE
    for k in range(SIDE):
        outs[k][...] = acc[k * rows:(k + 1) * rows].astype(outs[k].dtype)


def partial_input(rel, gate_weight, up_weight):
    tokens, both = rel.shape
    d, width = gate_weight.shape
    block = 512
    rows = tokens // SIDE
    return pl.pallas_call(
        partial_kernel,
        grid=(d // block,),
        in_specs=[
            pl.BlockSpec((tokens, both), lambda i: (0, 0)),
            pl.BlockSpec((block, width), lambda i: (i, 0)),
            pl.BlockSpec((block, width), lambda i: (i, 0)),
        ],
        out_specs=[pl.BlockSpec((rows, block), lambda i: (0, i))] * SIDE,
        out_shape=[shape(rows, d, dtype=F32)] + [shape(rows, d)] * (SIDE - 1),
        compiler_params=pltpu.CompilerParams(vmem_limit_bytes=24 * MIB),
        cost_estimate=pl.CostEstimate(
            flops=2 * tokens * both * d, bytes_accessed=4 * d * width, transcendentals=0
        ),
    )(rel, gate_weight, up_weight)


def sum_split_kernel(own, a, b, c, *outs):
    rows = own.shape[0] // SIDE
    for j in range(SIDE):
        cut = pl.ds(j * rows, rows)
        total = (own[cut, :] + a[cut, :].astype(F32)) + (b[cut, :].astype(F32) + c[cut, :].astype(F32))
        outs[j][...] = total.astype(outs[j].dtype)


def sum_kernel(own, a, b, c, out):
    total = (own[...].astype(F32) + b[...].astype(F32)) + (a[...].astype(F32) + c[...].astype(F32))
    out[...] = total.astype(out.dtype)


def place_kernel(which, pos, own, a, b, c, out):
    rows = own.shape[0]
    for k, block in enumerate((own, a, b, c)):
        at = (pos[which] + SIDE - k) % SIDE
        out[pl.ds(pl.multiple_of(at * rows, rows), rows), :] = block[...]


def left_kernel(pos, z_t, t0, t1, t2, t3, keep, send):
    core = pos[2]
    r = keep.shape[0]
    cols = t0.shape[2]
    for j, stack in enumerate((t0, t1, t2, t3)):
        half, base = j // 2, (j % 2) * SIDE * cols

        def emit(target):
            for k in range(SIDE):
                part = mm(z_t[...], stack[k], 1, 0)
                target[:, base + k * cols:base + (k + 1) * cols] = (
                    part[:r] + part[r:]
                ).astype(target.dtype)

        pl.when(core == half)(lambda: emit(keep))
        pl.when(core != half)(lambda: emit(send))


def right_kernel(pos, mine, other, gate, t0, t1, t2, t3, left, v_t, gram):
    core = pos[2]
    left[core] = mine[...]
    left[1 - core] = other[...]
    r = mine.shape[0]
    cols = t0.shape[2]
    w = jnp.zeros((gate.shape[0], r), F32)
    c = jnp.zeros((r, r), F32)
    for j, stack in enumerate((t0, t1, t2, t3)):
        for k in range(SIDE):
            at = (j % 2) * SIDE * cols + k * cols
            piece = left[j // 2, :, at:at + cols]
            w = w + mm(stack[k], piece, 1, 1)
            c = c + mm(piece, piece, 1, 1)
    gram[...] = c
    w_hi, w_lo = split_hi_lo(w)
    v = mm(jnp.concatenate([w_hi, w_lo], 1), gate[...], 0, 0)
    v_t[...] = v[:r] + v[r:]


def cholesky_kernel(gram, out):
    r = gram.shape[0]
    row_id = lax.broadcasted_iota(jnp.int32, (r, 2 * r), 0)
    lane_id = lax.broadcasted_iota(jnp.int32, (r, 2 * r), 1)
    eye = jnp.where(row_id + r == lane_id, 1.0, 0.0).astype(F32)
    a = jnp.concatenate([gram[...], jnp.zeros((r, r), F32)], 1) + eye
    for k in range(r):
        row = a[k:k + 1, :]
        col = a[:, k:k + 1]
        pivot = a[k:k + 1, k:k + 1]
        scale = jnp.where(row_id[:, :1] > k, col / pivot, 0.0)
        a = a - scale * row
    diag = jnp.sum(jnp.where(row_id == lane_id, a, 0.0), axis=1, keepdims=True)
    out[...] = a[:, r:] / jnp.sqrt(diag)


def residual_kernel(n_dp, slots, pos, v_t, inv, gate, left, t0, t1, t2, t3, gate_q_t, out, right):
    step = pl.program_id(0)
    r = v_t.shape[0]

    @pl.when(step == 0)
    def _():
        q = mm_exact(inv[...], v_t[...], 1, 0) * (1.0 / n_dp)
        gate_q_t[...] = q
        hi, lo = split_hi_lo(-mm_exact(inv[...], q, 0, 0))
        right[:r] = hi
        right[r:] = lo

    j, k = step // SIDE, step % SIDE
    cols = t0.shape[2]
    at = pl.multiple_of((j % 2) * SIDE * cols + k * cols, cols)
    piece = left[j // 2, :, pl.ds(at, cols)]
    low = mm(jnp.concatenate([piece, piece], 0), right[...], 0, 0)
    for n, stack in enumerate((t0, t1, t2, t3)):
        @pl.when(j == n)
        def _():
            out[...] = (mm(stack[k], gate[...], 0, 0) + low).astype(out.dtype)


def residual(slots, v_t, inv, gate, left, stacks, n_dp):
    r, width = v_t.shape
    tokens = gate.shape[0]
    cols = stacks[0].shape[2]
    n = SIDE * SIDE
    whole = lambda a: pl.BlockSpec(a.shape, lambda i, s, nd=a.ndim: (0,) * nd)
    ins = (v_t, inv, gate, left, *stacks)

    def kernel(slots_ref, *refs):
        residual_kernel(n_dp, slots_ref, None, *refs)

    return pl.pallas_call(
        kernel,
        grid_spec=pltpu.PrefetchScalarGridSpec(
            num_scalar_prefetch=1,
            grid=(n,),
            in_specs=[whole(a) for a in ins],
            out_specs=[
                pl.BlockSpec((r, width), lambda i, s: (0, 0)),
                pl.BlockSpec((cols, width), lambda i, s: (s[i], 0)),
            ],
            scratch_shapes=[pltpu.VMEM((2 * r, width), BF16)],
        ),
        out_shape=[shape(r, width, dtype=F32), shape(n * cols, width)],
        compiler_params=pltpu.CompilerParams(vmem_limit_bytes=32 * MIB),
        cost_estimate=pl.CostEstimate(
            flops=2 * n * cols * width * (tokens + 2 * r),
            bytes_accessed=2 * n * cols * width,
            transcendentals=0,
        ),
    )(slots, *ins)


def plane(dx, dy):
    return [
        (y * SIDE + x, ((y + dy) % SIDE) * SIDE + (x + dx) % SIDE)
        for y in range(SIDE)
        for x in range(SIDE)
    ]


def local(tokens, gate_pre, up_act, grad_hidden, gate_weight, up_weight, q_init):
    n_dp = lax.axis_size("dp")
    me = lax.axis_index("tensor")
    x, y = me % SIDE, me // SIDE
    core = lax.axis_index("dp") % 2
    pos = jnp.stack([x, y, core]).astype(jnp.int32)
    steps = jnp.arange(SIDE * SIDE, dtype=jnp.int32)
    slots = ((y - steps // SIDE) % SIDE) * SIDE + (x - steps % SIDE) % SIDE
    t_tok, width = gate_pre.shape
    r = q_init.shape[1]
    d = gate_weight.shape[0]

    def over_x(a, k):
        return lax.ppermute(a, "tensor", plane(k, 0))

    def over_y(a, j):
        return lax.ppermute(a, "tensor", plane(0, j))

    def over_z(a, k):
        return lax.ppermute(a, "dp", [(i, (i + 2 * k) % n_dp) for i in range(n_dp)])

    def over_core(a):
        return lax.ppermute(a, "dp", [(i, i ^ 1) for i in range(n_dp)])

    shifts = (1, 3, 2)

    got = {k: over_x(tokens, k) for k in shifts}
    stack0 = jnp.stack([tokens, got[1], got[2], got[3]])
    far = {j: over_y(stack0, j) for j in shifts}
    stacks = (stack0, far[1], far[2], far[3])

    gate, rel, z_t = call(
        gates_kernel,
        [shape(t_tok, width), shape(t_tok, 2 * width), shape(2 * r, t_tok)],
        4, 2 * t_tok * width * 2 * r, 8 * t_tok * width,
    )(pos, gate_pre, up_act, grad_hidden, q_init.T)

    parts = partial_input(rel, gate_weight, up_weight)
    got = {k: over_x(parts[k], k) for k in shifts}
    sums = call(
        sum_split_kernel,
        [shape(t_tok // 16, d, dtype=F32)] + [shape(t_tok // 16, d)] * 3,
        4, 4 * t_tok * d, 4 * t_tok * d, scalars=0,
    )(parts[0], got[1], got[2], got[3])
    got = {j: over_y(sums[j], j) for j in shifts}
    piece = call(
        sum_kernel, shape(t_tok // 16, d), 4, t_tok * d, t_tok * d, scalars=0
    )(sums[0], got[1], got[2], got[3])
    got = {j: over_y(piece, j) for j in shifts}
    quarter = call(
        lambda *refs: place_kernel(1, *refs), shape(t_tok // 4, d), 4, 0, t_tok * d
    )(pos, piece, got[1], got[2], got[3])
    got = {k: over_x(quarter, k) for k in shifts}
    grad_input = call(
        lambda *refs: place_kernel(0, *refs), shape(t_tok, d), 4, 0, 4 * t_tok * d
    )(pos, quarter, got[1], got[2], got[3])

    keep, send = call(
        left_kernel,
        [shape(r, d // 2, dtype=F32), shape(r, d // 2)],
        5, 2 * t_tok * d * 2 * r, 2 * t_tok * d,
    )(pos, z_t, *stacks)
    pair = (keep + over_core(send).astype(F32)).astype(BF16)
    got = {k: over_z(pair, k) for k in shifts}
    mine = call(sum_kernel, shape(r, d // 2), 4, r * d, 4 * r * d, scalars=0)(
        pair, got[1], got[2], got[3]
    )
    other = over_core(mine)

    left, v_t, gram = call(
        right_kernel,
        [shape(2, r, d // 2), shape(r, width, dtype=F32), shape(r, r, dtype=F32)],
        7, 2 * t_tok * d * r, 2 * t_tok * d,
    )(pos, mine, other, gate, *stacks)
    inv = call(
        cholesky_kernel, shape(r, r, dtype=F32), 1, 10 * MIB, r * r * 4, scalars=0
    )(gram)

    half = r // 2
    keep = lax.dynamic_slice_in_dim(v_t, core * half, half, 0)
    send = lax.dynamic_slice_in_dim(v_t, (1 - core) * half, half, 0)
    pair = keep + over_core(send)
    got = {k: over_z(pair, k) for k in shifts}
    mine = (pair + got[2]) + (got[1] + got[3])
    other = over_core(mine)
    v_sum = jnp.where(
        core == 0, jnp.concatenate([mine, other], 0), jnp.concatenate([other, mine], 0)
    )
    gate_q_t, error = residual(slots.astype(jnp.int32), v_sum, inv, gate, left, stacks, n_dp)
    return (grad_input, gate_q_t.T, error)


def solution(mesh):
    return jax.shard_map(
        local,
        mesh=mesh,
        in_specs=(
            P("dp", "tensor"),
            P("dp", "tensor"),
            P("dp", "tensor"),
            P("dp", "tensor"),
            P(None, "tensor"),
            P(None, "tensor"),
            P("tensor", None),
        ),
        out_specs=(P("dp", None), P("tensor", None), P("dp", "tensor")),
        check_vma=False,
    )
```

time: 509 us -> 160 us (0.31)
  matrix products: 202 us -> 0 us
  blocking collectives: 104 us -> 0 us
  loops' own time: 46.3 us -> 0 us
  starting transfers between devices: 0.12 us -> 44.7 us
  waiting for transfers between devices: 96.5 us -> 59.5 us
  Pallas kernels: 0 us -> 36.3 us
  local copies, waits for them, and re-layouts: 41.2 us -> 15.7 us
  between operations: 13.8 us -> 0.85 us
    dot_general x134 -> x0, matrix products: 202 us -> none  [the longest x64 78.6 us: column_step(): vector = column - jnp.dot(orthonormal, weights_col, precision=highest)]
    psum x1 -> x0, blocking collectives: 104 us -> none  [local(): grad_input = lax.psum(partial_input, 'tensor').astype(jnp.bfloat16)]
    ppermute x0 -> x28, waiting for transfers between devices: none -> 59.5 us  [the longest x9 27.9 us: over_x(): return lax.ppermute(a, 'tensor', plane(k, 0))]
    psum x2 -> x0, waiting for transfers between devices: 51.7 us -> none  [the longest x1 51.7 us: local(): lax.psum(jnp.dot(gradient, q_init, precision=highest).astype(jnp.bfloat16...]
    another operation x1 -> x0, loops' own time: 46.3 us -> none  [gram_schmidt(): lax.fori_loop(0, factor.shape[1], column_step, jnp.zeros_like(factor))]
    ppermute x0 -> x28, starting transfers between devices: none -> 44.7 us  [the longest x9 16.2 us: over_y(): return lax.ppermute(a, 'tensor', plane(0, j))]
    all_gather x1 -> x0, waiting for transfers between devices: 44 us -> none  [local(): lax.all_gather(tokens, 'tensor', axis=1, tiled=True)]
    pallas_call x0 -> x11, Pallas kernels: none -> 36.3 us  [the longest x1 13.4 us: residual(): pl.pallas_call(kernel, grid_spec=pltpu.PrefetchScalarGridSpec(num_scalar_...]
  transfers between devices with their start and end apart: 3 -> 28, of which waited for: 2 -> 15; matrix products, arithmetic and copies ran while one was open for 3% -> 0% of each run, Pallas kernels for 0% -> 14%
where the time goes in v1:
time: 160 us; the launch traced here: 158 us
  waiting for transfers between devices  59.5 us (37%)
  starting transfers between devices  44.7 us (28%)
  Pallas kernels  36.3 us (23%)
  local copies, waits for them, and re-layouts  15.7 us (10%)
    ppermute x9, waiting for transfers between devices, over_x(): return lax.ppermute(a, 'tensor', plane(k, 0))  27.9 us
    ppermute x9, waiting for transfers between devices, over_y(): return lax.ppermute(a, 'tensor', plane(0, j))  17 us
    ppermute x9, starting transfers between devices, over_y(): return lax.ppermute(a, 'tensor', plane(0, j))  16.2 us
    unnamed x26, local copies, waits for them, and re-layouts  15.7 us
    ppermute x9, starting transfers between devices, over_x(): return lax.ppermute(a, 'tensor', plane(k, 0))  14.7 us
    ppermute x6, starting transfers between devices, over_z(): return lax.ppermute(a, 'dp', [(i, (i + 2 * k) % n_dp) for i in range(n_dp)])  13.5 us
    pallas_call x1, Pallas kernels, residual(): pl.pallas_call(kernel, grid_spec=pltpu.PrefetchScalarGridSpec(num_scalar_...  13.4 us
    ppermute x6, waiting for transfers between devices, over_z(): return lax.ppermute(a, 'dp', [(i, (i + 2 * k) % n_dp) for i in range(n_dp)])  13 us
  transfers between devices with their start and end apart: 28, of which 15 were waited for; matrix products, arithmetic and copies ran while one was open for 0% of the time, Pallas kernels for 14%

profile of v1, /device:TPU:0, one launch (start us, length us, event | category | flops | bytes accessed | tf_op | source)
XLA Modules:
  0.0 158.1 jit_solution(6618138891824652018)
XLA Ops:
  0.6 1.6 %collective-permute-start.12 = (bf16[256,256]{1,0:T(8,128)(2,1)}, bf16[256,256]{1,0:T(8,128)(2,1)S(1)}, u32[]{:S(2)}, u32[]{:S(2)}) collective-permute-start(bf16[256,256]{1,0:T(8,128)(2,1)} %param.7), channel_id=1, source_target_pairs={{0,1},{1,2},{2,3},{3,0},{4,5},{5,6},{6,7},{7,4},{8,9},{9,10},{10,1... | collective-permute-start | bytes 393224 | tf_op jit(solution)/shard_map/ppermute | solution.py:262
  2.3 2.7 %collective-permute-start.13 = (bf16[256,256]{1,0:T(8,128)(2,1)}, bf16[256,256]{1,0:T(8,128)(2,1)S(1)}, u32[]{:S(2)}, u32[]{:S(2)}) collective-permute-start(bf16[256,256]{1,0:T(8,128)(2,1)} %param.7), channel_id=1, source_target_pairs={{0,2},{1,3},{2,0},{3,1},{4,6},{5,7},{6,4},{7,5},{8,10},{9,11},{10,... | collective-permute-start | bytes 393224 | tf_op jit(solution)/shard_map/ppermute | solution.py:262
  5.0 1.4 collective-permute-start.14
  7.2 4.0 %collective-permute-done.13 = bf16[256,256]{1,0:T(8,128)(2,1)S(1)} collective-permute-done((bf16[256,256]{1,0:T(8,128)(2,1)}, bf16[256,256]{1,0:T(8,128)(2,1)S(1)}, u32[]{:S(2)}, u32[]{:S(2)}) %collective-permute-start.13) | collective-permute-done | bytes 131104 | tf_op jit(solution)/shard_map/ppermute | solution.py:262
  12.2 1.6 %collective-permute-start.15 = (bf16[4,256,256]{2,1,0:T(8,128)(2,1)S(1)}, bf16[4,256,256]{2,1,0:T(8,128)(2,1)S(1)}, u32[]{:S(2)}, u32[]{:S(2)}) collective-permute-start(bf16[4,256,256]{2,1,0:T(8,128)(2,1)S(1)} %pad_maximum_fusion.t0.refs_4_), channel_id=1, source_target_pairs={{0,4},{1,5},{2,6},{3,7},{4,8},{5,9},{6,10},{7,11},{8,12},{9,13},{1... | collective-permute-start | bytes 1572872 | tf_op jit(solution)/shard_map/ppermute | solution.py:265
  13.9 2.9 %collective-permute-start.16 = (bf16[4,256,256]{2,1,0:T(8,128)(2,1)S(1)}, bf16[4,256,256]{2,1,0:T(8,128)(2,1)S(1)}, u32[]{:S(2)}, u32[]{:S(2)}) collective-permute-start(bf16[4,256,256]{2,1,0:T(8,128)(2,1)S(1)} %pad_maximum_fusion.t0.refs_4_), channel_id=1, source_target_pairs={{0,8},{1,9},{2,10},{3,11},{4,12},{5,13},{6,14},{7,15},{8,0},{9,1},... | collective-permute-start | bytes 1572872 | tf_op jit(solution)/shard_map/ppermute | solution.py:265
  16.8 1.3 collective-permute-start.17
  18.2 1.0 copy-done.5
  19.2 1.0 copy-done.6
  20.2 1.0 copy-done.7
  22.2 1.4 shard_map.94
  23.6 3.6 %collective-permute-done.15.t1.refs_5_ = bf16[4,256,256]{2,1,0:T(8,128)(2,1)S(1)} collective-permute-done((bf16[4,256,256]{2,1,0:T(8,128)(2,1)S(1)}, bf16[4,256,256]{2,1,0:T(8,128)(2,1)S(1)}, u32[]{:S(2)}, u32[]{:S(2)}) %collective-permute-start.15) | collective-permute-done | bytes 524320 | tf_op jit(solution)/shard_map/ppermute | solution.py:265
  27.2 11.5 %collective-permute-done.16.t2.refs_6_ = bf16[4,256,256]{2,1,0:T(8,128)(2,1)S(1)} collective-permute-done((bf16[4,256,256]{2,1,0:T(8,128)(2,1)S(1)}, bf16[4,256,256]{2,1,0:T(8,128)(2,1)S(1)}, u32[]{:S(2)}, u32[]{:S(2)}) %collective-permute-start.16) | collective-permute-done | bytes 524320 | tf_op jit(solution)/shard_map/ppermute | solution.py:265
  38.8 1.5 shard_map.100
  40.4 1.5 collective-permute-done.18
  41.9 2.0 %collective-permute-start.19 = (bf16[64,2048]{1,0:T(8,128)(2,1)S(1)}, bf16[64,2048]{1,0:T(8,128)(2,1)S(1)}, u32[]{:S(2)}, u32[]{:S(2)}) collective-permute-start(bf16[64,2048]{1,0:T(8,128)(2,1)S(1)} %add_convert_fusion.own), channel_id=1, source_target_pairs={{0,32},{16,48},{32,64},{48,80},{64,96},{80,112},{96,0},{112,16},{1... | collective-permute-start | bytes 786440 | tf_op jit(solution)/shard_map/ppermute | solution.py:268
  43.9 3.1 %copy-done = bf16[4096,896]{1,0:T(8,128)(2,1)S(1)} copy-done((bf16[4096,896]{1,0:T(8,128)(2,1)S(1)}, bf16[4096,896]{1,0:T(8,128)(2,1)}, u32[]{:S(2)}) %copy-start) | copy-done | bytes 7340056
  47.0 3.1 %copy-done.1 = bf16[4096,896]{1,0:T(8,128)(2,1)S(1)} copy-done((bf16[4096,896]{1,0:T(8,128)(2,1)S(1)}, bf16[4096,896]{1,0:T(8,128)(2,1)}, u32[]{:S(2)}) %copy-start.1) | copy-done | bytes 7340056
  50.1 6.8 %shard_map.95 = (f32[64,4096]{1,0:T(8,128)S(1)}, bf16[64,4096]{1,0:T(8,128)(2,1)}, bf16[64,4096]{1,0:T(8,128)(2,1)}, bf16[64,4096]{1,0:T(8,128)(2,1)}) custom-call(bf16[256,1792]{1,0:T(8,128)(2,1)S(1)} %get-tuple-element.21.rel, bf16[4096,896]{1,0:T(8,128)(2,1)S(1)} %copy-done, bf16[4096,896]{1,0:T(8,128)(2,1)S(1)} %copy-done.1), custom_call_target="tpu_custom_call" | custom-call | flops 3758096384 | bytes 14680064 | tf_op jit(solution)/shard_map/pallas_call | solution.py:94
  56.9 1.5 collective-permute-start
  58.3 2.5 %collective-permute-start.1 = (bf16[64,4096]{1,0:T(8,128)(2,1)}, bf16[64,4096]{1,0:T(8,128)(2,1)}, u32[]{:S(2)}, u32[]{:S(2)}) collective-permute-start(bf16[64,4096]{1,0:T(8,128)(2,1)} %get-tuple-element.24), channel_id=1, source_target_pairs={{0,2},{1,3},{2,0},{3,1},{4,6},{5,7},{6,4},{7,5},{8,10},{9,11},{10,... | collective-permute-start | bytes 1572872 | tf_op jit(solution)/shard_map/ppermute | solution.py:262
  61.6 3.6 %collective-permute-start.20 = (bf16[64,2048]{1,0:T(8,128)(2,1)S(1)}, bf16[64,2048]{1,0:T(8,128)(2,1)S(1)}, u32[]{:S(2)}, u32[]{:S(2)}) collective-permute-start(bf16[64,2048]{1,0:T(8,128)(2,1)S(1)} %add_convert_fusion.own), channel_id=1, source_target_pairs={{0,64},{16,80},{32,96},{48,112},{64,0},{80,16},{96,32},{112,48},{1... | collective-permute-start | bytes 786440 | tf_op jit(solution)/shard_map/ppermute | solution.py:268
  65.2 1.0 collective-permute-start.21
  66.2 4.5 %collective-permute-done.20.b = bf16[64,2048]{1,0:T(8,128)(2,1)S(1)} collective-permute-done((bf16[64,2048]{1,0:T(8,128)(2,1)S(1)}, bf16[64,2048]{1,0:T(8,128)(2,1)S(1)}, u32[]{:S(2)}, u32[]{:S(2)}) %collective-permute-start.20) | collective-permute-done | bytes 262176 | tf_op jit(solution)/shard_map/ppermute | solution.py:268
  70.6 5.1 %collective-permute-done.21.c = bf16[64,2048]{1,0:T(8,128)(2,1)S(1)} collective-permute-done((bf16[64,2048]{1,0:T(8,128)(2,1)S(1)}, bf16[64,2048]{1,0:T(8,128)(2,1)S(1)}, u32[]{:S(2)}, u32[]{:S(2)}) %collective-permute-start.21) | collective-permute-done | bytes 262176 | tf_op jit(solution)/shard_map/ppermute | solution.py:268
  76.0 8.0 %collective-permute-done.1.b = bf16[64,4096]{1,0:T(8,128)(2,1)} collective-permute-done((bf16[64,4096]{1,0:T(8,128)(2,1)}, bf16[64,4096]{1,0:T(8,128)(2,1)}, u32[]{:S(2)}, u32[]{:S(2)}) %collective-permute-start.1) | collective-permute-done | bytes 524320 | tf_op jit(solution)/shard_map/ppermute | solution.py:262
  84.0 2.2 %shard_map.96 = (f32[16,4096]{1,0:T(8,128)S(1)}, bf16[16,4096]{1,0:T(8,128)(2,1)}, bf16[16,4096]{1,0:T(8,128)(2,1)}, bf16[16,4096]{1,0:T(8,128)(2,1)S(1)}) custom-call(f32[64,4096]{1,0:T(8,128)S(1)} %get-tuple-element.22.own, bf16[64,4096]{1,0:T(8,128)(2,1)} %collective-permute-done.a, bf16[64,4096]{1,0:T(8,128)(2,1)} %collective-permute-done.1.b, ...), custom_call_target="tpu_custom_call" | custom-call | flops 4194304 | bytes 4194304 | tf_op jit(solution)/shard_map/pallas_call | solution.py:288
  86.9 1.2 collective-permute-start.3
  88.1 2.4 %collective-permute-start.4 = (bf16[16,4096]{1,0:T(8,128)(2,1)}, bf16[16,4096]{1,0:T(8,128)(2,1)S(1)}, u32[]{:S(2)}, u32[]{:S(2)}) collective-permute-start(bf16[16,4096]{1,0:T(8,128)(2,1)} %get-tuple-element.28), channel_id=1, source_target_pairs={{0,8},{1,9},{2,10},{3,11},{4,12},{5,13},{6,14},{7,15},{8,0},{9,1},... | collective-permute-start | bytes 393224 | tf_op jit(solution)/shard_map/ppermute | solution.py:265
  90.5 1.6 %collective-permute-start.5 = (bf16[16,4096]{1,0:T(8,128)(2,1)S(1)}, bf16[16,4096]{1,0:T(8,128)(2,1)S(1)}, u32[]{:S(2)}, u32[]{:S(2)}) collective-permute-start(bf16[16,4096]{1,0:T(8,128)(2,1)S(1)} %get-tuple-element.29), channel_id=1, source_target_pairs={{0,12},{1,13},{2,14},{3,15},{4,0},{5,1},{6,2},{7,3},{8,4},{9,5},{1... | collective-permute-start | bytes 393224 | tf_op jit(solution)/shard_map/ppermute | solution.py:265
  92.1 1.0 copy-done.3
  93.1 2.3 %shard_map.102 = (bf16[2,64,2048]{2,1,0:T(8,128)(2,1)S(1)}, f32[64,896]{1,0:T(8,128)S(1)}, f32[64,64]{1,0:T(8,128)S(1)}) custom-call(s32[3]{0:T(128)S(1)} %pad_add_fusion.pos.refs_0_, bf16[64,2048]{1,0:T(8,128)(2,1)S(1)} %shard_map.101.mine, bf16[64,2048]{1,0:T(8,128)(2,1)} %collective-permute-done.22.other, bf16[256,896]{1,0:T(8,128)(2,1)S(1)} %copy-done.3, ...), custom_call_target="tpu_custom_call" | custom-call | flops 134217728 | bytes 2097152 | tf_op jit(solution)/shard_map/pallas_call | solution.py:318
  97.3 1.4 collective-permute-start.6
  98.7 2.6 %collective-permute-start.7 = (bf16[16,4096]{1,0:T(8,128)(2,1)S(1)}, bf16[16,4096]{1,0:T(8,128)(2,1)S(1)}, u32[]{:S(2)}, u32[]{:S(2)}) collective-permute-start(bf16[16,4096]{1,0:T(8,128)(2,1)S(1)} %shard_map.97.refs_1_), channel_id=1, source_target_pairs={{0,8},{1,9},{2,10},{3,11},{4,12},{5,13},{6,14},{7,15},{8,0},{9,1},... | collective-permute-start | bytes 393224 | tf_op jit(solution)/shard_map/ppermute | solution.py:265
  101.3 1.1 collective-permute-start.8
  102.4 3.7 %collective-permute-start.24 = (f32[32,896]{1,0:T(8,128)S(1)}, f32[32,896]{1,0:T(8,128)S(1)}, u32[]{:S(2)}, u32[]{:S(2)}) collective-permute-start(f32[32,896]{1,0:T(8,128)S(1)} %dynamic-slice_add_fusion), channel_id=1, source_target_pairs={{0,64},{16,80},{32,96},{48,112},{64,0},{80,16},{96,32},{112,48},{1... | collective-permute-start | bytes 344072 | tf_op jit(solution)/shard_map/ppermute | solution.py:268
  106.1 1.2 collective-permute-done.6.refs_2_
  108.5 2.1 %collective-permute-start.10 = (bf16[64,4096]{1,0:T(8,128)(2,1)S(1)}, bf16[64,4096]{1,0:T(8,128)(2,1)S(1)}, u32[]{:S(2)}, u32[]{:S(2)}) collective-permute-start(bf16[64,4096]{1,0:T(8,128)(2,1)S(1)} %shard_map.98.refs_1_), channel_id=1, source_target_pairs={{0,2},{1,3},{2,0},{3,1},{4,6},{5,7},{6,4},{7,5},{8,10},{9,11},{10,... | collective-permute-start | bytes 1572872 | tf_op jit(solution)/shard_map/ppermute | solution.py:262
  110.6 2.1 %collective-permute-start.11 = (bf16[64,4096]{1,0:T(8,128)(2,1)S(1)}, bf16[64,4096]{1,0:T(8,128)(2,1)}, u32[]{:S(2)}, u32[]{:S(2)}) collective-permute-start(bf16[64,4096]{1,0:T(8,128)(2,1)S(1)} %shard_map.98.refs_1_), channel_id=1, source_target_pairs={{0,3},{1,0},{2,1},{3,2},{4,7},{5,4},{6,5},{7,6},{8,11},{9,8},{10,9... | collective-permute-start | bytes 1572872 | tf_op jit(solution)/shard_map/ppermute | solution.py:262
  112.7 1.9 %collective-permute-start.25 = (f32[32,896]{1,0:T(8,128)S(1)}, f32[32,896]{1,0:T(8,128)S(1)}, u32[]{:S(2)}, u32[]{:S(2)}) collective-permute-start(f32[32,896]{1,0:T(8,128)S(1)} %dynamic-slice_add_fusion), channel_id=1, source_target_pairs={{0,32},{16,48},{32,64},{48,80},{64,96},{80,112},{96,0},{112,16},{1... | collective-permute-start | bytes 344072 | tf_op jit(solution)/shard_map/ppermute | solution.py:268
  114.6 1.3 collective-permute-start.26
  116.0 2.8 %collective-permute-done.25 = f32[32,896]{1,0:T(8,128)S(1)} collective-permute-done((f32[32,896]{1,0:T(8,128)S(1)}, f32[32,896]{1,0:T(8,128)S(1)}, u32[]{:S(2)}, u32[]{:S(2)}) %collective-permute-start.25) | collective-permute-done | bytes 114720 | tf_op jit(solution)/shard_map/ppermute | solution.py:268
  119.6 5.4 %collective-permute-done.10.refs_3_ = bf16[64,4096]{1,0:T(8,128)(2,1)S(1)} collective-permute-done((bf16[64,4096]{1,0:T(8,128)(2,1)S(1)}, bf16[64,4096]{1,0:T(8,128)(2,1)S(1)}, u32[]{:S(2)}, u32[]{:S(2)}) %collective-permute-start.10) | collective-permute-done | bytes 524320 | tf_op jit(solution)/shard_map/ppermute | solution.py:262
  125.0 9.0 %collective-permute-done.11.refs_4_ = bf16[64,4096]{1,0:T(8,128)(2,1)} collective-permute-done((bf16[64,4096]{1,0:T(8,128)(2,1)S(1)}, bf16[64,4096]{1,0:T(8,128)(2,1)}, u32[]{:S(2)}, u32[]{:S(2)}) %collective-permute-start.11) | collective-permute-done | bytes 524320 | tf_op jit(solution)/shard_map/ppermute | solution.py:262
  134.6 2.7 %shard_map.99 = bf16[256,4096]{1,0:T(8,128)(2,1)} custom-call(s32[3]{0:T(128)S(1)} %pad_add_fusion.pos.refs_0_, bf16[64,4096]{1,0:T(8,128)(2,1)S(1)} %shard_map.98.refs_1_, bf16[64,4096]{1,0:T(8,128)(2,1)} %collective-permute-done.9.refs_2_, bf16[64,4096]{1,0:T(8,128)(2,1)S(1)} %collective-permute-done.10.refs_3_, ...), custom_call_target="tpu_custom_call" | custom-call | bytes 4194304 | tf_op jit(solution)/shard_map/pallas_call | solution.py:302
  137.3 5.4 %shard_map.103.refs_1_ = f32[64,64]{1,0:T(8,128)S(1)} custom-call(f32[64,64]{1,0:T(8,128)S(1)} %get-tuple-element.35.gram), custom_call_target="tpu_custom_call" | custom-call | flops 10485760 | bytes 16384 | tf_op jit(solution)/shard_map/pallas_call | solution.py:323
  143.7 1.0 copy-done.12
  144.8 13.4 %shard_map.104 = (f32[64,896]{1,0:T(8,128)}, bf16[4096,896]{1,0:T(8,128)(2,1)}) custom-call(s32[16]{0:T(128)S(1)} %fusion.1.slots_ref, f32[64,896]{1,0:T(8,128)S(1)} %maximum_select_fusion.refs_0_, f32[64,64]{1,0:T(8,128)S(1)} %shard_map.103.refs_1_, bf16[256,896]{1,0:T(8,128)(2,1)S(1)} %copy-done.4, bf16[2,64,2048]{2,1,0:T(8,128)(2,1)S(1)} %copy-done.12, ...), custom_call_target="tpu_custom_call" | custom-call | flops 2818572288 | bytes 7340032 | tf_op jit(solution)/shard_map/pallas_call | solution.py:219
  (53 shorter events, 10.3 us)
Async XLA Ops:
  0.6 6.6 %collective-permute-start.12 = (bf16[256,256]{1,0:T(8,128)(2,1)}, bf16[256,256]{1,0:T(8,128)(2,1)S(1)}, u32[]{:S(2)}, u32[]{:S(2)}) collective-permute-start(bf16[256,256]{1,0:T(8,128)(2,1)} %param.7), channel_id=1, source_target_pairs={{0,1},{1,2},{2,3},{3,0},{4,5},{5,6},{6,7},{7,4},{8,9},{9,10},{10,1... | collective-permute-start | bytes 393224 | tf_op jit(solution)/shard_map/ppermute | solution.py:262
  2.3 9.0 %collective-permute-start.13 = (bf16[256,256]{1,0:T(8,128)(2,1)}, bf16[256,256]{1,0:T(8,128)(2,1)S(1)}, u32[]{:S(2)}, u32[]{:S(2)}) collective-permute-start(bf16[256,256]{1,0:T(8,128)(2,1)} %param.7), channel_id=1, source_target_pairs={{0,2},{1,3},{2,0},{3,1},{4,6},{5,7},{6,4},{7,5},{8,10},{9,11},{10,... | collective-permute-start | bytes 393224 | tf_op jit(solution)/shard_map/ppermute | solution.py:262
  5.0 6.2 %collective-permute-start.14 = (bf16[256,256]{1,0:T(8,128)(2,1)}, bf16[256,256]{1,0:T(8,128)(2,1)S(1)}, u32[]{:S(2)}, u32[]{:S(2)}) collective-permute-start(bf16[256,256]{1,0:T(8,128)(2,1)} %param.7), channel_id=1, source_target_pairs={{0,3},{1,0},{2,1},{3,2},{4,7},{5,4},{6,5},{7,6},{8,11},{9,8},{10,9... | collective-permute-start | bytes 393224 | tf_op jit(solution)/shard_map/ppermute | solution.py:262
  12.2 15.0 %collective-permute-start.15 = (bf16[4,256,256]{2,1,0:T(8,128)(2,1)S(1)}, bf16[4,256,256]{2,1,0:T(8,128)(2,1)S(1)}, u32[]{:S(2)}, u32[]{:S(2)}) collective-permute-start(bf16[4,256,256]{2,1,0:T(8,128)(2,1)S(1)} %pad_maximum_fusion.t0.refs_4_), channel_id=1, source_target_pairs={{0,4},{1,5},{2,6},{3,7},{4,8},{5,9},{6,10},{7,11},{8,12},{9,13},{1... | collective-permute-start | bytes 1572872 | tf_op jit(solution)/shard_map/ppermute | solution.py:265
  13.9 24.9 %collective-permute-start.16 = (bf16[4,256,256]{2,1,0:T(8,128)(2,1)S(1)}, bf16[4,256,256]{2,1,0:T(8,128)(2,1)S(1)}, u32[]{:S(2)}, u32[]{:S(2)}) collective-permute-start(bf16[4,256,256]{2,1,0:T(8,128)(2,1)S(1)} %pad_maximum_fusion.t0.refs_4_), channel_id=1, source_target_pairs={{0,8},{1,9},{2,10},{3,11},{4,12},{5,13},{6,14},{7,15},{8,0},{9,1},... | collective-permute-start | bytes 1572872 | tf_op jit(solution)/shard_map/ppermute | solution.py:265
  16.8 22.0 %collective-permute-start.17 = (bf16[4,256,256]{2,1,0:T(8,128)(2,1)S(1)}, bf16[4,256,256]{2,1,0:T(8,128)(2,1)S(1)}, u32[]{:S(2)}, u32[]{:S(2)}) collective-permute-start(bf16[4,256,256]{2,1,0:T(8,128)(2,1)S(1)} %pad_maximum_fusion.t0.refs_4_), channel_id=1, source_target_pairs={{0,12},{1,13},{2,14},{3,15},{4,0},{5,1},{6,2},{7,3},{8,4},{9,5},{1... | collective-permute-start | bytes 1572872 | tf_op jit(solution)/shard_map/ppermute | solution.py:265
  18.2 1.0 copy-start.5
  19.2 1.0 copy-start.6
  20.2 1.0 copy-start.7
  21.2 0.9 copy-start.10
  23.6 20.3 %copy-start.2 = (bf16[256,896]{1,0:T(8,128)(2,1)}, bf16[256,896]{1,0:T(8,128)(2,1)S(1)}, u32[]{:S(2)}) copy-start(bf16[256,896]{1,0:T(8,128)(2,1)S(1)} %get-tuple-element.33.gate.refs_2_) | copy-start | bytes 1376260
  40.3 1.6 %collective-permute-start.18 = (bf16[64,2048]{1,0:T(8,128)(2,1)S(1)}, bf16[64,2048]{1,0:T(8,128)(2,1)S(1)}, u32[]{:S(2)}, u32[]{:S(2)}) collective-permute-start(bf16[64,2048]{1,0:T(8,128)(2,1)S(1)} %get-tuple-element.32), channel_id=1, source_target_pairs={{0,16},{16,0},{32,48},{48,32},{64,80},{80,64},{96,112},{112,96},{1... | collective-permute-start | bytes 786440 | tf_op jit(solution)/shard_map/ppermute | solution.py:271
  41.9 23.2 %collective-permute-start.19 = (bf16[64,2048]{1,0:T(8,128)(2,1)S(1)}, bf16[64,2048]{1,0:T(8,128)(2,1)S(1)}, u32[]{:S(2)}, u32[]{:S(2)}) collective-permute-start(bf16[64,2048]{1,0:T(8,128)(2,1)S(1)} %add_convert_fusion.own), channel_id=1, source_target_pairs={{0,32},{16,48},{32,64},{48,80},{64,96},{80,112},{96,0},{112,16},{1... | collective-permute-start | bytes 786440 | tf_op jit(solution)/shard_map/ppermute | solution.py:268
  43.9 3.1 %copy-start = (bf16[4096,896]{1,0:T(8,128)(2,1)S(1)}, bf16[4096,896]{1,0:T(8,128)(2,1)}, u32[]{:S(2)}) copy-start(bf16[4096,896]{1,0:T(8,128)(2,1)} %gate_weight.1) | copy-start | bytes 22020100
  47.0 3.1 %copy-start.1 = (bf16[4096,896]{1,0:T(8,128)(2,1)S(1)}, bf16[4096,896]{1,0:T(8,128)(2,1)}, u32[]{:S(2)}) copy-start(bf16[4096,896]{1,0:T(8,128)(2,1)} %up_weight.1) | copy-start | bytes 22020100
  56.9 19.1 %collective-permute-start = (bf16[64,4096]{1,0:T(8,128)(2,1)}, bf16[64,4096]{1,0:T(8,128)(2,1)}, u32[]{:S(2)}, u32[]{:S(2)}) collective-permute-start(bf16[64,4096]{1,0:T(8,128)(2,1)} %get-tuple-element.23), channel_id=1, source_target_pairs={{0,1},{1,2},{2,3},{3,0},{4,5},{5,6},{6,7},{7,4},{8,9},{9,10},{10,1... | collective-permute-start | bytes 1572872 | tf_op jit(solution)/shard_map/ppermute | solution.py:262
  58.3 25.7 %collective-permute-start.1 = (bf16[64,4096]{1,0:T(8,128)(2,1)}, bf16[64,4096]{1,0:T(8,128)(2,1)}, u32[]{:S(2)}, u32[]{:S(2)}) collective-permute-start(bf16[64,4096]{1,0:T(8,128)(2,1)} %get-tuple-element.24), channel_id=1, source_target_pairs={{0,2},{1,3},{2,0},{3,1},{4,6},{5,7},{6,4},{7,5},{8,10},{9,11},{10,... | collective-permute-start | bytes 1572872 | tf_op jit(solution)/shard_map/ppermute | solution.py:262
  60.8 23.2 %collective-permute-start.2 = (bf16[64,4096]{1,0:T(8,128)(2,1)}, bf16[64,4096]{1,0:T(8,128)(2,1)}, u32[]{:S(2)}, u32[]{:S(2)}) collective-permute-start(bf16[64,4096]{1,0:T(8,128)(2,1)} %get-tuple-element.25), channel_id=1, source_target_pairs={{0,3},{1,0},{2,1},{3,2},{4,7},{5,4},{6,5},{7,6},{8,11},{9,8},{10,9... | collective-permute-start | bytes 1572872 | tf_op jit(solution)/shard_map/ppermute | solution.py:262
  61.6 9.1 %collective-permute-start.20 = (bf16[64,2048]{1,0:T(8,128)(2,1)S(1)}, bf16[64,2048]{1,0:T(8,128)(2,1)S(1)}, u32[]{:S(2)}, u32[]{:S(2)}) collective-permute-start(bf16[64,2048]{1,0:T(8,128)(2,1)S(1)} %add_convert_fusion.own), channel_id=1, source_target_pairs={{0,64},{16,80},{32,96},{48,112},{64,0},{80,16},{96,32},{112,48},{1... | collective-permute-start | bytes 786440 | tf_op jit(solution)/shard_map/ppermute | solution.py:268
  65.2 10.6 %collective-permute-start.21 = (bf16[64,2048]{1,0:T(8,128)(2,1)S(1)}, bf16[64,2048]{1,0:T(8,128)(2,1)S(1)}, u32[]{:S(2)}, u32[]{:S(2)}) collective-permute-start(bf16[64,2048]{1,0:T(8,128)(2,1)S(1)} %add_convert_fusion.own), channel_id=1, source_target_pairs={{0,96},{16,112},{32,0},{48,16},{64,32},{80,48},{96,64},{112,80},{1... | collective-permute-start | bytes 786440 | tf_op jit(solution)/shard_map/ppermute | solution.py:268
  75.9 16.2 %collective-permute-start.22 = (bf16[64,2048]{1,0:T(8,128)(2,1)S(1)}, bf16[64,2048]{1,0:T(8,128)(2,1)}, u32[]{:S(2)}, u32[]{:S(2)}) collective-permute-start(bf16[64,2048]{1,0:T(8,128)(2,1)S(1)} %shard_map.101.mine), channel_id=1, source_target_pairs={{0,16},{16,0},{32,48},{48,32},{64,80},{80,64},{96,112},{112,96},{1... | collective-permute-start | bytes 786440 | tf_op jit(solution)/shard_map/ppermute | solution.py:271
  86.2 0.7 copy-start.8
  86.9 9.4 %collective-permute-start.3 = (bf16[16,4096]{1,0:T(8,128)(2,1)}, bf16[16,4096]{1,0:T(8,128)(2,1)S(1)}, u32[]{:S(2)}, u32[]{:S(2)}) collective-permute-start(bf16[16,4096]{1,0:T(8,128)(2,1)} %get-tuple-element.27), channel_id=1, source_target_pairs={{0,4},{1,5},{2,6},{3,7},{4,8},{5,9},{6,10},{7,11},{8,12},{9,13},{1... | collective-permute-start | bytes 393224 | tf_op jit(solution)/shard_map/ppermute | solution.py:265
  88.1 8.2 %collective-permute-start.4 = (bf16[16,4096]{1,0:T(8,128)(2,1)}, bf16[16,4096]{1,0:T(8,128)(2,1)S(1)}, u32[]{:S(2)}, u32[]{:S(2)}) collective-permute-start(bf16[16,4096]{1,0:T(8,128)(2,1)} %get-tuple-element.28), channel_id=1, source_target_pairs={{0,8},{1,9},{2,10},{3,11},{4,12},{5,13},{6,14},{7,15},{8,0},{9,1},... | collective-permute-start | bytes 393224 | tf_op jit(solution)/shard_map/ppermute | solution.py:265
  90.5 5.8 %collective-permute-start.5 = (bf16[16,4096]{1,0:T(8,128)(2,1)S(1)}, bf16[16,4096]{1,0:T(8,128)(2,1)S(1)}, u32[]{:S(2)}, u32[]{:S(2)}) collective-permute-start(bf16[16,4096]{1,0:T(8,128)(2,1)S(1)} %get-tuple-element.29), channel_id=1, source_target_pairs={{0,12},{1,13},{2,14},{3,15},{4,0},{5,1},{6,2},{7,3},{8,4},{9,5},{1... | collective-permute-start | bytes 393224 | tf_op jit(solution)/shard_map/ppermute | solution.py:265
  92.1 1.0 copy-start.3
  95.4 0.8 copy-start.11
  96.2 6.2 %collective-permute-start.23 = (f32[32,896]{1,0:T(8,128)S(1)}, f32[32,896]{1,0:T(8,128)S(1)}, u32[]{:S(2)}, u32[]{:S(2)}) collective-permute-start(f32[32,896]{1,0:T(8,128)S(1)} %constant_dynamic-slice_fusion), channel_id=1, source_target_pairs={{0,16},{16,0},{32,48},{48,32},{64,80},{80,64},{96,112},{112,96},{1... | collective-permute-start | bytes 344072 | tf_op jit(solution)/shard_map/ppermute | solution.py:271
  96.3 1.0 copy-start.9
  97.3 10.0 %collective-permute-start.6 = (bf16[16,4096]{1,0:T(8,128)(2,1)S(1)}, bf16[16,4096]{1,0:T(8,128)(2,1)S(1)}, u32[]{:S(2)}, u32[]{:S(2)}) collective-permute-start(bf16[16,4096]{1,0:T(8,128)(2,1)S(1)} %shard_map.97.refs_1_), channel_id=1, source_target_pairs={{0,4},{1,5},{2,6},{3,7},{4,8},{5,9},{6,10},{7,11},{8,12},{9,13},{1... | collective-permute-start | bytes 393224 | tf_op jit(solution)/shard_map/ppermute | solution.py:265
  98.7 8.6 %collective-permute-start.7 = (bf16[16,4096]{1,0:T(8,128)(2,1)S(1)}, bf16[16,4096]{1,0:T(8,128)(2,1)S(1)}, u32[]{:S(2)}, u32[]{:S(2)}) collective-permute-start(bf16[16,4096]{1,0:T(8,128)(2,1)S(1)} %shard_map.97.refs_1_), channel_id=1, source_target_pairs={{0,8},{1,9},{2,10},{3,11},{4,12},{5,13},{6,14},{7,15},{8,0},{9,1},... | collective-permute-start | bytes 393224 | tf_op jit(solution)/shard_map/ppermute | solution.py:265
  101.3 6.6 %collective-permute-start.8 = (bf16[16,4096]{1,0:T(8,128)(2,1)S(1)}, bf16[16,4096]{1,0:T(8,128)(2,1)S(1)}, u32[]{:S(2)}, u32[]{:S(2)}) collective-permute-start(bf16[16,4096]{1,0:T(8,128)(2,1)S(1)} %shard_map.97.refs_1_), channel_id=1, source_target_pairs={{0,12},{1,13},{2,14},{3,15},{4,0},{5,1},{6,2},{7,3},{8,4},{9,5},{1... | collective-permute-start | bytes 393224 | tf_op jit(solution)/shard_map/ppermute | solution.py:265
  102.4 12.2 %collective-permute-start.24 = (f32[32,896]{1,0:T(8,128)S(1)}, f32[32,896]{1,0:T(8,128)S(1)}, u32[]{:S(2)}, u32[]{:S(2)}) collective-permute-start(f32[32,896]{1,0:T(8,128)S(1)} %dynamic-slice_add_fusion), channel_id=1, source_target_pairs={{0,64},{16,80},{32,96},{48,112},{64,0},{80,16},{96,32},{112,48},{1... | collective-permute-start | bytes 344072 | tf_op jit(solution)/shard_map/ppermute | solution.py:268
  108.5 16.5 %collective-permute-start.10 = (bf16[64,4096]{1,0:T(8,128)(2,1)S(1)}, bf16[64,4096]{1,0:T(8,128)(2,1)S(1)}, u32[]{:S(2)}, u32[]{:S(2)}) collective-permute-start(bf16[64,4096]{1,0:T(8,128)(2,1)S(1)} %shard_map.98.refs_1_), channel_id=1, source_target_pairs={{0,2},{1,3},{2,0},{3,1},{4,6},{5,7},{6,4},{7,5},{8,10},{9,11},{10,... | collective-permute-start | bytes 1572872 | tf_op jit(solution)/shard_map/ppermute | solution.py:262
  110.6 23.4 %collective-permute-start.11 = (bf16[64,4096]{1,0:T(8,128)(2,1)S(1)}, bf16[64,4096]{1,0:T(8,128)(2,1)}, u32[]{:S(2)}, u32[]{:S(2)}) collective-permute-start(bf16[64,4096]{1,0:T(8,128)(2,1)S(1)} %shard_map.98.refs_1_), channel_id=1, source_target_pairs={{0,3},{1,0},{2,1},{3,2},{4,7},{5,4},{6,5},{7,6},{8,11},{9,8},{10,9... | collective-permute-start | bytes 1572872 | tf_op jit(solution)/shard_map/ppermute | solution.py:262
  112.7 21.9 %collective-permute-start.9 = (bf16[64,4096]{1,0:T(8,128)(2,1)S(1)}, bf16[64,4096]{1,0:T(8,128)(2,1)}, u32[]{:S(2)}, u32[]{:S(2)}) collective-permute-start(bf16[64,4096]{1,0:T(8,128)(2,1)S(1)} %shard_map.98.refs_1_), channel_id=1, source_target_pairs={{0,1},{1,2},{2,3},{3,0},{4,5},{5,6},{6,7},{7,4},{8,9},{9,10},{10,1... | collective-permute-start | bytes 1572872 | tf_op jit(solution)/shard_map/ppermute | solution.py:262
  112.7 6.0 %collective-permute-start.25 = (f32[32,896]{1,0:T(8,128)S(1)}, f32[32,896]{1,0:T(8,128)S(1)}, u32[]{:S(2)}, u32[]{:S(2)}) collective-permute-start(f32[32,896]{1,0:T(8,128)S(1)} %dynamic-slice_add_fusion), channel_id=1, source_target_pairs={{0,32},{16,48},{32,64},{48,80},{64,96},{80,112},{96,0},{112,16},{1... | collective-permute-start | bytes 344072 | tf_op jit(solution)/shard_map/ppermute | solution.py:268
  114.6 4.8 %collective-permute-start.26 = (f32[32,896]{1,0:T(8,128)S(1)}, f32[32,896]{1,0:T(8,128)S(1)}, u32[]{:S(2)}, u32[]{:S(2)}) collective-permute-start(f32[32,896]{1,0:T(8,128)S(1)} %dynamic-slice_add_fusion), channel_id=1, source_target_pairs={{0,96},{16,112},{32,0},{48,16},{64,32},{80,48},{96,64},{112,80},{1... | collective-permute-start | bytes 344072 | tf_op jit(solution)/shard_map/ppermute | solution.py:268
  119.5 23.2 %collective-permute-start.27 = (f32[32,896]{1,0:T(8,128)S(1)}, f32[32,896]{1,0:T(8,128)S(1)}, u32[]{:S(2)}, u32[]{:S(2)}) collective-permute-start(f32[32,896]{1,0:T(8,128)S(1)} %add_add_fusion), channel_id=1, source_target_pairs={{0,16},{16,0},{32,48},{48,32},{64,80},{80,64},{96,112},{112,96},{1... | collective-permute-start | bytes 344072 | tf_op jit(solution)/shard_map/ppermute | solution.py:271
  142.7 1.0 copy-start.4
  143.7 1.0 copy-start.12

commit v2 on v0

v2 whole, which is shorter than its diff:
```python
import jax
import jax.numpy as jnp
from jax import lax
from jax.experimental import pallas as pl
from jax.experimental.pallas import tpu as pltpu
from jax.sharding import PartitionSpec as P

F32 = jnp.float32
BF16 = jnp.bfloat16
SIDE = 4
MIB = 1024 * 1024


def mm(a, b, ca, cb):
    return lax.dot_general(a, b, (((ca,), (cb,)), ((), ())), preferred_element_type=F32)


def mm_exact(a, b, ca, cb):
    return lax.dot_general(
        a, b, (((ca,), (cb,)), ((), ())),
        precision=lax.Precision.HIGHEST, preferred_element_type=F32,
    )


def split_hi_lo(a):
    hi = a.astype(BF16)
    return hi, (a - hi.astype(F32)).astype(BF16)


def vmem():
    return pl.BlockSpec(memory_space=pltpu.VMEM)


def hbm():
    return pl.BlockSpec(memory_space=pl.ANY)


def smem():
    return pl.BlockSpec(memory_space=pltpu.SMEM)


def call(kernel, outs, ins, flops, nbytes, scratch=(), mib=32, pos=None, after=()):
    lead = 0 if pos is None else 1
    several = isinstance(outs, (list, tuple))

    def body(*refs):
        kernel(*refs[:lead + len(ins)], *refs[lead + len(ins) + len(after):])

    specs = [x[0] if isinstance(x, tuple) else vmem() for x in ins]
    arrays = [x[1] if isinstance(x, tuple) else x for x in ins]
    return pl.pallas_call(
        body,
        out_shape=outs,
        in_specs=[smem()] * lead + specs + [hbm()] * len(after),
        out_specs=[vmem()] * len(outs) if several else vmem(),
        scratch_shapes=list(scratch),
        compiler_params=pltpu.CompilerParams(vmem_limit_bytes=mib * MIB),
        cost_estimate=pl.CostEstimate(flops=flops, bytes_accessed=nbytes, transcendentals=0),
    )(*([pos] if lead else []), *arrays, *after)


def shape(*dims, dtype=BF16):
    return jax.ShapeDtypeStruct(dims, dtype)


def gates_kernel(pos, pre_hbm, up_hbm, cot_hbm, q_t, gate, rel, z_t, pre_v, up_v, cot_v, sems):
    copies = [
        pltpu.make_async_copy(src, dst, sems.at[n])
        for n, (src, dst) in enumerate(((pre_hbm, pre_v), (up_hbm, up_v), (cot_hbm, cot_v)))
    ]
    for copy in copies:
        copy.start()
    for copy in copies:
        copy.wait()
    a, b = pos[0], pos[1]
    tokens, width = pre_v.shape
    rows = tokens // (SIDE * SIDE)
    for k in range(SIDE):
        for j in range(SIDE):
            src = ((a + k) % SIDE) * SIDE + (b + j) % SIDE
            src = pl.ds(pl.multiple_of(src * rows, rows), rows)
            dst = pl.ds((k * SIDE + j) * rows, rows)
            pre = pre_v[src, :].astype(F32)
            cot = cot_v[src, :].astype(F32)
            sig = 1.0 / (1.0 + jnp.exp(-pre))
            rel[dst, width:] = (cot * pre * sig).astype(BF16)
            grad_gate = (
                cot * up_v[src, :].astype(F32) * sig * (1.0 + pre * (1.0 - sig))
            ).astype(BF16)
            rel[dst, :width] = grad_gate
            gate[src, :] = grad_gate
    q_hi, q_lo = split_hi_lo(q_t[...])
    z = mm(jnp.concatenate([q_hi, q_lo], 0), gate[...], 1, 1)
    r = q_t.shape[0]
    z_hi, z_lo = split_hi_lo(z[:r] + z[r:])
    z_t[:r] = z_hi
    z_t[r:] = z_lo


def partial_kernel(rel, gate_hbm, up_hbm, o0, o1, o2, o3, gate_v, up_v, sems):
    blocks = sems.shape[0]
    d, width = gate_v.shape
    block = d // blocks

    def copies(i):
        at = pl.ds(pl.multiple_of(i * block, block), block)
        return (
            pltpu.make_async_copy(gate_hbm.at[at], gate_v.at[at], sems.at[i, 0]),
            pltpu.make_async_copy(up_hbm.at[at], up_v.at[at], sems.at[i, 1]),
        )

    for i in range(blocks):
        for copy in copies(i):
            copy.start()

    def step(i, carry):
        for copy in copies(i):
            copy.wait()
        at = pl.ds(pl.multiple_of(i * block, block), block)
        acc = mm(rel[:, :width], gate_v[at, :], 1, 1) + mm(rel[:, width:], up_v[at, :], 1, 1)
        rows = acc.shape[0] // SIDE
        for k, out in enumerate((o0, o1, o2, o3)):
            out[:, at] = acc[k * rows:(k + 1) * rows].astype(out.dtype)
        return carry

    lax.fori_loop(0, blocks, step, 0)


def stack_kernel(own, a, b, c, out):
    for k, block in enumerate((own, a, b, c)):
        out[k] = block[...]


def sum_split_kernel(own, a, b, c, *outs):
    rows = own.shape[0] // SIDE
    for j in range(SIDE):
        cut = pl.ds(j * rows, rows)
        total = (own[cut, :] + a[cut, :].astype(F32)) + (b[cut, :].astype(F32) + c[cut, :].astype(F32))
        outs[j][...] = total.astype(outs[j].dtype)


def sum_kernel(own, a, b, c, out):
    total = (own[...].astype(F32) + b[...].astype(F32)) + (a[...].astype(F32) + c[...].astype(F32))
    out[...] = total.astype(out.dtype)


def add_kernel(one, two, out):
    out[...] = (one[...].astype(F32) + two[...].astype(F32)).astype(out.dtype)


def place_kernel(which, pos, own, a, b, c, out):
    rows = own.shape[0]
    for k, block in enumerate((own, a, b, c)):
        at = (pos[which] + SIDE - k) % SIDE
        out[pl.ds(pl.multiple_of(at * rows, rows), rows), :] = block[...]


def column_block(pos, j, k):
    first, second = (pos[0] + SIDE - k) % SIDE, (pos[1] + SIDE - j) % SIDE
    return jnp.where(pos[2] == 0, second * SIDE + first, first * SIDE + second)


def left_kernel(pos, z_t, t0, t1, t2, t3, keep, send, whole):
    half, r = keep.shape[0], keep.shape[1]
    for j, stack in enumerate((t0, t1, t2, t3)):
        for k in range(SIDE):
            part = mm(z_t[...], stack[k], 1, 0)
            whole[column_block(pos, j, k)] = part[:r] + part[r:]
    keep[...] = whole[pl.ds(pos[2] * half, half)]
    send[...] = whole[pl.ds((1 - pos[2]) * half, half)].astype(send.dtype)


def turn_kernel(pos, t0, t1, t2, t3, out):
    for j, stack in enumerate((t0, t1, t2, t3)):
        for k in range(SIDE):
            out[column_block(pos, j, k)] = stack[k].T


def right_kernel(pos, mine, other, gate, t0, t1, t2, t3, left, keep, send, gram):
    half, r = mine.shape[0], mine.shape[1]
    left[pl.ds(pos[2] * half, half)] = mine[...]
    left[pl.ds((1 - pos[2]) * half, half)] = other[...]
    w = jnp.zeros((gate.shape[0], r), F32)
    c = jnp.zeros((r, r), F32)
    for j, stack in enumerate((t0, t1, t2, t3)):
        for k in range(SIDE):
            piece = left[column_block(pos, j, k)]
            w = w + mm(stack[k], piece, 1, 1)
            c = c + mm(piece, piece, 1, 1)
    gram[...] = c
    w_hi, w_lo = split_hi_lo(w)
    v = mm(jnp.concatenate([w_hi, w_lo], 1), gate[...], 0, 0)
    v = v[:r] + v[r:]
    low, high = v[:r // 2], v[r // 2:]
    keep[...] = jnp.where(pos[2] == 0, low, high)
    send[...] = jnp.where(pos[2] == 0, high, low)


def cholesky_kernel(gram, left, out, left_n):
    r = gram.shape[0]
    row_id = lax.broadcasted_iota(jnp.int32, (r, 2 * r), 0)
    lane_id = lax.broadcasted_iota(jnp.int32, (r, 2 * r), 1)
    eye = jnp.where(row_id + r == lane_id, 1.0, 0.0).astype(F32)
    a = jnp.concatenate([gram[...], jnp.zeros((r, r), F32)], 1) + eye
    for k in range(r):
        row = a[k:k + 1, :]
        col = a[:, k:k + 1]
        pivot = a[k:k + 1, k:k + 1]
        scale = jnp.where(row_id[:, :1] > k, col / pivot, 0.0)
        a = a - scale * row
    diag = jnp.sum(jnp.where(row_id == lane_id, a, 0.0), axis=1, keepdims=True)
    out[...] = a[:, r:] / jnp.sqrt(diag)
    for s in range(left.shape[0]):
        left_n[s] = jnp.concatenate([left[s], left[s]], 0).T


def residual_kernel(n_dp, pos, mine, other, inv, gate, left_n, turned, gate_q_t, out_hbm, right, out, sems):
    low = jnp.where(pos[2] == 0, mine[...], other[...])
    high = jnp.where(pos[2] == 0, other[...], mine[...])
    v_t = jnp.concatenate([low, high], 0)
    tokens = gate.shape[0]
    r = v_t.shape[0]
    q = mm_exact(inv[...], v_t, 1, 0) * (1.0 / n_dp)
    gate_q_t[...] = q
    hi, lo = split_hi_lo(-mm_exact(inv[...], q, 0, 0))
    right[:tokens] = gate[...]
    right[tokens:tokens + r] = hi
    right[tokens + r:] = lo
    blocks = sems.shape[0]
    slots, cols = turned.shape[0], turned.shape[1]
    each = slots // blocks
    rows = each * cols

    def copy(i):
        at = pl.ds(pl.multiple_of(i * rows, rows), rows)
        return pltpu.make_async_copy(out.at[at], out_hbm.at[at], sems.at[i])

    def step(i, carry):
        for e in range(each):
            s = i * each + e
            both = jnp.concatenate([turned[s], left_n[s]], 1)
            at = pl.ds(pl.multiple_of(s * cols, cols), cols)
            out[at, :] = mm(both, right[...], 1, 0).astype(out.dtype)
        copy(i).start()
        return carry

    lax.fori_loop(0, blocks, step, 0)

    def finish(i, carry):
        copy(i).wait()
        return carry

    lax.fori_loop(0, blocks, finish, 0)


def residual(pos, mine, other, inv, gate, left_n, turned, n_dp, after=()):
    tokens, width = gate.shape
    n, cols, twice = left_n.shape
    d = n * cols
    blocks = 8

    def body(*refs):
        residual_kernel(n_dp, *refs[:7], *refs[7 + len(after):])

    return pl.pallas_call(
        body,
        in_specs=[smem()] + [vmem()] * 6 + [hbm()] * len(after),
        out_specs=[vmem(), hbm()],
        out_shape=[shape(twice // 2, width, dtype=F32), shape(d, width)],
        scratch_shapes=[
            pltpu.VMEM((tokens + twice, width), BF16),
            pltpu.VMEM((d, width), BF16),
            pltpu.SemaphoreType.DMA((blocks,)),
        ],
        compiler_params=pltpu.CompilerParams(vmem_limit_bytes=32 * MIB),
        cost_estimate=pl.CostEstimate(
            flops=2 * d * width * (tokens + twice), bytes_accessed=2 * d * width, transcendentals=0
        ),
    )(pos, mine, other, inv, gate, left_n, turned, *after)


def plane(n_dp, first, shift):
    pairs = []
    for i in range(n_dp):
        along_x = (i % 2 == 0) == first
        for y in range(SIDE):
            for x in range(SIDE):
                to = (y, (x + shift) % SIDE) if along_x else ((y + shift) % SIDE, x)
                n = SIDE * SIDE
                pairs.append((i * n + y * SIDE + x, i * n + to[0] * SIDE + to[1]))
    return pairs


def ring_pairs(n_dp, step):
    pairs = []
    for i in range(n_dp):
        z, core = i // 2, i % 2
        partner = z ^ 1 if core == step else SIDE - 1 - z
        pairs.append((i, partner * 2 + core))
    return pairs


def local(tokens, gate_pre, up_act, grad_hidden, gate_weight, up_weight, q_init):
    n_dp = lax.axis_size("dp")
    me = lax.axis_index("tensor")
    x, y = me % SIDE, me // SIDE
    core = lax.axis_index("dp") % 2
    a, b = jnp.where(core == 0, x, y), jnp.where(core == 0, y, x)
    pos = jnp.stack([a, b, core]).astype(jnp.int32)
    t_tok, width = gate_pre.shape
    r = q_init.shape[1]
    d = gate_weight.shape[0]
    n = SIDE * SIDE
    cols = d // n

    def over_first(a, k):
        return lax.ppermute(a, ("dp", "tensor"), plane(n_dp, True, k))

    def over_second(a, j):
        return lax.ppermute(a, ("dp", "tensor"), plane(n_dp, False, j))

    def over_ring(a, step):
        return lax.ppermute(a, "dp", ring_pairs(n_dp, step))

    def over_core(a):
        return lax.ppermute(a, "dp", [(i, i ^ 1) for i in range(n_dp)])

    shifts = (1, 3, 2)
    act = pltpu.VMEM((t_tok, width), BF16)
    weights = pltpu.VMEM((d, width), BF16)

    def add(one, two, out, after=()):
        return call(add_kernel, out, [one, two], 1, 1, after=after)

    got = {k: over_first(tokens, k) for k in shifts}
    gate, rel, z_t = call(
        gates_kernel,
        [shape(t_tok, width), shape(t_tok, 2 * width), shape(2 * r, t_tok)],
        [(hbm(), gate_pre), (hbm(), up_act), (hbm(), grad_hidden), q_init.T],
        20 * t_tok * width, 8 * t_tok * width,
        scratch=[act, act, act, pltpu.SemaphoreType.DMA((3,))], pos=pos,
    )
    stack0 = call(
        stack_kernel, shape(SIDE, t_tok, cols), [tokens, got[1], got[2], got[3]], 1, t_tok * d,
        after=[rel],
    )
    far = {j: over_second(stack0, j) for j in shifts}
    stacks = [stack0, far[1], far[2], far[3]]

    parts = call(
        partial_kernel,
        [shape(t_tok // SIDE, d, dtype=F32)] + [shape(t_tok // SIDE, d)] * 3,
        [rel, (hbm(), gate_weight), (hbm(), up_weight)],
        4 * t_tok * width * d, 4 * d * width,
        scratch=[weights, weights, pltpu.SemaphoreType.DMA((8, 2))], mib=48, after=[stack0],
    )
    got = {k: over_first(parts[k], k) for k in shifts}

    keep, send = call(
        left_kernel,
        [shape(n // 2, r, cols, dtype=F32), shape(n // 2, r, cols)],
        [z_t, *stacks], 2 * t_tok * d * 2 * r, 2 * t_tok * d,
        scratch=[pltpu.VMEM((n, r, cols), F32)], pos=pos, after=[parts[0]],
    )
    part_left = shape(n // 2, r, cols)
    pair = add(keep, over_core(send), part_left)
    near = over_ring(pair, 0)
    sums = call(
        sum_split_kernel,
        [shape(t_tok // n, d, dtype=F32)] + [shape(t_tok // n, d)] * 3,
        [parts[0], got[1], got[2], got[3]], 4 * t_tok * d, 4 * t_tok * d, after=[pair],
    )
    got = {j: over_second(sums[j], j) for j in shifts}
    pair = add(pair, near, part_left, after=[sums[0]])
    near = over_ring(pair, 1)
    turned = call(
        turn_kernel, shape(n, cols, t_tok), stacks, 4 * MIB, 4 * t_tok * d, pos=pos, after=[pair]
    )
    piece = call(
        sum_kernel, shape(t_tok // n, d), [sums[0], got[1], got[2], got[3]],
        t_tok * d, t_tok * d, after=[turned],
    )
    got = {j: over_second(piece, j) for j in shifts}
    mine = add(pair, near, part_left, after=[piece])
    other = over_core(mine)
    left, keep, send, gram = call(
        right_kernel,
        [shape(n, r, cols)] + [shape(r // 2, width, dtype=F32)] * 2 + [shape(r, r, dtype=F32)],
        [mine, other, gate, *stacks], 2 * t_tok * d * r, 2 * t_tok * d, pos=pos,
    )
    part_right = shape(r // 2, width, dtype=F32)
    pair = add(keep, over_core(send), part_right)
    near = over_ring(pair, 0)
    quarter = call(
        lambda *refs: place_kernel(1, *refs), shape(t_tok // SIDE, d),
        [piece, got[1], got[2], got[3]], 1, t_tok * d, pos=pos, after=[pair],
    )
    got = {k: over_first(quarter, k) for k in shifts}
    pair = add(pair, near, part_right, after=[quarter])
    near = over_ring(pair, 1)
    inv, left_n = call(
        cholesky_kernel, [shape(r, r, dtype=F32), shape(n, cols, 2 * r)], [gram, left],
        10 * MIB, 4 * r * d, after=[pair],
    )
    mine = add(pair, near, part_right, after=[inv])
    other = over_core(mine)
    gate_q_t, error = residual(pos, mine, other, inv, gate, left_n, turned, n_dp)
    grad_input = call(
        lambda *refs: place_kernel(0, *refs), shape(t_tok, d),
        [quarter, got[1], got[2], got[3]], 1, 4 * t_tok * d, pos=pos, after=[gate_q_t],
    )
    return (grad_input, gate_q_t.T, error)


def solution(mesh):
    return jax.shard_map(
        local,
        mesh=mesh,
        in_specs=(
            P("dp", "tensor"),
            P("dp", "tensor"),
            P("dp", "tensor"),
            P("dp", "tensor"),
            P(None, "tensor"),
            P(None, "tensor"),
            P("tensor", None),
        ),
        out_specs=(P("dp", None), P("tensor", None), P("dp", "tensor")),
        check_vma=False,
    )
```

time: 509 us -> 96.9 us (0.19)
  matrix products: 202 us -> 0 us
  blocking collectives: 104 us -> 0 us
  waiting for transfers between devices: 96.5 us -> 21.1 us
  loops' own time: 46.3 us -> 0 us
  starting transfers between devices: 0.12 us -> 37 us
  local copies, waits for them, and re-layouts: 41.2 us -> 5.83 us
  Pallas kernels: 0 us -> 30.6 us
  between operations: 13.8 us -> 0.86 us
    dot_general x134 -> x0, matrix products: 202 us -> none  [the longest x64 78.6 us: column_step(): vector = column - jnp.dot(orthonormal, weights_col, precision=highest)]
    psum x1 -> x0, blocking collectives: 104 us -> none  [local(): grad_input = lax.psum(partial_input, 'tensor').astype(jnp.bfloat16)]
    psum x2 -> x0, waiting for transfers between devices: 51.7 us -> none  [the longest x1 51.7 us: local(): lax.psum(jnp.dot(gradient, q_init, precision=highest).astype(jnp.bfloat16...]
    another operation x1 -> x0, loops' own time: 46.3 us -> none  [gram_schmidt(): lax.fori_loop(0, factor.shape[1], column_step, jnp.zeros_like(factor))]
    all_gather x1 -> x0, waiting for transfers between devices: 44 us -> none  [local(): lax.all_gather(tokens, 'tensor', axis=1, tiled=True)]
    ppermute x0 -> x26, starting transfers between devices: none -> 37 us  [the longest x9 17.2 us: over_second(): return lax.ppermute(a, ('dp', 'tensor'), plane(n_dp, False, j))]
    pallas_call x0 -> x18, Pallas kernels: none -> 30.6 us  [the longest x17 22.3 us: call(): pl.pallas_call(body, out_shape=outs, in_specs=[smem()] * lead + specs + [...]
    dynamic_update_slice x64 -> x0, local copies, waits for them, and re-layouts: 25.1 us -> none  [column_step(): return lax.dynamic_update_slice_in_dim(orthonormal, vector, column_id, 1)]
  transfers between devices with their start and end apart: 3 -> 26, of which waited for: 2 -> 13; matrix products, arithmetic and copies ran while one was open for 3% -> 0% of each run, Pallas kernels for 0% -> 28%
where the time goes in v2:
time: 96.9 us; the launch traced here: 95.5 us
  starting transfers between devices  37 us (38%)
  Pallas kernels  30.6 us (32%)
  waiting for transfers between devices  21.1 us (22%)
  local copies, waits for them, and re-layouts  5.83 us (6%)
    pallas_call x17, Pallas kernels, call(): pl.pallas_call(body, out_shape=outs, in_specs=[smem()] * lead + specs + [...  22.3 us
    ppermute x9, starting transfers between devices, over_second(): return lax.ppermute(a, ('dp', 'tensor'), plane(n_dp, False, j))  17.2 us
    ppermute x9, starting transfers between devices, over_first(): return lax.ppermute(a, ('dp', 'tensor'), plane(n_dp, True, k))  12.7 us
    ppermute x9, waiting for transfers between devices, over_second(): return lax.ppermute(a, ('dp', 'tensor'), plane(n_dp, False, j))  12.1 us
    pallas_call x1, Pallas kernels, residual(): pl.pallas_call(body, in_specs=[smem()] + [vmem()] * 6 + [hbm()] * len(aft...  8.29 us
    ppermute x4, starting transfers between devices, over_ring(): return lax.ppermute(a, 'dp', ring_pairs(n_dp, step))  6.63 us
    unnamed x12, local copies, waits for them, and re-layouts  5.83 us
    ppermute x4, waiting for transfers between devices, over_core(): return lax.ppermute(a, 'dp', [(i, i ^ 1) for i in range(n_dp)])  4.36 us
  transfers between devices with their start and end apart: 26, of which 13 were waited for; matrix products, arithmetic and copies ran while one was open for 0% of the time, Pallas kernels for 28%

profile of v2, /device:TPU:0, one launch (start us, length us, event | category | flops | bytes accessed | tf_op | source)
XLA Modules:
  0.0 95.5 jit_solution(14082034220714490293)
XLA Ops:
  0.6 1.6 %collective-permute-start = (bf16[256,256]{1,0:T(8,128)(2,1)}, bf16[256,256]{1,0:T(8,128)(2,1)S(1)}, u32[]{:S(2)}, u32[]{:S(2)}) collective-permute-start(bf16[256,256]{1,0:T(8,128)(2,1)} %refs_0_.1), channel_id=1, source_target_pairs={{0,1},{1,2},{2,3},{3,0},{4,5},{5,6},{6,7},{7,4},{8,9},{9,10},{10,1... | collective-permute-start | bytes 393224 | tf_op jit(solution)/shard_map/ppermute | solution.py:317
  2.3 2.7 %collective-permute-start.1 = (bf16[256,256]{1,0:T(8,128)(2,1)}, bf16[256,256]{1,0:T(8,128)(2,1)S(1)}, u32[]{:S(2)}, u32[]{:S(2)}) collective-permute-start(bf16[256,256]{1,0:T(8,128)(2,1)} %refs_0_.1), channel_id=1, source_target_pairs={{0,2},{1,3},{2,0},{3,1},{4,6},{5,7},{6,4},{7,5},{8,10},{9,11},{10,... | collective-permute-start | bytes 393224 | tf_op jit(solution)/shard_map/ppermute | solution.py:317
  5.0 1.4 %collective-permute-start.2 = (bf16[256,256]{1,0:T(8,128)(2,1)}, bf16[256,256]{1,0:T(8,128)(2,1)S(1)}, u32[]{:S(2)}, u32[]{:S(2)}) collective-permute-start(bf16[256,256]{1,0:T(8,128)(2,1)} %refs_0_.1), channel_id=1, source_target_pairs={{0,3},{1,0},{2,1},{3,2},{4,7},{5,4},{6,5},{7,6},{8,11},{9,8},{10,9... | collective-permute-start | bytes 393224 | tf_op jit(solution)/shard_map/ppermute | solution.py:317
  6.5 1.0 %copy-done = bf16[256,896]{1,0:T(8,128)(2,1)S(1)} copy-done((bf16[256,896]{1,0:T(8,128)(2,1)S(1)}, bf16[256,896]{1,0:T(8,128)(2,1)}, u32[]{:S(2)}) %copy-start) | copy-done | bytes 458776
  7.5 1.0 %copy-done.1 = bf16[256,896]{1,0:T(8,128)(2,1)S(1)} copy-done((bf16[256,896]{1,0:T(8,128)(2,1)S(1)}, bf16[256,896]{1,0:T(8,128)(2,1)}, u32[]{:S(2)}) %copy-start.1) | copy-done | bytes 458776
  8.6 1.0 %copy-done.2 = bf16[256,896]{1,0:T(8,128)(2,1)S(1)} copy-done((bf16[256,896]{1,0:T(8,128)(2,1)S(1)}, bf16[256,896]{1,0:T(8,128)(2,1)}, u32[]{:S(2)}) %copy-start.2) | copy-done | bytes 458776
  9.6 0.9 copy-done.3
  10.5 2.2 %shard_map.94 = (bf16[256,896]{1,0:T(8,128)(2,1)S(1)}, bf16[256,1792]{1,0:T(8,128)(2,1)S(1)}, bf16[128,256]{1,0:T(8,128)(2,1)S(1)}) custom-call(s32[3]{0:T(128)S(1)} %pad_add_fusion.refs_0_, bf16[256,896]{1,0:T(8,128)(2,1)S(1)} %copy-done, bf16[256,896]{1,0:T(8,128)(2,1)S(1)} %copy-done.1, bf16[256,896]{1,0:T(8,128)(2,1)S(1)} %copy-done.2, f32[64,896]{1,0:T(8,128)S(1)} %bitcast.5), custom_call_target="tpu_custom_call" | custom-call | flops 4587520 | bytes 1835008 | tf_op jit(solution)/shard_map/pallas_call | solution.py:51
  12.8 0.9 copy-done.5
  13.7 1.6 %collective-permute-start.6 = (bf16[4,256,256]{2,1,0:T(8,128)(2,1)S(1)}, bf16[4,256,256]{2,1,0:T(8,128)(2,1)S(1)}, u32[]{:S(2)}, u32[]{:S(2)}) collective-permute-start(bf16[4,256,256]{2,1,0:T(8,128)(2,1)S(1)} %shard_map.95.refs_3_.refs_2_.refs_1_.refs_4_), channel_id=1, source_target_pairs={{0,4},{1,5},{2,6},{3,7},{4,8},{5,9},{6,10},{7,11},{8,12},{9,13},{1... | collective-permute-start | bytes 1572872 | tf_op jit(solution)/shard_map/ppermute | solution.py:320
  15.4 2.9 %collective-permute-start.7 = (bf16[4,256,256]{2,1,0:T(8,128)(2,1)S(1)}, bf16[4,256,256]{2,1,0:T(8,128)(2,1)S(1)}, u32[]{:S(2)}, u32[]{:S(2)}) collective-permute-start(bf16[4,256,256]{2,1,0:T(8,128)(2,1)S(1)} %shard_map.95.refs_3_.refs_2_.refs_1_.refs_4_), channel_id=1, source_target_pairs={{0,8},{1,9},{2,10},{3,11},{4,12},{5,13},{6,14},{7,15},{8,0},{9,1},... | collective-permute-start | bytes 1572872 | tf_op jit(solution)/shard_map/ppermute | solution.py:320
  18.3 1.3 %collective-permute-start.8 = (bf16[4,256,256]{2,1,0:T(8,128)(2,1)S(1)}, bf16[4,256,256]{2,1,0:T(8,128)(2,1)S(1)}, u32[]{:S(2)}, u32[]{:S(2)}) collective-permute-start(bf16[4,256,256]{2,1,0:T(8,128)(2,1)S(1)} %shard_map.95.refs_3_.refs_2_.refs_1_.refs_4_), channel_id=1, source_target_pairs={{0,12},{1,13},{2,14},{3,15},{4,0},{5,1},{6,2},{7,3},{8,4},{9,5},{1... | collective-permute-start | bytes 1572872 | tf_op jit(solution)/shard_map/ppermute | solution.py:320
  19.6 7.5 %shard_map.96 = (f32[64,4096]{1,0:T(8,128)S(1)}, bf16[64,4096]{1,0:T(8,128)(2,1)S(1)}, bf16[64,4096]{1,0:T(8,128)(2,1)S(1)}, bf16[64,4096]{1,0:T(8,128)(2,1)S(1)}) custom-call(bf16[256,1792]{1,0:T(8,128)(2,1)S(1)} %get-tuple-element.24.refs_4_.refs_0_, bf16[4096,896]{1,0:T(8,128)(2,1)} %refs_1_.3, bf16[4096,896]{1,0:T(8,128)(2,1)} %refs_2_.3, ...), custom_call_target="tpu_custom_call" | custom-call | flops 3758096384 | bytes 14680064 | tf_op jit(solution)/shard_map/pallas_call | solution.py:51
  27.1 0.7 collective-permute-start.3
  27.8 0.9 collective-permute-start.4
  28.7 1.8 %collective-permute-start.5 = (bf16[64,4096]{1,0:T(8,128)(2,1)S(1)}, bf16[64,4096]{1,0:T(8,128)(2,1)S(1)}, u32[]{:S(2)}, u32[]{:S(2)}) collective-permute-start(bf16[64,4096]{1,0:T(8,128)(2,1)S(1)} %get-tuple-element.28), channel_id=1, source_target_pairs={{0,3},{1,0},{2,1},{3,2},{4,7},{5,4},{6,5},{7,6},{8,11},{9,8},{10,9... | collective-permute-start | bytes 1572872 | tf_op jit(solution)/shard_map/ppermute | solution.py:317
  30.6 3.7 %collective-permute-done.7.refs_4_.refs_3_.refs_6_ = bf16[4,256,256]{2,1,0:T(8,128)(2,1)S(1)} collective-permute-done((bf16[4,256,256]{2,1,0:T(8,128)(2,1)S(1)}, bf16[4,256,256]{2,1,0:T(8,128)(2,1)S(1)}, u32[]{:S(2)}, u32[]{:S(2)}) %collective-permute-start.7) | collective-permute-done | bytes 524320 | tf_op jit(solution)/shard_map/ppermute | solution.py:320
  34.3 1.7 %collective-permute-done.8.refs_5_.refs_4_.refs_7_ = bf16[4,256,256]{2,1,0:T(8,128)(2,1)S(1)} collective-permute-done((bf16[4,256,256]{2,1,0:T(8,128)(2,1)S(1)}, bf16[4,256,256]{2,1,0:T(8,128)(2,1)S(1)}, u32[]{:S(2)}, u32[]{:S(2)}) %collective-permute-start.8) | collective-permute-done | bytes 524320 | tf_op jit(solution)/shard_map/ppermute | solution.py:320
  36.0 1.0 %shard_map.97 = (f32[8,64,256]{2,1,0:T(8,128)S(1)}, bf16[8,64,256]{2,1,0:T(8,128)(2,1)S(1)}) custom-call(s32[3]{0:T(128)S(1)} %pad_add_fusion.refs_0_, bf16[128,256]{1,0:T(8,128)(2,1)S(1)} %get-tuple-element.29.refs_1_, bf16[4,256,256]{2,1,0:T(8,128)(2,1)S(1)} %shard_map.95.refs_3_.refs_2_.refs_1_.refs_4_, ...), custom_call_target="tpu_custom_call" | custom-call | flops 268435456 | bytes 2097152 | tf_op jit(solution)/shard_map/pallas_call | solution.py:51
  37.2 1.5 %collective-permute-done.9.refs_1_ = bf16[8,64,256]{2,1,0:T(8,128)(2,1)S(1)} collective-permute-done((bf16[8,64,256]{2,1,0:T(8,128)(2,1)S(1)}, bf16[8,64,256]{2,1,0:T(8,128)(2,1)S(1)}, u32[]{:S(2)}, u32[]{:S(2)}) %collective-permute-start.9) | collective-permute-done | bytes 262176 | tf_op jit(solution)/shard_map/ppermute | solution.py:326
  38.7 2.0 %collective-permute-start.13 = (bf16[8,64,256]{2,1,0:T(8,128)(2,1)S(1)}, bf16[8,64,256]{2,1,0:T(8,128)(2,1)S(1)}, u32[]{:S(2)}, u32[]{:S(2)}) collective-permute-start(bf16[8,64,256]{2,1,0:T(8,128)(2,1)S(1)} %shard_map.98.refs_4_.refs_0_), channel_id=1, source_target_pairs={{0,32},{16,112},{32,0},{48,80},{64,96},{80,48},{96,64},{112,16},{1... | collective-permute-start | bytes 786440 | tf_op jit(solution)/shard_map/ppermute | solution.py:323
  40.7 2.5 %collective-permute-done.3.refs_1_ = bf16[64,4096]{1,0:T(8,128)(2,1)S(1)} collective-permute-done((bf16[64,4096]{1,0:T(8,128)(2,1)S(1)}, bf16[64,4096]{1,0:T(8,128)(2,1)S(1)}, u32[]{:S(2)}, u32[]{:S(2)}) %collective-permute-start.3) | collective-permute-done | bytes 524320 | tf_op jit(solution)/shard_map/ppermute | solution.py:317
  43.2 0.9 collective-permute-done.5.refs_3_
  44.3 0.9 collective-permute-done.13.refs_1_
  45.3 4.1 %collective-permute-start.17 = (bf16[8,64,256]{2,1,0:T(8,128)(2,1)S(1)}, bf16[8,64,256]{2,1,0:T(8,128)(2,1)S(1)}, u32[]{:S(2)}, u32[]{:S(2)}) collective-permute-start(bf16[8,64,256]{2,1,0:T(8,128)(2,1)S(1)} %shard_map.100.refs_5_.refs_0_), channel_id=1, source_target_pairs={{0,96},{16,48},{32,64},{48,16},{64,32},{80,112},{96,0},{112,80},{1... | collective-permute-start | bytes 786440 | tf_op jit(solution)/shard_map/ppermute | solution.py:323
  49.4 4.0 %collective-permute-start.10 = (bf16[16,4096]{1,0:T(8,128)(2,1)S(1)}, bf16[16,4096]{1,0:T(8,128)(2,1)S(1)}, u32[]{:S(2)}, u32[]{:S(2)}) collective-permute-start(bf16[16,4096]{1,0:T(8,128)(2,1)S(1)} %get-tuple-element.33), channel_id=1, source_target_pairs={{0,4},{1,5},{2,6},{3,7},{4,8},{5,9},{6,10},{7,11},{8,12},{9,13},{1... | collective-permute-start | bytes 393224 | tf_op jit(solution)/shard_map/ppermute | solution.py:320
  53.4 1.3 %collective-permute-start.11 = (bf16[16,4096]{1,0:T(8,128)(2,1)S(1)}, bf16[16,4096]{1,0:T(8,128)(2,1)S(1)}, u32[]{:S(2)}, u32[]{:S(2)}) collective-permute-start(bf16[16,4096]{1,0:T(8,128)(2,1)S(1)} %get-tuple-element.34), channel_id=1, source_target_pairs={{0,8},{1,9},{2,10},{3,11},{4,12},{5,13},{6,14},{7,15},{8,0},{9,1},... | collective-permute-start | bytes 393224 | tf_op jit(solution)/shard_map/ppermute | solution.py:320
  54.7 1.4 %collective-permute-start.12 = (bf16[16,4096]{1,0:T(8,128)(2,1)S(1)}, bf16[16,4096]{1,0:T(8,128)(2,1)S(1)}, u32[]{:S(2)}, u32[]{:S(2)}) collective-permute-start(bf16[16,4096]{1,0:T(8,128)(2,1)S(1)} %get-tuple-element.35), channel_id=1, source_target_pairs={{0,12},{1,13},{2,14},{3,15},{4,0},{5,1},{6,2},{7,3},{8,4},{9,5},{1... | collective-permute-start | bytes 393224 | tf_op jit(solution)/shard_map/ppermute | solution.py:320
  56.0 1.1 %shard_map.101.refs_4_.refs_6_ = bf16[16,256,256]{2,1,0:T(8,128)(2,1)S(1)} custom-call(s32[3]{0:T(128)S(1)} %pad_add_fusion.refs_0_, bf16[4,256,256]{2,1,0:T(8,128)(2,1)S(1)} %shard_map.95.refs_3_.refs_2_.refs_1_.refs_4_, bf16[4,256,256]{2,1,0:T(8,128)(2,1)S(1)} %collective-permute-done.6.refs_3_.refs_2_.refs_5_, ...), custom_call_target="tpu_custom_call" | custom-call | flops 4194304 | bytes 4194304 | tf_op jit(solution)/shard_map/pallas_call | solution.py:51
  57.2 2.7 %collective-permute-done.11.refs_2_ = bf16[16,4096]{1,0:T(8,128)(2,1)S(1)} collective-permute-done((bf16[16,4096]{1,0:T(8,128)(2,1)S(1)}, bf16[16,4096]{1,0:T(8,128)(2,1)S(1)}, u32[]{:S(2)}, u32[]{:S(2)}) %collective-permute-start.11) | collective-permute-done | bytes 131104 | tf_op jit(solution)/shard_map/ppermute | solution.py:320
  60.1 1.5 %collective-permute-done.18.refs_2_ = bf16[8,64,256]{2,1,0:T(8,128)(2,1)S(1)} collective-permute-done((bf16[8,64,256]{2,1,0:T(8,128)(2,1)S(1)}, bf16[8,64,256]{2,1,0:T(8,128)(2,1)S(1)}, u32[]{:S(2)}, u32[]{:S(2)}) %collective-permute-start.18) | collective-permute-done | bytes 262176 | tf_op jit(solution)/shard_map/ppermute | solution.py:326
  61.6 1.9 %shard_map.104 = (bf16[16,64,256]{2,1,0:T(8,128)(2,1)S(1)}, f32[32,896]{1,0:T(8,128)S(1)}, f32[32,896]{1,0:T(8,128)S(1)}, f32[64,64]{1,0:T(8,128)S(1)}) custom-call(s32[3]{0:T(128)S(1)} %pad_add_fusion.refs_0_, bf16[8,64,256]{2,1,0:T(8,128)(2,1)S(1)} %shard_map.103.refs_1_, bf16[8,64,256]{2,1,0:T(8,128)(2,1)S(1)} %collective-permute-done.18.refs_2_, ...), custom_call_target="tpu_custom_call" | custom-call | flops 134217728 | bytes 2097152 | tf_op jit(solution)/shard_map/pallas_call | solution.py:51
  63.7 1.4 %collective-permute-start.14 = (bf16[16,4096]{1,0:T(8,128)(2,1)S(1)}, bf16[16,4096]{1,0:T(8,128)(2,1)S(1)}, u32[]{:S(2)}, u32[]{:S(2)}) collective-permute-start(bf16[16,4096]{1,0:T(8,128)(2,1)S(1)} %shard_map.102.refs_2_.refs_1_), channel_id=1, source_target_pairs={{0,4},{1,5},{2,6},{3,7},{4,8},{5,9},{6,10},{7,11},{8,12},{9,13},{1... | collective-permute-start | bytes 393224 | tf_op jit(solution)/shard_map/ppermute | solution.py:320
  65.0 2.5 %collective-permute-start.15 = (bf16[16,4096]{1,0:T(8,128)(2,1)S(1)}, bf16[16,4096]{1,0:T(8,128)(2,1)S(1)}, u32[]{:S(2)}, u32[]{:S(2)}) collective-permute-start(bf16[16,4096]{1,0:T(8,128)(2,1)S(1)} %shard_map.102.refs_2_.refs_1_), channel_id=1, source_target_pairs={{0,8},{1,9},{2,10},{3,11},{4,12},{5,13},{6,14},{7,15},{8,0},{9,1},... | collective-permute-start | bytes 393224 | tf_op jit(solution)/shard_map/ppermute | solution.py:320
  67.5 0.8 collective-permute-start.16
  68.5 1.4 %collective-permute-done.14.refs_2_ = bf16[16,4096]{1,0:T(8,128)(2,1)S(1)} collective-permute-done((bf16[16,4096]{1,0:T(8,128)(2,1)S(1)}, bf16[16,4096]{1,0:T(8,128)(2,1)S(1)}, u32[]{:S(2)}, u32[]{:S(2)}) %collective-permute-start.14) | collective-permute-done | bytes 131104 | tf_op jit(solution)/shard_map/ppermute | solution.py:320
  69.9 2.0 %collective-permute-done.15.refs_3_ = bf16[16,4096]{1,0:T(8,128)(2,1)S(1)} collective-permute-done((bf16[16,4096]{1,0:T(8,128)(2,1)S(1)}, bf16[16,4096]{1,0:T(8,128)(2,1)S(1)}, u32[]{:S(2)}, u32[]{:S(2)}) %collective-permute-start.15) | collective-permute-done | bytes 131104 | tf_op jit(solution)/shard_map/ppermute | solution.py:320
  71.9 0.6 collective-permute-done.16.refs_4_
  72.5 0.6 shard_map.106.refs_2_.refs_1_
  73.1 0.7 collective-permute-start.20
  73.7 0.8 collective-permute-start.21
  74.5 2.0 %collective-permute-start.22 = (bf16[64,4096]{1,0:T(8,128)(2,1)S(1)}, bf16[64,4096]{1,0:T(8,128)(2,1)S(1)}, u32[]{:S(2)}, u32[]{:S(2)}) collective-permute-start(bf16[64,4096]{1,0:T(8,128)(2,1)S(1)} %shard_map.106.refs_2_.refs_1_), channel_id=1, source_target_pairs={{0,3},{1,0},{2,1},{3,2},{4,7},{5,4},{6,5},{7,6},{8,11},{9,8},{10,9... | collective-permute-start | bytes 1572872 | tf_op jit(solution)/shard_map/ppermute | solution.py:317
  76.5 0.4 collective-permute-start.24
  77.0 5.4 %shard_map.108 = (f32[64,64]{1,0:T(8,128)S(1)}, bf16[16,256,128]{2,1,0:T(8,128)(2,1)S(1)}) custom-call(f32[64,64]{1,0:T(8,128)S(1)} %get-tuple-element.39.refs_0_, bf16[16,64,256]{2,1,0:T(8,128)(2,1)S(1)} %get-tuple-element.40.refs_1_, f32[32,896]{1,0:T(8,128)S(1)} %shard_map.107.refs_2_.refs_0_), custom_call_target="tpu_custom_call" | custom-call | flops 10485760 | bytes 1048576 | tf_op jit(solution)/shard_map/pallas_call | solution.py:51
  82.9 1.3 %collective-permute-done.25.refs_2_ = f32[32,896]{1,0:T(8,128)S(1)} collective-permute-done((f32[32,896]{1,0:T(8,128)S(1)}, f32[32,896]{1,0:T(8,128)S(1)}, u32[]{:S(2)}, u32[]{:S(2)}) %collective-permute-start.25) | collective-permute-done | bytes 114720 | tf_op jit(solution)/shard_map/ppermute | solution.py:326
  84.2 8.3 %shard_map.110 = (f32[64,896]{1,0:T(8,128)}, bf16[4096,896]{1,0:T(8,128)(2,1)}) custom-call(s32[3]{0:T(128)S(1)} %pad_add_fusion.refs_0_, f32[32,896]{1,0:T(8,128)S(1)} %shard_map.109.refs_1_, f32[32,896]{1,0:T(8,128)S(1)} %collective-permute-done.25.refs_2_, f32[64,64]{1,0:T(8,128)S(1)} %get-tuple-element.41.refs_2_.refs_3_, ...), custom_call_target="tpu_custom_call" | custom-call | flops 2818572288 | bytes 7340032 | tf_op jit(solution)/shard_map/pallas_call | solution.py:265
  92.6 0.9 copy-done.4
  93.5 2.0 %shard_map.111 = bf16[256,4096]{1,0:T(8,128)(2,1)} custom-call(s32[3]{0:T(128)S(1)} %pad_add_fusion.refs_0_, bf16[64,4096]{1,0:T(8,128)(2,1)S(1)} %shard_map.106.refs_2_.refs_1_, bf16[64,4096]{1,0:T(8,128)(2,1)S(1)} %collective-permute-done.20.refs_2_, bf16[64,4096]{1,0:T(8,128)(2,1)S(1)} %collective-permute-done.21.refs_3_, ...), custom_call_target="tpu_custom_call" | custom-call | flops 1 | bytes 4194304 | tf_op jit(solution)/shard_map/pallas_call | solution.py:51
  (35 shorter events, 1.6 us)
Async XLA Ops:
  0.6 12.1 %collective-permute-start = (bf16[256,256]{1,0:T(8,128)(2,1)}, bf16[256,256]{1,0:T(8,128)(2,1)S(1)}, u32[]{:S(2)}, u32[]{:S(2)}) collective-permute-start(bf16[256,256]{1,0:T(8,128)(2,1)} %refs_0_.1), channel_id=1, source_target_pairs={{0,1},{1,2},{2,3},{3,0},{4,5},{5,6},{6,7},{7,4},{8,9},{9,10},{10,1... | collective-permute-start | bytes 393224 | tf_op jit(solution)/shard_map/ppermute | solution.py:317
  2.3 10.5 %collective-permute-start.1 = (bf16[256,256]{1,0:T(8,128)(2,1)}, bf16[256,256]{1,0:T(8,128)(2,1)S(1)}, u32[]{:S(2)}, u32[]{:S(2)}) collective-permute-start(bf16[256,256]{1,0:T(8,128)(2,1)} %refs_0_.1), channel_id=1, source_target_pairs={{0,2},{1,3},{2,0},{3,1},{4,6},{5,7},{6,4},{7,5},{8,10},{9,11},{10,... | collective-permute-start | bytes 393224 | tf_op jit(solution)/shard_map/ppermute | solution.py:317
  5.0 7.8 %collective-permute-start.2 = (bf16[256,256]{1,0:T(8,128)(2,1)}, bf16[256,256]{1,0:T(8,128)(2,1)S(1)}, u32[]{:S(2)}, u32[]{:S(2)}) collective-permute-start(bf16[256,256]{1,0:T(8,128)(2,1)} %refs_0_.1), channel_id=1, source_target_pairs={{0,3},{1,0},{2,1},{3,2},{4,7},{5,4},{6,5},{7,6},{8,11},{9,8},{10,9... | collective-permute-start | bytes 393224 | tf_op jit(solution)/shard_map/ppermute | solution.py:317
  6.5 1.0 %copy-start = (bf16[256,896]{1,0:T(8,128)(2,1)S(1)}, bf16[256,896]{1,0:T(8,128)(2,1)}, u32[]{:S(2)}) copy-start(bf16[256,896]{1,0:T(8,128)(2,1)} %refs_1_.2) | copy-start | bytes 1376260
  7.5 1.0 %copy-start.1 = (bf16[256,896]{1,0:T(8,128)(2,1)S(1)}, bf16[256,896]{1,0:T(8,128)(2,1)}, u32[]{:S(2)}) copy-start(bf16[256,896]{1,0:T(8,128)(2,1)} %refs_2_.2) | copy-start | bytes 1376260
  8.6 1.0 %copy-start.2 = (bf16[256,896]{1,0:T(8,128)(2,1)S(1)}, bf16[256,896]{1,0:T(8,128)(2,1)}, u32[]{:S(2)}) copy-start(bf16[256,896]{1,0:T(8,128)(2,1)} %refs_3_.1) | copy-start | bytes 1376260
  9.6 0.9 copy-start.3
  12.8 0.9 copy-start.5
  13.7 15.0 %collective-permute-start.6 = (bf16[4,256,256]{2,1,0:T(8,128)(2,1)S(1)}, bf16[4,256,256]{2,1,0:T(8,128)(2,1)S(1)}, u32[]{:S(2)}, u32[]{:S(2)}) collective-permute-start(bf16[4,256,256]{2,1,0:T(8,128)(2,1)S(1)} %shard_map.95.refs_3_.refs_2_.refs_1_.refs_4_), channel_id=1, source_target_pairs={{0,4},{1,5},{2,6},{3,7},{4,8},{5,9},{6,10},{7,11},{8,12},{9,13},{1... | collective-permute-start | bytes 1572872 | tf_op jit(solution)/shard_map/ppermute | solution.py:320
  15.4 19.0 %collective-permute-start.7 = (bf16[4,256,256]{2,1,0:T(8,128)(2,1)S(1)}, bf16[4,256,256]{2,1,0:T(8,128)(2,1)S(1)}, u32[]{:S(2)}, u32[]{:S(2)}) collective-permute-start(bf16[4,256,256]{2,1,0:T(8,128)(2,1)S(1)} %shard_map.95.refs_3_.refs_2_.refs_1_.refs_4_), channel_id=1, source_target_pairs={{0,8},{1,9},{2,10},{3,11},{4,12},{5,13},{6,14},{7,15},{8,0},{9,1},... | collective-permute-start | bytes 1572872 | tf_op jit(solution)/shard_map/ppermute | solution.py:320
  18.3 17.8 %collective-permute-start.8 = (bf16[4,256,256]{2,1,0:T(8,128)(2,1)S(1)}, bf16[4,256,256]{2,1,0:T(8,128)(2,1)S(1)}, u32[]{:S(2)}, u32[]{:S(2)}) collective-permute-start(bf16[4,256,256]{2,1,0:T(8,128)(2,1)S(1)} %shard_map.95.refs_3_.refs_2_.refs_1_.refs_4_), channel_id=1, source_target_pairs={{0,12},{1,13},{2,14},{3,15},{4,0},{5,1},{6,2},{7,3},{8,4},{9,5},{1... | collective-permute-start | bytes 1572872 | tf_op jit(solution)/shard_map/ppermute | solution.py:320
  27.1 16.1 %collective-permute-start.3 = (bf16[64,4096]{1,0:T(8,128)(2,1)S(1)}, bf16[64,4096]{1,0:T(8,128)(2,1)S(1)}, u32[]{:S(2)}, u32[]{:S(2)}) collective-permute-start(bf16[64,4096]{1,0:T(8,128)(2,1)S(1)} %get-tuple-element.26), channel_id=1, source_target_pairs={{0,1},{1,2},{2,3},{3,0},{4,5},{5,6},{6,7},{7,4},{8,9},{9,10},{10,1... | collective-permute-start | bytes 1572872 | tf_op jit(solution)/shard_map/ppermute | solution.py:317
  27.8 15.4 %collective-permute-start.4 = (bf16[64,4096]{1,0:T(8,128)(2,1)S(1)}, bf16[64,4096]{1,0:T(8,128)(2,1)S(1)}, u32[]{:S(2)}, u32[]{:S(2)}) collective-permute-start(bf16[64,4096]{1,0:T(8,128)(2,1)S(1)} %get-tuple-element.27), channel_id=1, source_target_pairs={{0,2},{1,3},{2,0},{3,1},{4,6},{5,7},{6,4},{7,5},{8,10},{9,11},{10,... | collective-permute-start | bytes 1572872 | tf_op jit(solution)/shard_map/ppermute | solution.py:317
  28.7 15.4 %collective-permute-start.5 = (bf16[64,4096]{1,0:T(8,128)(2,1)S(1)}, bf16[64,4096]{1,0:T(8,128)(2,1)S(1)}, u32[]{:S(2)}, u32[]{:S(2)}) collective-permute-start(bf16[64,4096]{1,0:T(8,128)(2,1)S(1)} %get-tuple-element.28), channel_id=1, source_target_pairs={{0,3},{1,0},{2,1},{3,2},{4,7},{5,4},{6,5},{7,6},{8,11},{9,8},{10,9... | collective-permute-start | bytes 1572872 | tf_op jit(solution)/shard_map/ppermute | solution.py:317
  37.1 1.6 %collective-permute-start.9 = (bf16[8,64,256]{2,1,0:T(8,128)(2,1)S(1)}, bf16[8,64,256]{2,1,0:T(8,128)(2,1)S(1)}, u32[]{:S(2)}, u32[]{:S(2)}) collective-permute-start(bf16[8,64,256]{2,1,0:T(8,128)(2,1)S(1)} %get-tuple-element.31), channel_id=1, source_target_pairs={{0,16},{16,0},{32,48},{48,32},{64,80},{80,64},{96,112},{112,96},{1... | collective-permute-start | bytes 786440 | tf_op jit(solution)/shard_map/ppermute | solution.py:326
  38.7 6.5 %collective-permute-start.13 = (bf16[8,64,256]{2,1,0:T(8,128)(2,1)S(1)}, bf16[8,64,256]{2,1,0:T(8,128)(2,1)S(1)}, u32[]{:S(2)}, u32[]{:S(2)}) collective-permute-start(bf16[8,64,256]{2,1,0:T(8,128)(2,1)S(1)} %shard_map.98.refs_4_.refs_0_), channel_id=1, source_target_pairs={{0,32},{16,112},{32,0},{48,80},{64,96},{80,48},{96,64},{112,16},{1... | collective-permute-start | bytes 786440 | tf_op jit(solution)/shard_map/ppermute | solution.py:323
  45.3 14.7 %collective-permute-start.17 = (bf16[8,64,256]{2,1,0:T(8,128)(2,1)S(1)}, bf16[8,64,256]{2,1,0:T(8,128)(2,1)S(1)}, u32[]{:S(2)}, u32[]{:S(2)}) collective-permute-start(bf16[8,64,256]{2,1,0:T(8,128)(2,1)S(1)} %shard_map.100.refs_5_.refs_0_), channel_id=1, source_target_pairs={{0,96},{16,48},{32,64},{48,16},{64,32},{80,112},{96,0},{112,80},{1... | collective-permute-start | bytes 786440 | tf_op jit(solution)/shard_map/ppermute | solution.py:323
  49.4 7.8 %collective-permute-start.10 = (bf16[16,4096]{1,0:T(8,128)(2,1)S(1)}, bf16[16,4096]{1,0:T(8,128)(2,1)S(1)}, u32[]{:S(2)}, u32[]{:S(2)}) collective-permute-start(bf16[16,4096]{1,0:T(8,128)(2,1)S(1)} %get-tuple-element.33), channel_id=1, source_target_pairs={{0,4},{1,5},{2,6},{3,7},{4,8},{5,9},{6,10},{7,11},{8,12},{9,13},{1... | collective-permute-start | bytes 393224 | tf_op jit(solution)/shard_map/ppermute | solution.py:320
  53.4 6.5 %collective-permute-start.11 = (bf16[16,4096]{1,0:T(8,128)(2,1)S(1)}, bf16[16,4096]{1,0:T(8,128)(2,1)S(1)}, u32[]{:S(2)}, u32[]{:S(2)}) collective-permute-start(bf16[16,4096]{1,0:T(8,128)(2,1)S(1)} %get-tuple-element.34), channel_id=1, source_target_pairs={{0,8},{1,9},{2,10},{3,11},{4,12},{5,13},{6,14},{7,15},{8,0},{9,1},... | collective-permute-start | bytes 393224 | tf_op jit(solution)/shard_map/ppermute | solution.py:320
  54.7 5.2 %collective-permute-start.12 = (bf16[16,4096]{1,0:T(8,128)(2,1)S(1)}, bf16[16,4096]{1,0:T(8,128)(2,1)S(1)}, u32[]{:S(2)}, u32[]{:S(2)}) collective-permute-start(bf16[16,4096]{1,0:T(8,128)(2,1)S(1)} %get-tuple-element.35), channel_id=1, source_target_pairs={{0,12},{1,13},{2,14},{3,15},{4,0},{5,1},{6,2},{7,3},{8,4},{9,5},{1... | collective-permute-start | bytes 393224 | tf_op jit(solution)/shard_map/ppermute | solution.py:320
  60.0 1.6 %collective-permute-start.18 = (bf16[8,64,256]{2,1,0:T(8,128)(2,1)S(1)}, bf16[8,64,256]{2,1,0:T(8,128)(2,1)S(1)}, u32[]{:S(2)}, u32[]{:S(2)}) collective-permute-start(bf16[8,64,256]{2,1,0:T(8,128)(2,1)S(1)} %shard_map.103.refs_1_), channel_id=1, source_target_pairs={{0,16},{16,0},{32,48},{48,32},{64,80},{80,64},{96,112},{112,96},{1... | collective-permute-start | bytes 786440 | tf_op jit(solution)/shard_map/ppermute | solution.py:326
  63.5 4.9 %collective-permute-start.19 = (f32[32,896]{1,0:T(8,128)S(1)}, f32[32,896]{1,0:T(8,128)S(1)}, u32[]{:S(2)}, u32[]{:S(2)}) collective-permute-start(f32[32,896]{1,0:T(8,128)S(1)} %get-tuple-element.38), channel_id=1, source_target_pairs={{0,16},{16,0},{32,48},{48,32},{64,80},{80,64},{96,112},{112,96},{1... | collective-permute-start | bytes 344072 | tf_op jit(solution)/shard_map/ppermute | solution.py:326
  63.7 6.2 %collective-permute-start.14 = (bf16[16,4096]{1,0:T(8,128)(2,1)S(1)}, bf16[16,4096]{1,0:T(8,128)(2,1)S(1)}, u32[]{:S(2)}, u32[]{:S(2)}) collective-permute-start(bf16[16,4096]{1,0:T(8,128)(2,1)S(1)} %shard_map.102.refs_2_.refs_1_), channel_id=1, source_target_pairs={{0,4},{1,5},{2,6},{3,7},{4,8},{5,9},{6,10},{7,11},{8,12},{9,13},{1... | collective-permute-start | bytes 393224 | tf_op jit(solution)/shard_map/ppermute | solution.py:320
  65.0 6.8 %collective-permute-start.15 = (bf16[16,4096]{1,0:T(8,128)(2,1)S(1)}, bf16[16,4096]{1,0:T(8,128)(2,1)S(1)}, u32[]{:S(2)}, u32[]{:S(2)}) collective-permute-start(bf16[16,4096]{1,0:T(8,128)(2,1)S(1)} %shard_map.102.refs_2_.refs_1_), channel_id=1, source_target_pairs={{0,8},{1,9},{2,10},{3,11},{4,12},{5,13},{6,14},{7,15},{8,0},{9,1},... | collective-permute-start | bytes 393224 | tf_op jit(solution)/shard_map/ppermute | solution.py:320
  67.5 5.0 %collective-permute-start.16 = (bf16[16,4096]{1,0:T(8,128)(2,1)S(1)}, bf16[16,4096]{1,0:T(8,128)(2,1)S(1)}, u32[]{:S(2)}, u32[]{:S(2)}) collective-permute-start(bf16[16,4096]{1,0:T(8,128)(2,1)S(1)} %shard_map.102.refs_2_.refs_1_), channel_id=1, source_target_pairs={{0,12},{1,13},{2,14},{3,15},{4,0},{5,1},{6,2},{7,3},{8,4},{9,5},{1... | collective-permute-start | bytes 393224 | tf_op jit(solution)/shard_map/ppermute | solution.py:320
  68.4 8.1 %collective-permute-start.23 = (f32[32,896]{1,0:T(8,128)S(1)}, f32[32,896]{1,0:T(8,128)S(1)}, u32[]{:S(2)}, u32[]{:S(2)}) collective-permute-start(f32[32,896]{1,0:T(8,128)S(1)} %shard_map.105.refs_5_.refs_0_), channel_id=1, source_target_pairs={{0,32},{16,112},{32,0},{48,80},{64,96},{80,48},{96,64},{112,16},{1... | collective-permute-start | bytes 344072 | tf_op jit(solution)/shard_map/ppermute | solution.py:323
  73.1 19.4 %collective-permute-start.20 = (bf16[64,4096]{1,0:T(8,128)(2,1)S(1)}, bf16[64,4096]{1,0:T(8,128)(2,1)S(1)}, u32[]{:S(2)}, u32[]{:S(2)}) collective-permute-start(bf16[64,4096]{1,0:T(8,128)(2,1)S(1)} %shard_map.106.refs_2_.refs_1_), channel_id=1, source_target_pairs={{0,1},{1,2},{2,3},{3,0},{4,5},{5,6},{6,7},{7,4},{8,9},{9,10},{10,1... | collective-permute-start | bytes 1572872 | tf_op jit(solution)/shard_map/ppermute | solution.py:317
  73.7 18.8 %collective-permute-start.21 = (bf16[64,4096]{1,0:T(8,128)(2,1)S(1)}, bf16[64,4096]{1,0:T(8,128)(2,1)S(1)}, u32[]{:S(2)}, u32[]{:S(2)}) collective-permute-start(bf16[64,4096]{1,0:T(8,128)(2,1)S(1)} %shard_map.106.refs_2_.refs_1_), channel_id=1, source_target_pairs={{0,2},{1,3},{2,0},{3,1},{4,6},{5,7},{6,4},{7,5},{8,10},{9,11},{10,... | collective-permute-start | bytes 1572872 | tf_op jit(solution)/shard_map/ppermute | solution.py:317
  74.5 18.0 %collective-permute-start.22 = (bf16[64,4096]{1,0:T(8,128)(2,1)S(1)}, bf16[64,4096]{1,0:T(8,128)(2,1)S(1)}, u32[]{:S(2)}, u32[]{:S(2)}) collective-permute-start(bf16[64,4096]{1,0:T(8,128)(2,1)S(1)} %shard_map.106.refs_2_.refs_1_), channel_id=1, source_target_pairs={{0,3},{1,0},{2,1},{3,2},{4,7},{5,4},{6,5},{7,6},{8,11},{9,8},{10,9... | collective-permute-start | bytes 1572872 | tf_op jit(solution)/shard_map/ppermute | solution.py:317
  76.5 6.3 %collective-permute-start.24 = (f32[32,896]{1,0:T(8,128)S(1)}, f32[32,896]{1,0:T(8,128)S(1)}, u32[]{:S(2)}, u32[]{:S(2)}) collective-permute-start(f32[32,896]{1,0:T(8,128)S(1)} %shard_map.107.refs_2_.refs_0_), channel_id=1, source_target_pairs={{0,96},{16,48},{32,64},{48,16},{64,32},{80,112},{96,0},{112,80},{1... | collective-permute-start | bytes 344072 | tf_op jit(solution)/shard_map/ppermute | solution.py:323
  82.8 1.4 %collective-permute-start.25 = (f32[32,896]{1,0:T(8,128)S(1)}, f32[32,896]{1,0:T(8,128)S(1)}, u32[]{:S(2)}, u32[]{:S(2)}) collective-permute-start(f32[32,896]{1,0:T(8,128)S(1)} %shard_map.109.refs_1_), channel_id=1, source_target_pairs={{0,16},{16,0},{32,48},{48,32},{64,80},{80,64},{96,112},{112,96},{1... | collective-permute-start | bytes 344072 | tf_op jit(solution)/shard_map/ppermute | solution.py:326
  92.5 0.9 copy-start.4

commit v3 on v2

--- a/solution.py
+++ b/solution.py
@@ -9,6 +9,26 @@
 BF16 = jnp.bfloat16
 SIDE = 4
 MIB = 1024 * 1024
+COST = {
+    "gates": 3,
+    "stack": 0.1,
+    "partial": 7,
+    "left": 1,
+    "pair0": 0.1,
+    "sums": 0.2,
+    "pair1": 0.1,
+    "mine": 0.1,
+    "right": 0.1,
+    "pair2": 0.1,
+    "cholesky": 0.5,
+    "pair3": 0.1,
+    "turn": 1,
+    "quarter": 0.6,
+    "mine2": 0.1,
+    "residual": 3.6,
+    "rows": 0.5,
+    "own": 3,
+}
 
 
 def mm(a, b, ca, cb):
@@ -39,7 +59,11 @@
     return pl.BlockSpec(memory_space=pltpu.SMEM)
 
 
-def call(kernel, outs, ins, flops, nbytes, scratch=(), mib=32, pos=None, after=()):
+def cost(name):
+    return pl.CostEstimate(flops=int(COST[name] * 10**9), bytes_accessed=0, transcendentals=0)
+
+
+def call(name, kernel, outs, ins, scratch=(), mib=32, pos=None, after=()):
     lead = 0 if pos is None else 1
     several = isinstance(outs, (list, tuple))
 
@@ -55,7 +79,7 @@
         out_specs=[vmem()] * len(outs) if several else vmem(),
         scratch_shapes=list(scratch),
         compiler_params=pltpu.CompilerParams(vmem_limit_bytes=mib * MIB),
-        cost_estimate=pl.CostEstimate(flops=flops, bytes_accessed=nbytes, transcendentals=0),
+        cost_estimate=cost(name),
     )(*([pos] if lead else []), *arrays, *after)
 
 
@@ -63,21 +87,20 @@
     return jax.ShapeDtypeStruct(dims, dtype)
 
 
-def gates_kernel(pos, pre_hbm, up_hbm, cot_hbm, q_t, gate, rel, z_t, pre_v, up_v, cot_v, sems):
-    copies = [
-        pltpu.make_async_copy(src, dst, sems.at[n])
-        for n, (src, dst) in enumerate(((pre_hbm, pre_v), (up_hbm, up_v), (cot_hbm, cot_v)))
-    ]
+def gates_kernel(pre_hbm, up_hbm, cot_hbm, q_hbm, tok_hbm, gate, rel, z_t, own, pre_v, up_v, cot_v, q_t, sems):
+    pairs = ((pre_hbm, pre_v), (cot_hbm, cot_v), (up_hbm, up_v), (q_hbm, q_t), (tok_hbm, own))
+    copies = [pltpu.make_async_copy(src, dst, sems.at[n]) for n, (src, dst) in enumerate(pairs)]
     for copy in copies:
         copy.start()
     for copy in copies:
         copy.wait()
-    a, b = pos[0], pos[1]
+    me = lax.axis_index("tensor")
+    a = jnp.where(lax.axis_index("dp") % 2 == 0, me % SIDE, me // SIDE)
     tokens, width = pre_v.shape
     rows = tokens // (SIDE * SIDE)
     for k in range(SIDE):
         for j in range(SIDE):
-            src = ((a + k) % SIDE) * SIDE + (b + j) % SIDE
+            src = ((a + k) % SIDE) * SIDE + j
             src = pl.ds(pl.multiple_of(src * rows, rows), rows)
             dst = pl.ds((k * SIDE + j) * rows, rows)
             pre = pre_v[src, :].astype(F32)
@@ -131,33 +154,52 @@
         out[k] = block[...]
 
 
-def sum_split_kernel(own, a, b, c, *outs):
-    rows = own.shape[0] // SIDE
-    for j in range(SIDE):
-        cut = pl.ds(j * rows, rows)
-        total = (own[cut, :] + a[cut, :].astype(F32)) + (b[cut, :].astype(F32) + c[cut, :].astype(F32))
-        outs[j][...] = total.astype(outs[j].dtype)
-
-
 def sum_kernel(own, a, b, c, out):
     total = (own[...].astype(F32) + b[...].astype(F32)) + (a[...].astype(F32) + c[...].astype(F32))
     out[...] = total.astype(out.dtype)
 
 
+def copy_kernel(one, out):
+    out[...] = one[...]
+
+
 def add_kernel(one, two, out):
     out[...] = (one[...].astype(F32) + two[...].astype(F32)).astype(out.dtype)
-
-
-def place_kernel(which, pos, own, a, b, c, out):
-    rows = own.shape[0]
-    for k, block in enumerate((own, a, b, c)):
-        at = (pos[which] + SIDE - k) % SIDE
-        out[pl.ds(pl.multiple_of(at * rows, rows), rows), :] = block[...]
 
 
 def column_block(pos, j, k):
     first, second = (pos[0] + SIDE - k) % SIDE, (pos[1] + SIDE - j) % SIDE
     return jnp.where(pos[2] == 0, second * SIDE + first, first * SIDE + second)
+
+
+def place_rows(steps, pos, blocks, out, sems):
+    rows = blocks[0].shape[0]
+    copies = []
+    for i, k in enumerate(steps):
+        at = (pos[0] + SIDE - k) % SIDE
+        at = pl.ds(pl.multiple_of(at * rows, rows), rows)
+        copies.append(pltpu.make_async_copy(blocks[i], out.at[at], sems.at[i]))
+        copies[-1].start()
+    return copies
+
+
+def put_rows(steps, pos, blocks, so_far):
+    n = len(blocks)
+
+    def kernel(pos, *refs):
+        for copy in place_rows(steps, pos, refs[:n], refs[n + 1], refs[n + 2]):
+            copy.wait()
+
+    return pl.pallas_call(
+        kernel,
+        in_specs=[smem()] + [vmem()] * n + [hbm()],
+        out_specs=hbm(),
+        out_shape=shape(*so_far.shape),
+        scratch_shapes=[pltpu.SemaphoreType.DMA((n,))],
+        input_output_aliases={1 + n: 0},
+        compiler_params=pltpu.CompilerParams(vmem_limit_bytes=MIB),
+        cost_estimate=cost("rows"),
+    )(pos, *blocks, so_far)
 
 
 def left_kernel(pos, z_t, t0, t1, t2, t3, keep, send, whole):
@@ -214,69 +256,56 @@
         left_n[s] = jnp.concatenate([left[s], left[s]], 0).T
 
 
-def residual_kernel(n_dp, pos, mine, other, inv, gate, left_n, turned, gate_q_t, out_hbm, right, out, sems):
+def residual_kernel(
+    n_dp, pos, mine, other, inv, gate, left_n, turned, quarter,
+    gate_q_t, out_hbm, grad_input, right, out, sems, row_sems,
+):
+    own_rows = place_rows((0,), pos, (quarter,), grad_input, row_sems)
     low = jnp.where(pos[2] == 0, mine[...], other[...])
     high = jnp.where(pos[2] == 0, other[...], mine[...])
     v_t = jnp.concatenate([low, high], 0)
-    tokens = gate.shape[0]
     r = v_t.shape[0]
     q = mm_exact(inv[...], v_t, 1, 0) * (1.0 / n_dp)
     gate_q_t[...] = q
     hi, lo = split_hi_lo(-mm_exact(inv[...], q, 0, 0))
-    right[:tokens] = gate[...]
-    right[tokens:tokens + r] = hi
-    right[tokens + r:] = lo
+    right[:r] = hi
+    right[r:] = lo
     blocks = sems.shape[0]
     slots, cols = turned.shape[0], turned.shape[1]
     each = slots // blocks
     rows = each * cols
-
-    def copy(i):
-        at = pl.ds(pl.multiple_of(i * rows, rows), rows)
-        return pltpu.make_async_copy(out.at[at], out_hbm.at[at], sems.at[i])
-
-    def step(i, carry):
-        for e in range(each):
-            s = i * each + e
-            both = jnp.concatenate([turned[s], left_n[s]], 1)
-            at = pl.ds(pl.multiple_of(s * cols, cols), cols)
-            out[at, :] = mm(both, right[...], 1, 0).astype(out.dtype)
-        copy(i).start()
-        return carry
-
-    lax.fori_loop(0, blocks, step, 0)
-
-    def finish(i, carry):
-        copy(i).wait()
-        return carry
-
-    lax.fori_loop(0, blocks, finish, 0)
-
-
-def residual(pos, mine, other, inv, gate, left_n, turned, n_dp, after=()):
+    copies = []
+    for i in range(blocks):
+        for s in range(i * each, (i + 1) * each):
+            out[s * cols:(s + 1) * cols, :] = (
+                mm(turned[s], gate[...], 1, 0) + mm(left_n[s], right[...], 1, 0)
+            ).astype(out.dtype)
+        at = pl.ds(i * rows, rows)
+        copies.append(pltpu.make_async_copy(out.at[at], out_hbm.at[at], sems.at[i]))
+        copies[-1].start()
+    for copy in copies + own_rows:
+        copy.wait()
+
+
+def residual(pos, mine, other, inv, gate, left_n, turned, quarter, n_dp):
     tokens, width = gate.shape
     n, cols, twice = left_n.shape
     d = n * cols
     blocks = 8
-
-    def body(*refs):
-        residual_kernel(n_dp, *refs[:7], *refs[7 + len(after):])
-
     return pl.pallas_call(
-        body,
-        in_specs=[smem()] + [vmem()] * 6 + [hbm()] * len(after),
-        out_specs=[vmem(), hbm()],
-        out_shape=[shape(twice // 2, width, dtype=F32), shape(d, width)],
+        lambda *refs: residual_kernel(n_dp, *refs),
+        in_specs=[smem()] + [vmem()] * 7,
+        out_specs=[vmem(), hbm(), hbm()],
+        out_shape=[shape(twice // 2, width, dtype=F32), shape(d, width), shape(tokens, d)],
         scratch_shapes=[
-            pltpu.VMEM((tokens + twice, width), BF16),
+            pltpu.VMEM((twice, width), BF16),
             pltpu.VMEM((d, width), BF16),
             pltpu.SemaphoreType.DMA((blocks,)),
+            pltpu.SemaphoreType.DMA((1,)),
         ],
         compiler_params=pltpu.CompilerParams(vmem_limit_bytes=32 * MIB),
-        cost_estimate=pl.CostEstimate(
-            flops=2 * d * width * (tokens + twice), bytes_accessed=2 * d * width, transcendentals=0
-        ),
-    )(pos, mine, other, inv, gate, left_n, turned, *after)
+        cost_estimate=cost("residual"),
+    )(pos, mine, other, inv, gate, left_n, turned, quarter)
 
 
 def plane(n_dp, first, shift):
@@ -329,86 +358,73 @@
     act = pltpu.VMEM((t_tok, width), BF16)
     weights = pltpu.VMEM((d, width), BF16)
 
-    def add(one, two, out, after=()):
-        return call(add_kernel, out, [one, two], 1, 1, after=after)
+    def add(name, one, two, out, after=()):
+        return call(name, add_kernel, out, [one, two], after=after)
 
     got = {k: over_first(tokens, k) for k in shifts}
-    gate, rel, z_t = call(
-        gates_kernel,
-        [shape(t_tok, width), shape(t_tok, 2 * width), shape(2 * r, t_tok)],
-        [(hbm(), gate_pre), (hbm(), up_act), (hbm(), grad_hidden), q_init.T],
-        20 * t_tok * width, 8 * t_tok * width,
-        scratch=[act, act, act, pltpu.SemaphoreType.DMA((3,))], pos=pos,
-    )
+    gate, rel, z_t, own = call(
+        "gates", gates_kernel,
+        [shape(t_tok, width), shape(t_tok, 2 * width), shape(2 * r, t_tok), shape(t_tok, cols)],
+        [(hbm(), a) for a in (gate_pre, up_act, grad_hidden, q_init.T, tokens)],
+        scratch=[act, act, act, pltpu.VMEM((r, width), F32), pltpu.SemaphoreType.DMA((5,))],
+        mib=60,
+    )
+    own = call("own", copy_kernel, shape(t_tok, cols), [own])
     stack0 = call(
-        stack_kernel, shape(SIDE, t_tok, cols), [tokens, got[1], got[2], got[3]], 1, t_tok * d,
-        after=[rel],
+        "stack", stack_kernel, shape(SIDE, t_tok, cols), [own, got[1], got[2], got[3]]
     )
     far = {j: over_second(stack0, j) for j in shifts}
     stacks = [stack0, far[1], far[2], far[3]]
 
     parts = call(
-        partial_kernel,
+        "partial", partial_kernel,
         [shape(t_tok // SIDE, d, dtype=F32)] + [shape(t_tok // SIDE, d)] * 3,
         [rel, (hbm(), gate_weight), (hbm(), up_weight)],
-        4 * t_tok * width * d, 4 * d * width,
         scratch=[weights, weights, pltpu.SemaphoreType.DMA((8, 2))], mib=48, after=[stack0],
     )
     got = {k: over_first(parts[k], k) for k in shifts}
 
+    part_left = shape(n // 2, r, cols)
     keep, send = call(
-        left_kernel,
-        [shape(n // 2, r, cols, dtype=F32), shape(n // 2, r, cols)],
-        [z_t, *stacks], 2 * t_tok * d * 2 * r, 2 * t_tok * d,
+        "left", left_kernel, [shape(n // 2, r, cols, dtype=F32), part_left], [z_t, *stacks],
         scratch=[pltpu.VMEM((n, r, cols), F32)], pos=pos, after=[parts[0]],
     )
-    part_left = shape(n // 2, r, cols)
-    pair = add(keep, over_core(send), part_left)
+    pair = add("pair0", keep, over_core(send), part_left)
     near = over_ring(pair, 0)
+    turned = call("turn", turn_kernel, shape(n, cols, t_tok), stacks, pos=pos, after=[pair])
     sums = call(
-        sum_split_kernel,
-        [shape(t_tok // n, d, dtype=F32)] + [shape(t_tok // n, d)] * 3,
-        [parts[0], got[1], got[2], got[3]], 4 * t_tok * d, 4 * t_tok * d, after=[pair],
-    )
-    got = {j: over_second(sums[j], j) for j in shifts}
-    pair = add(pair, near, part_left, after=[sums[0]])
+        "sums", sum_kernel, shape(t_tok // SIDE, d), [parts[0], got[1], got[2], got[3]],
+        after=[turned],
+    )
+    got = {j: over_second(sums, j) for j in shifts}
+    pair = add("pair1", pair, near, part_left, after=[sums])
     near = over_ring(pair, 1)
-    turned = call(
-        turn_kernel, shape(n, cols, t_tok), stacks, 4 * MIB, 4 * t_tok * d, pos=pos, after=[pair]
-    )
-    piece = call(
-        sum_kernel, shape(t_tok // n, d), [sums[0], got[1], got[2], got[3]],
-        t_tok * d, t_tok * d, after=[turned],
-    )
-    got = {j: over_second(piece, j) for j in shifts}
-    mine = add(pair, near, part_left, after=[piece])
+    mine = add("mine", pair, near, part_left)
     other = over_core(mine)
     left, keep, send, gram = call(
-        right_kernel,
+        "right", right_kernel,
         [shape(n, r, cols)] + [shape(r // 2, width, dtype=F32)] * 2 + [shape(r, r, dtype=F32)],
-        [mine, other, gate, *stacks], 2 * t_tok * d * r, 2 * t_tok * d, pos=pos,
-    )
+        [mine, other, gate, *stacks], pos=pos,
+    )
+
     part_right = shape(r // 2, width, dtype=F32)
-    pair = add(keep, over_core(send), part_right)
+    pair = add("pair2", keep, over_core(send), part_right)
     near = over_ring(pair, 0)
+    inv, left_n = call(
+        "cholesky", cholesky_kernel, [shape(r, r, dtype=F32), shape(n, cols, 2 * r)], [gram, left],
+        after=[pair],
+    )
+    pair = add("pair3", pair, near, part_right, after=[inv])
+    near = over_ring(pair, 1)
     quarter = call(
-        lambda *refs: place_kernel(1, *refs), shape(t_tok // SIDE, d),
-        [piece, got[1], got[2], got[3]], 1, t_tok * d, pos=pos, after=[pair],
+        "quarter", sum_kernel, shape(t_tok // SIDE, d), [sums, got[1], got[2], got[3]],
+        after=[pair],
     )
     got = {k: over_first(quarter, k) for k in shifts}
-    pair = add(pair, near, part_right, after=[quarter])
-    near = over_ring(pair, 1)
-    inv, left_n = call(
-        cholesky_kernel, [shape(r, r, dtype=F32), shape(n, cols, 2 * r)], [gram, left],
-        10 * MIB, 4 * r * d, after=[pair],
-    )
-    mine = add(pair, near, part_right, after=[inv])
+    mine = add("mine2", pair, near, part_right, after=[quarter])
     other = over_core(mine)
-    gate_q_t, error = residual(pos, mine, other, inv, gate, left_n, turned, n_dp)
-    grad_input = call(
-        lambda *refs: place_kernel(0, *refs), shape(t_tok, d),
-        [quarter, got[1], got[2], got[3]], 1, 4 * t_tok * d, pos=pos, after=[gate_q_t],
-    )
+    gate_q_t, error, rows = residual(pos, mine, other, inv, gate, left_n, turned, quarter, n_dp)
+    grad_input = put_rows((2, 1, 3), pos, [got[k] for k in (2, 1, 3)], rows)
     return (grad_input, gate_q_t.T, error)
 
 

time: 96.9 us -> 86.8 us (0.90)
  the two profiles are of different devices: /device:TPU:0 before, /device:TPU:8 now
where the time goes in v3:
time: 86.8 us; the launch traced here: 86.6 us
  starting transfers between devices  35.2 us (41%)
  Pallas kernels  29.6 us (34%)
  waiting for transfers between devices  19.7 us (23%)
  between operations  1.05 us (1%)
  local copies, waits for them, and re-layouts  1 us (1%)
    pallas_call x16, Pallas kernels, call(): pl.pallas_call(body, out_shape=outs, in_specs=[smem()] * lead + specs + [...  20.8 us
    ppermute x9, starting transfers between devices, over_first(): return lax.ppermute(a, ('dp', 'tensor'), plane(n_dp, True, k))  17 us
    ppermute x4, starting transfers between devices, over_ring(): return lax.ppermute(a, 'dp', ring_pairs(n_dp, step))  9.52 us
    ppermute x6, starting transfers between devices, over_second(): return lax.ppermute(a, ('dp', 'tensor'), plane(n_dp, False, j))  8.26 us
    ppermute x6, waiting for transfers between devices, over_second(): return lax.ppermute(a, ('dp', 'tensor'), plane(n_dp, False, j))  7.29 us
    pallas_call x1, Pallas kernels, residual(): pl.pallas_call(lambda *refs: residual_kernel(n_dp, *refs), in_specs=[smem...  7.02 us
    ppermute x4, waiting for transfers between devices, over_core(): return lax.ppermute(a, 'dp', [(i, i ^ 1) for i in range(n_dp)])  5.54 us
    ppermute x4, waiting for transfers between devices, over_ring(): return lax.ppermute(a, 'dp', ring_pairs(n_dp, step))  4.11 us
  transfers between devices with their start and end apart: 23, of which 9 were waited for; matrix products, arithmetic and copies ran while one was open for 0% of the time, Pallas kernels for 32%

profile of v3, /device:TPU:8, one launch (start us, length us, event | category | flops | bytes accessed | tf_op | source)
XLA Modules:
  0.0 86.6 jit_solution(17869460298100141804)
XLA Ops:
  0.6 1.6 %collective-permute-start = (bf16[256,256]{1,0:T(8,128)(2,1)}, bf16[256,256]{1,0:T(8,128)(2,1)S(1)}, u32[]{:S(2)}, u32[]{:S(2)}) collective-permute-start(bf16[256,256]{1,0:T(8,128)(2,1)} %refs_4_.1), channel_id=1, source_target_pairs={{0,1},{1,2},{2,3},{3,0},{4,5},{5,6},{6,7},{7,4},{8,9},{9,10},{10,1... | collective-permute-start | bytes 393224 | tf_op jit(solution)/shard_map/ppermute | solution.py:346
  2.2 2.7 %collective-permute-start.1 = (bf16[256,256]{1,0:T(8,128)(2,1)}, bf16[256,256]{1,0:T(8,128)(2,1)S(1)}, u32[]{:S(2)}, u32[]{:S(2)}) collective-permute-start(bf16[256,256]{1,0:T(8,128)(2,1)} %refs_4_.1), channel_id=1, source_target_pairs={{0,2},{1,3},{2,0},{3,1},{4,6},{5,7},{6,4},{7,5},{8,10},{9,11},{10,... | collective-permute-start | bytes 393224 | tf_op jit(solution)/shard_map/ppermute | solution.py:346
  4.9 1.4 %collective-permute-start.2 = (bf16[256,256]{1,0:T(8,128)(2,1)}, bf16[256,256]{1,0:T(8,128)(2,1)S(1)}, u32[]{:S(2)}, u32[]{:S(2)}) collective-permute-start(bf16[256,256]{1,0:T(8,128)(2,1)} %refs_4_.1), channel_id=1, source_target_pairs={{0,3},{1,0},{2,1},{3,2},{4,7},{5,4},{6,5},{7,6},{8,11},{9,8},{10,9... | collective-permute-start | bytes 393224 | tf_op jit(solution)/shard_map/ppermute | solution.py:346
  6.4 3.0 %shard_map.94 = (bf16[256,896]{1,0:T(8,128)(2,1)}, bf16[256,1792]{1,0:T(8,128)(2,1)}, bf16[128,256]{1,0:T(8,128)(2,1)}, bf16[256,256]{1,0:T(8,128)(2,1)}) custom-call(bf16[256,896]{1,0:T(8,128)(2,1)} %refs_0_.1, bf16[256,896]{1,0:T(8,128)(2,1)} %refs_1_.2, bf16[256,896]{1,0:T(8,128)(2,1)} %refs_2_.2, f32[64,896]{1,0:T(8,128)} %bitcast.5, ...), custom_call_target="tpu_custom_call" | custom-call | flops 3000000000 | tf_op jit(solution)/shard_map/pallas_call | solution.py:75
  9.4 0.0 copy-start.2
  9.4 0.0 copy-start.3
  9.4 1.0 %copy-done.3 = bf16[256,256]{1,0:T(8,128)(2,1)S(1)} copy-done((bf16[256,256]{1,0:T(8,128)(2,1)S(1)}, bf16[256,256]{1,0:T(8,128)(2,1)}, u32[]{:S(2)}) %copy-start.3) | copy-done | bytes 131096
  10.4 0.1 pad_add_fusion.refs_0_.pos
  10.6 1.6 %collective-permute-start.6 = (bf16[4,256,256]{2,1,0:T(8,128)(2,1)S(1)}, bf16[4,256,256]{2,1,0:T(8,128)(2,1)S(1)}, u32[]{:S(2)}, u32[]{:S(2)}) collective-permute-start(bf16[4,256,256]{2,1,0:T(8,128)(2,1)S(1)} %shard_map.96.refs_3_.refs_2_.refs_1_.refs_4_), channel_id=1, source_target_pairs={{0,4},{1,5},{2,6},{3,7},{4,8},{5,9},{6,10},{7,11},{8,12},{9,13},{1... | collective-permute-start | bytes 1572872 | tf_op jit(solution)/shard_map/ppermute | solution.py:349
  12.2 0.9 %collective-permute-start.7 = (bf16[4,256,256]{2,1,0:T(8,128)(2,1)S(1)}, bf16[4,256,256]{2,1,0:T(8,128)(2,1)S(1)}, u32[]{:S(2)}, u32[]{:S(2)}) collective-permute-start(bf16[4,256,256]{2,1,0:T(8,128)(2,1)S(1)} %shard_map.96.refs_3_.refs_2_.refs_1_.refs_4_), channel_id=1, source_target_pairs={{0,8},{1,9},{2,10},{3,11},{4,12},{5,13},{6,14},{7,15},{8,0},{9,1},... | collective-permute-start | bytes 1572872 | tf_op jit(solution)/shard_map/ppermute | solution.py:349
  13.2 2.4 %collective-permute-start.8 = (bf16[4,256,256]{2,1,0:T(8,128)(2,1)S(1)}, bf16[4,256,256]{2,1,0:T(8,128)(2,1)S(1)}, u32[]{:S(2)}, u32[]{:S(2)}) collective-permute-start(bf16[4,256,256]{2,1,0:T(8,128)(2,1)S(1)} %shard_map.96.refs_3_.refs_2_.refs_1_.refs_4_), channel_id=1, source_target_pairs={{0,12},{1,13},{2,14},{3,15},{4,0},{5,1},{6,2},{7,3},{8,4},{9,5},{1... | collective-permute-start | bytes 1572872 | tf_op jit(solution)/shard_map/ppermute | solution.py:349
  15.6 7.6 %shard_map.97 = (f32[64,4096]{1,0:T(8,128)S(1)}, bf16[64,4096]{1,0:T(8,128)(2,1)S(1)}, bf16[64,4096]{1,0:T(8,128)(2,1)S(1)}, bf16[64,4096]{1,0:T(8,128)(2,1)S(1)}) custom-call(bf16[256,1792]{1,0:T(8,128)(2,1)S(1)} %copy-done.2, bf16[4096,896]{1,0:T(8,128)(2,1)} %refs_1_.3, bf16[4096,896]{1,0:T(8,128)(2,1)} %refs_2_.3, ...), custom_call_target="tpu_custom_call" | custom-call | flops 7000000000 | tf_op jit(solution)/shard_map/pallas_call | solution.py:75
  23.1 0.9 %collective-permute-start.3 = (bf16[64,4096]{1,0:T(8,128)(2,1)S(1)}, bf16[64,4096]{1,0:T(8,128)(2,1)S(1)}, u32[]{:S(2)}, u32[]{:S(2)}) collective-permute-start(bf16[64,4096]{1,0:T(8,128)(2,1)S(1)} %get-tuple-element.25), channel_id=1, source_target_pairs={{0,1},{1,2},{2,3},{3,0},{4,5},{5,6},{6,7},{7,4},{8,9},{9,10},{10,1... | collective-permute-start | bytes 1572872 | tf_op jit(solution)/shard_map/ppermute | solution.py:346
  24.0 2.8 %collective-permute-start.4 = (bf16[64,4096]{1,0:T(8,128)(2,1)S(1)}, bf16[64,4096]{1,0:T(8,128)(2,1)S(1)}, u32[]{:S(2)}, u32[]{:S(2)}) collective-permute-start(bf16[64,4096]{1,0:T(8,128)(2,1)S(1)} %get-tuple-element.26), channel_id=1, source_target_pairs={{0,2},{1,3},{2,0},{3,1},{4,6},{5,7},{6,4},{7,5},{8,10},{9,11},{10,... | collective-permute-start | bytes 1572872 | tf_op jit(solution)/shard_map/ppermute | solution.py:346
  26.9 0.8 collective-permute-start.5
  27.7 7.3 %collective-permute-done.8.refs_5_.refs_4_.refs_7_ = bf16[4,256,256]{2,1,0:T(8,128)(2,1)S(1)} collective-permute-done((bf16[4,256,256]{2,1,0:T(8,128)(2,1)S(1)}, bf16[4,256,256]{2,1,0:T(8,128)(2,1)S(1)}, u32[]{:S(2)}, u32[]{:S(2)}) %collective-permute-start.8) | collective-permute-done | bytes 524320 | tf_op jit(solution)/shard_map/ppermute | solution.py:349
  35.0 1.0 %shard_map.98 = (f32[8,64,256]{2,1,0:T(8,128)S(1)}, bf16[8,64,256]{2,1,0:T(8,128)(2,1)S(1)}) custom-call(s32[3]{0:T(128)S(1)} %pad_add_fusion.refs_0_.pos, bf16[128,256]{1,0:T(8,128)(2,1)S(1)} %copy-done.1, bf16[4,256,256]{2,1,0:T(8,128)(2,1)S(1)} %shard_map.96.refs_3_.refs_2_.refs_1_.refs_4_, ...), custom_call_target="tpu_custom_call" | custom-call | flops 1000000000 | tf_op jit(solution)/shard_map/pallas_call | solution.py:75
  36.1 0.1 collective-permute-start.9
  36.2 1.5 %collective-permute-done.9.refs_1_ = bf16[8,64,256]{2,1,0:T(8,128)(2,1)S(1)} collective-permute-done((bf16[8,64,256]{2,1,0:T(8,128)(2,1)S(1)}, bf16[8,64,256]{2,1,0:T(8,128)(2,1)S(1)}, u32[]{:S(2)}, u32[]{:S(2)}) %collective-permute-start.9) | collective-permute-done | bytes 262176 | tf_op jit(solution)/shard_map/ppermute | solution.py:355
  37.7 0.1 shard_map.99.refs_5_.refs_0_
  37.7 2.0 %collective-permute-start.13 = (bf16[8,64,256]{2,1,0:T(8,128)(2,1)S(1)}, bf16[8,64,256]{2,1,0:T(8,128)(2,1)S(1)}, u32[]{:S(2)}, u32[]{:S(2)}) collective-permute-start(bf16[8,64,256]{2,1,0:T(8,128)(2,1)S(1)} %shard_map.99.refs_5_.refs_0_), channel_id=1, source_target_pairs={{0,32},{16,112},{32,0},{48,80},{64,96},{80,48},{96,64},{112,16},{1... | collective-permute-start | bytes 786440 | tf_op jit(solution)/shard_map/ppermute | solution.py:352
  39.8 1.1 %shard_map.100.refs_4_.refs_6_ = bf16[16,256,256]{2,1,0:T(8,128)(2,1)S(1)} custom-call(s32[3]{0:T(128)S(1)} %pad_add_fusion.refs_0_.pos, bf16[4,256,256]{2,1,0:T(8,128)(2,1)S(1)} %shard_map.96.refs_3_.refs_2_.refs_1_.refs_4_, bf16[4,256,256]{2,1,0:T(8,128)(2,1)S(1)} %collective-permute-done.6.refs_3_.refs_2_.refs_5_, ...), custom_call_target="tpu_custom_call" | custom-call | flops 1000000000 | tf_op jit(solution)/shard_map/pallas_call | solution.py:75
  40.9 0.3 shard_map.101.refs_2_.refs_0_
  41.2 3.0 %collective-permute-done.13.refs_1_ = bf16[8,64,256]{2,1,0:T(8,128)(2,1)S(1)} collective-permute-done((bf16[8,64,256]{2,1,0:T(8,128)(2,1)S(1)}, bf16[8,64,256]{2,1,0:T(8,128)(2,1)S(1)}, u32[]{:S(2)}, u32[]{:S(2)}) %collective-permute-start.13) | collective-permute-done | bytes 262176 | tf_op jit(solution)/shard_map/ppermute | solution.py:352
  44.2 0.1 shard_map.102.refs_0_
  44.3 4.1 %collective-permute-start.14 = (bf16[8,64,256]{2,1,0:T(8,128)(2,1)S(1)}, bf16[8,64,256]{2,1,0:T(8,128)(2,1)S(1)}, u32[]{:S(2)}, u32[]{:S(2)}) collective-permute-start(bf16[8,64,256]{2,1,0:T(8,128)(2,1)S(1)} %shard_map.102.refs_0_), channel_id=1, source_target_pairs={{0,96},{16,48},{32,64},{48,16},{64,32},{80,112},{96,0},{112,80},{1... | collective-permute-start | bytes 786440 | tf_op jit(solution)/shard_map/ppermute | solution.py:352
  48.4 0.6 collective-permute-start.11
  49.0 2.6 %collective-permute-start.12 = (bf16[64,4096]{1,0:T(8,128)(2,1)S(1)}, bf16[64,4096]{1,0:T(8,128)(2,1)S(1)}, u32[]{:S(2)}, u32[]{:S(2)}) collective-permute-start(bf16[64,4096]{1,0:T(8,128)(2,1)S(1)} %shard_map.101.refs_2_.refs_0_), channel_id=1, source_target_pairs={{0,12},{1,13},{2,14},{3,15},{4,0},{5,1},{6,2},{7,3},{8,4},{9,5},{1... | collective-permute-start | bytes 1572872 | tf_op jit(solution)/shard_map/ppermute | solution.py:349
  51.7 1.1 %collective-permute-done.14.refs_1_ = bf16[8,64,256]{2,1,0:T(8,128)(2,1)S(1)} collective-permute-done((bf16[8,64,256]{2,1,0:T(8,128)(2,1)S(1)}, bf16[8,64,256]{2,1,0:T(8,128)(2,1)S(1)}, u32[]{:S(2)}, u32[]{:S(2)}) %collective-permute-start.14) | collective-permute-done | bytes 262176 | tf_op jit(solution)/shard_map/ppermute | solution.py:352
  52.7 0.1 shard_map.103.refs_1_
  52.8 0.1 collective-permute-start.15
  52.9 1.5 %collective-permute-done.15.refs_2_ = bf16[8,64,256]{2,1,0:T(8,128)(2,1)S(1)} collective-permute-done((bf16[8,64,256]{2,1,0:T(8,128)(2,1)S(1)}, bf16[8,64,256]{2,1,0:T(8,128)(2,1)S(1)}, u32[]{:S(2)}, u32[]{:S(2)}) %collective-permute-start.15) | collective-permute-done | bytes 262176 | tf_op jit(solution)/shard_map/ppermute | solution.py:355
  54.4 1.8 %shard_map.104 = (bf16[16,64,256]{2,1,0:T(8,128)(2,1)S(1)}, f32[32,896]{1,0:T(8,128)S(1)}, f32[32,896]{1,0:T(8,128)S(1)}, f32[64,64]{1,0:T(8,128)S(1)}) custom-call(s32[3]{0:T(128)S(1)} %pad_add_fusion.refs_0_.pos, bf16[8,64,256]{2,1,0:T(8,128)(2,1)S(1)} %shard_map.103.refs_1_, bf16[8,64,256]{2,1,0:T(8,128)(2,1)S(1)} %collective-permute-done.15.refs_2_, ...), custom_call_target="tpu_custom_call" | custom-call | flops 100000000 | tf_op jit(solution)/shard_map/pallas_call | solution.py:75
  56.3 0.2 collective-permute-start.16
  56.5 1.2 %collective-permute-done.16.refs_1_ = f32[32,896]{1,0:T(8,128)S(1)} collective-permute-done((f32[32,896]{1,0:T(8,128)S(1)}, f32[32,896]{1,0:T(8,128)S(1)}, u32[]{:S(2)}, u32[]{:S(2)}) %collective-permute-start.16) | collective-permute-done | bytes 114720 | tf_op jit(solution)/shard_map/ppermute | solution.py:355
  57.7 0.1 collective-permute-start.17
  57.8 5.4 %shard_map.106 = (f32[64,64]{1,0:T(8,128)S(1)}, bf16[16,256,128]{2,1,0:T(8,128)(2,1)S(1)}) custom-call(f32[64,64]{1,0:T(8,128)S(1)} %get-tuple-element.34.refs_0_, bf16[16,64,256]{2,1,0:T(8,128)(2,1)S(1)} %get-tuple-element.35.refs_1_, f32[32,896]{1,0:T(8,128)S(1)} %shard_map.105.refs_2_.refs_0_), custom_call_target="tpu_custom_call" | custom-call | flops 500000000 | tf_op jit(solution)/shard_map/pallas_call | solution.py:75
  63.3 3.3 %collective-permute-start.21 = (f32[32,896]{1,0:T(8,128)S(1)}, f32[32,896]{1,0:T(8,128)S(1)}, u32[]{:S(2)}, u32[]{:S(2)}) collective-permute-start(f32[32,896]{1,0:T(8,128)S(1)} %shard_map.107.refs_4_.refs_0_), channel_id=1, source_target_pairs={{0,96},{16,48},{32,64},{48,16},{64,32},{80,112},{96,0},{112,80},{1... | collective-permute-start | bytes 344072 | tf_op jit(solution)/shard_map/ppermute | solution.py:352
  66.6 0.3 shard_map.108.refs_2_.refs_7_
  66.8 3.5 %collective-permute-start.18 = (bf16[64,4096]{1,0:T(8,128)(2,1)S(1)}, bf16[64,4096]{1,0:T(8,128)(2,1)S(1)}, u32[]{:S(2)}, u32[]{:S(2)}) collective-permute-start(bf16[64,4096]{1,0:T(8,128)(2,1)S(1)} %shard_map.108.refs_2_.refs_7_), channel_id=1, source_target_pairs={{0,2},{1,3},{2,0},{3,1},{4,6},{5,7},{6,4},{7,5},{8,10},{9,11},{10,... | collective-permute-start | bytes 1572872 | tf_op jit(solution)/shard_map/ppermute | solution.py:346
  70.3 1.6 %collective-permute-start.19 = (bf16[64,4096]{1,0:T(8,128)(2,1)S(1)}, bf16[64,4096]{1,0:T(8,128)(2,1)S(1)}, u32[]{:S(2)}, u32[]{:S(2)}) collective-permute-start(bf16[64,4096]{1,0:T(8,128)(2,1)S(1)} %shard_map.108.refs_2_.refs_7_), channel_id=1, source_target_pairs={{0,1},{1,2},{2,3},{3,0},{4,5},{5,6},{6,7},{7,4},{8,9},{9,10},{10,1... | collective-permute-start | bytes 1572872 | tf_op jit(solution)/shard_map/ppermute | solution.py:346
  71.9 1.6 %collective-permute-start.20 = (bf16[64,4096]{1,0:T(8,128)(2,1)S(1)}, bf16[64,4096]{1,0:T(8,128)(2,1)S(1)}, u32[]{:S(2)}, u32[]{:S(2)}) collective-permute-start(bf16[64,4096]{1,0:T(8,128)(2,1)S(1)} %shard_map.108.refs_2_.refs_7_), channel_id=1, source_target_pairs={{0,3},{1,0},{2,1},{3,2},{4,7},{5,4},{6,5},{7,6},{8,11},{9,8},{10,9... | collective-permute-start | bytes 1572872 | tf_op jit(solution)/shard_map/ppermute | solution.py:346
  73.6 0.1 collective-permute-start.22
  73.6 1.3 %collective-permute-done.22.refs_2_ = f32[32,896]{1,0:T(8,128)S(1)} collective-permute-done((f32[32,896]{1,0:T(8,128)S(1)}, f32[32,896]{1,0:T(8,128)S(1)}, u32[]{:S(2)}, u32[]{:S(2)}) %collective-permute-start.22) | collective-permute-done | bytes 114720 | tf_op jit(solution)/shard_map/ppermute | solution.py:355
  75.0 7.0 %shard_map.110 = (f32[64,896]{1,0:T(8,128)}, bf16[4096,896]{1,0:T(8,128)(2,1)}, bf16[256,4096]{1,0:T(8,128)(2,1)}) custom-call(s32[3]{0:T(128)S(1)} %pad_add_fusion.refs_0_.pos, f32[32,896]{1,0:T(8,128)S(1)} %shard_map.109.refs_1_, f32[32,896]{1,0:T(8,128)S(1)} %collective-permute-done.22.refs_2_, f32[64,64]{1,0:T(8,128)S(1)} %get-tuple-element.36.refs_2_.refs_3_, ...), custom_call_target="tpu_custom_call" | custom-call | flops 3600000000 | tf_op jit(solution)/shard_map/pallas_call | solution.py:295
  82.0 1.2 %collective-permute-done.19.refs_1_ = bf16[64,4096]{1,0:T(8,128)(2,1)S(1)} collective-permute-done((bf16[64,4096]{1,0:T(8,128)(2,1)S(1)}, bf16[64,4096]{1,0:T(8,128)(2,1)S(1)}, u32[]{:S(2)}, u32[]{:S(2)}) %collective-permute-start.19) | collective-permute-done | bytes 524320 | tf_op jit(solution)/shard_map/ppermute | solution.py:346
  83.2 1.5 %collective-permute-done.20.refs_2_ = bf16[64,4096]{1,0:T(8,128)(2,1)S(1)} collective-permute-done((bf16[64,4096]{1,0:T(8,128)(2,1)S(1)}, bf16[64,4096]{1,0:T(8,128)(2,1)S(1)}, u32[]{:S(2)}, u32[]{:S(2)}) %collective-permute-start.20) | collective-permute-done | bytes 524320 | tf_op jit(solution)/shard_map/ppermute | solution.py:346
  84.7 1.7 %shard_map.111 = bf16[256,4096]{1,0:T(8,128)(2,1)} custom-call(s32[3]{0:T(128)S(1)} %pad_add_fusion.refs_0_.pos, bf16[64,4096]{1,0:T(8,128)(2,1)S(1)} %collective-permute-done.18.refs_0_, bf16[64,4096]{1,0:T(8,128)(2,1)S(1)} %collective-permute-done.19.refs_1_, bf16[64,4096]{1,0:T(8,128)(2,1)S(1)} %collective-permute-done.20.refs_2_, ...), custom_call_target="tpu_custom_call", output_to_operand_aliasing={{}: (4, {})} | custom-call | flops 500000000 | tf_op jit(solution)/shard_map/pallas_call | solution.py:193
  (25 shorter events, 0.1 us)
Async XLA Ops:
  0.6 9.9 %collective-permute-start = (bf16[256,256]{1,0:T(8,128)(2,1)}, bf16[256,256]{1,0:T(8,128)(2,1)S(1)}, u32[]{:S(2)}, u32[]{:S(2)}) collective-permute-start(bf16[256,256]{1,0:T(8,128)(2,1)} %refs_4_.1), channel_id=1, source_target_pairs={{0,1},{1,2},{2,3},{3,0},{4,5},{5,6},{6,7},{7,4},{8,9},{9,10},{10,1... | collective-permute-start | bytes 393224 | tf_op jit(solution)/shard_map/ppermute | solution.py:346
  2.2 8.3 %collective-permute-start.1 = (bf16[256,256]{1,0:T(8,128)(2,1)}, bf16[256,256]{1,0:T(8,128)(2,1)S(1)}, u32[]{:S(2)}, u32[]{:S(2)}) collective-permute-start(bf16[256,256]{1,0:T(8,128)(2,1)} %refs_4_.1), channel_id=1, source_target_pairs={{0,2},{1,3},{2,0},{3,1},{4,6},{5,7},{6,4},{7,5},{8,10},{9,11},{10,... | collective-permute-start | bytes 393224 | tf_op jit(solution)/shard_map/ppermute | solution.py:346
  4.9 5.6 %collective-permute-start.2 = (bf16[256,256]{1,0:T(8,128)(2,1)}, bf16[256,256]{1,0:T(8,128)(2,1)S(1)}, u32[]{:S(2)}, u32[]{:S(2)}) collective-permute-start(bf16[256,256]{1,0:T(8,128)(2,1)} %refs_4_.1), channel_id=1, source_target_pairs={{0,3},{1,0},{2,1},{3,2},{4,7},{5,4},{6,5},{7,6},{8,11},{9,8},{10,9... | collective-permute-start | bytes 393224 | tf_op jit(solution)/shard_map/ppermute | solution.py:346
  9.4 6.2 %copy-start.2 = (bf16[256,1792]{1,0:T(8,128)(2,1)S(1)}, bf16[256,1792]{1,0:T(8,128)(2,1)}, u32[]{:S(2)}) copy-start(bf16[256,1792]{1,0:T(8,128)(2,1)} %get-tuple-element.22.refs_0_) | copy-start | bytes 2752516
  9.4 1.0 %copy-start.3 = (bf16[256,256]{1,0:T(8,128)(2,1)S(1)}, bf16[256,256]{1,0:T(8,128)(2,1)}, u32[]{:S(2)}) copy-start(bf16[256,256]{1,0:T(8,128)(2,1)} %get-tuple-element.23.refs_0_) | copy-start | bytes 393220
  10.6 16.3 %collective-permute-start.6 = (bf16[4,256,256]{2,1,0:T(8,128)(2,1)S(1)}, bf16[4,256,256]{2,1,0:T(8,128)(2,1)S(1)}, u32[]{:S(2)}, u32[]{:S(2)}) collective-permute-start(bf16[4,256,256]{2,1,0:T(8,128)(2,1)S(1)} %shard_map.96.refs_3_.refs_2_.refs_1_.refs_4_), channel_id=1, source_target_pairs={{0,4},{1,5},{2,6},{3,7},{4,8},{5,9},{6,10},{7,11},{8,12},{9,13},{1... | collective-permute-start | bytes 1572872 | tf_op jit(solution)/shard_map/ppermute | solution.py:349
  12.2 15.5 %collective-permute-start.7 = (bf16[4,256,256]{2,1,0:T(8,128)(2,1)S(1)}, bf16[4,256,256]{2,1,0:T(8,128)(2,1)S(1)}, u32[]{:S(2)}, u32[]{:S(2)}) collective-permute-start(bf16[4,256,256]{2,1,0:T(8,128)(2,1)S(1)} %shard_map.96.refs_3_.refs_2_.refs_1_.refs_4_), channel_id=1, source_target_pairs={{0,8},{1,9},{2,10},{3,11},{4,12},{5,13},{6,14},{7,15},{8,0},{9,1},... | collective-permute-start | bytes 1572872 | tf_op jit(solution)/shard_map/ppermute | solution.py:349
  13.2 21.8 %collective-permute-start.8 = (bf16[4,256,256]{2,1,0:T(8,128)(2,1)S(1)}, bf16[4,256,256]{2,1,0:T(8,128)(2,1)S(1)}, u32[]{:S(2)}, u32[]{:S(2)}) collective-permute-start(bf16[4,256,256]{2,1,0:T(8,128)(2,1)S(1)} %shard_map.96.refs_3_.refs_2_.refs_1_.refs_4_), channel_id=1, source_target_pairs={{0,12},{1,13},{2,14},{3,15},{4,0},{5,1},{6,2},{7,3},{8,4},{9,5},{1... | collective-permute-start | bytes 1572872 | tf_op jit(solution)/shard_map/ppermute | solution.py:349
  15.6 19.4 %copy-start.1 = (bf16[128,256]{1,0:T(8,128)(2,1)S(1)}, bf16[128,256]{1,0:T(8,128)(2,1)}, u32[]{:S(2)}) copy-start(bf16[128,256]{1,0:T(8,128)(2,1)} %get-tuple-element.28.refs_1_) | copy-start | bytes 196612
  23.1 17.7 %collective-permute-start.3 = (bf16[64,4096]{1,0:T(8,128)(2,1)S(1)}, bf16[64,4096]{1,0:T(8,128)(2,1)S(1)}, u32[]{:S(2)}, u32[]{:S(2)}) collective-permute-start(bf16[64,4096]{1,0:T(8,128)(2,1)S(1)} %get-tuple-element.25), channel_id=1, source_target_pairs={{0,1},{1,2},{2,3},{3,0},{4,5},{5,6},{6,7},{7,4},{8,9},{9,10},{10,1... | collective-permute-start | bytes 1572872 | tf_op jit(solution)/shard_map/ppermute | solution.py:346
  24.0 16.8 %collective-permute-start.4 = (bf16[64,4096]{1,0:T(8,128)(2,1)S(1)}, bf16[64,4096]{1,0:T(8,128)(2,1)S(1)}, u32[]{:S(2)}, u32[]{:S(2)}) collective-permute-start(bf16[64,4096]{1,0:T(8,128)(2,1)S(1)} %get-tuple-element.26), channel_id=1, source_target_pairs={{0,2},{1,3},{2,0},{3,1},{4,6},{5,7},{6,4},{7,5},{8,10},{9,11},{10,... | collective-permute-start | bytes 1572872 | tf_op jit(solution)/shard_map/ppermute | solution.py:346
  26.9 14.0 %collective-permute-start.5 = (bf16[64,4096]{1,0:T(8,128)(2,1)S(1)}, bf16[64,4096]{1,0:T(8,128)(2,1)S(1)}, u32[]{:S(2)}, u32[]{:S(2)}) collective-permute-start(bf16[64,4096]{1,0:T(8,128)(2,1)S(1)} %get-tuple-element.27), channel_id=1, source_target_pairs={{0,3},{1,0},{2,1},{3,2},{4,7},{5,4},{6,5},{7,6},{8,11},{9,8},{10,9... | collective-permute-start | bytes 1572872 | tf_op jit(solution)/shard_map/ppermute | solution.py:346
  36.1 18.4 %copy-start = (bf16[256,896]{1,0:T(8,128)(2,1)S(1)}, bf16[256,896]{1,0:T(8,128)(2,1)}, u32[]{:S(2)}) copy-start(bf16[256,896]{1,0:T(8,128)(2,1)} %get-tuple-element.31.refs_3_.refs_4_) | copy-start | bytes 1376260
  36.1 1.6 %collective-permute-start.9 = (bf16[8,64,256]{2,1,0:T(8,128)(2,1)S(1)}, bf16[8,64,256]{2,1,0:T(8,128)(2,1)S(1)}, u32[]{:S(2)}, u32[]{:S(2)}) collective-permute-start(bf16[8,64,256]{2,1,0:T(8,128)(2,1)S(1)} %get-tuple-element.30), channel_id=1, source_target_pairs={{0,16},{16,0},{32,48},{48,32},{64,80},{80,64},{96,112},{112,96},{1... | collective-permute-start | bytes 786440 | tf_op jit(solution)/shard_map/ppermute | solution.py:355
  37.7 6.5 %collective-permute-start.13 = (bf16[8,64,256]{2,1,0:T(8,128)(2,1)S(1)}, bf16[8,64,256]{2,1,0:T(8,128)(2,1)S(1)}, u32[]{:S(2)}, u32[]{:S(2)}) collective-permute-start(bf16[8,64,256]{2,1,0:T(8,128)(2,1)S(1)} %shard_map.99.refs_5_.refs_0_), channel_id=1, source_target_pairs={{0,32},{16,112},{32,0},{48,80},{64,96},{80,48},{96,64},{112,16},{1... | collective-permute-start | bytes 786440 | tf_op jit(solution)/shard_map/ppermute | solution.py:352
  44.3 8.5 %collective-permute-start.14 = (bf16[8,64,256]{2,1,0:T(8,128)(2,1)S(1)}, bf16[8,64,256]{2,1,0:T(8,128)(2,1)S(1)}, u32[]{:S(2)}, u32[]{:S(2)}) collective-permute-start(bf16[8,64,256]{2,1,0:T(8,128)(2,1)S(1)} %shard_map.102.refs_0_), channel_id=1, source_target_pairs={{0,96},{16,48},{32,64},{48,16},{64,32},{80,112},{96,0},{112,80},{1... | collective-permute-start | bytes 786440 | tf_op jit(solution)/shard_map/ppermute | solution.py:352
  48.4 18.2 %collective-permute-start.10 = (bf16[64,4096]{1,0:T(8,128)(2,1)S(1)}, bf16[64,4096]{1,0:T(8,128)(2,1)S(1)}, u32[]{:S(2)}, u32[]{:S(2)}) collective-permute-start(bf16[64,4096]{1,0:T(8,128)(2,1)S(1)} %shard_map.101.refs_2_.refs_0_), channel_id=1, source_target_pairs={{0,4},{1,5},{2,6},{3,7},{4,8},{5,9},{6,10},{7,11},{8,12},{9,13},{1... | collective-permute-start | bytes 1572872 | tf_op jit(solution)/shard_map/ppermute | solution.py:349
  48.4 18.2 %collective-permute-start.11 = (bf16[64,4096]{1,0:T(8,128)(2,1)S(1)}, bf16[64,4096]{1,0:T(8,128)(2,1)S(1)}, u32[]{:S(2)}, u32[]{:S(2)}) collective-permute-start(bf16[64,4096]{1,0:T(8,128)(2,1)S(1)} %shard_map.101.refs_2_.refs_0_), channel_id=1, source_target_pairs={{0,8},{1,9},{2,10},{3,11},{4,12},{5,13},{6,14},{7,15},{8,0},{9,1},... | collective-permute-start | bytes 1572872 | tf_op jit(solution)/shard_map/ppermute | solution.py:349
  49.0 17.5 %collective-permute-start.12 = (bf16[64,4096]{1,0:T(8,128)(2,1)S(1)}, bf16[64,4096]{1,0:T(8,128)(2,1)S(1)}, u32[]{:S(2)}, u32[]{:S(2)}) collective-permute-start(bf16[64,4096]{1,0:T(8,128)(2,1)S(1)} %shard_map.101.refs_2_.refs_0_), channel_id=1, source_target_pairs={{0,12},{1,13},{2,14},{3,15},{4,0},{5,1},{6,2},{7,3},{8,4},{9,5},{1... | collective-permute-start | bytes 1572872 | tf_op jit(solution)/shard_map/ppermute | solution.py:349
  52.8 1.6 %collective-permute-start.15 = (bf16[8,64,256]{2,1,0:T(8,128)(2,1)S(1)}, bf16[8,64,256]{2,1,0:T(8,128)(2,1)S(1)}, u32[]{:S(2)}, u32[]{:S(2)}) collective-permute-start(bf16[8,64,256]{2,1,0:T(8,128)(2,1)S(1)} %shard_map.103.refs_1_), channel_id=1, source_target_pairs={{0,16},{16,0},{32,48},{48,32},{64,80},{80,64},{96,112},{112,96},{1... | collective-permute-start | bytes 786440 | tf_op jit(solution)/shard_map/ppermute | solution.py:355
  56.3 1.4 %collective-permute-start.16 = (f32[32,896]{1,0:T(8,128)S(1)}, f32[32,896]{1,0:T(8,128)S(1)}, u32[]{:S(2)}, u32[]{:S(2)}) collective-permute-start(f32[32,896]{1,0:T(8,128)S(1)} %get-tuple-element.33), channel_id=1, source_target_pairs={{0,16},{16,0},{32,48},{48,32},{64,80},{80,64},{96,112},{112,96},{1... | collective-permute-start | bytes 344072 | tf_op jit(solution)/shard_map/ppermute | solution.py:355
  57.7 5.5 %collective-permute-start.17 = (f32[32,896]{1,0:T(8,128)S(1)}, f32[32,896]{1,0:T(8,128)S(1)}, u32[]{:S(2)}, u32[]{:S(2)}) collective-permute-start(f32[32,896]{1,0:T(8,128)S(1)} %shard_map.105.refs_2_.refs_0_), channel_id=1, source_target_pairs={{0,32},{16,112},{32,0},{48,80},{64,96},{80,48},{96,64},{112,16},{1... | collective-permute-start | bytes 344072 | tf_op jit(solution)/shard_map/ppermute | solution.py:352
  63.3 10.3 %collective-permute-start.21 = (f32[32,896]{1,0:T(8,128)S(1)}, f32[32,896]{1,0:T(8,128)S(1)}, u32[]{:S(2)}, u32[]{:S(2)}) collective-permute-start(f32[32,896]{1,0:T(8,128)S(1)} %shard_map.107.refs_4_.refs_0_), channel_id=1, source_target_pairs={{0,96},{16,48},{32,64},{48,16},{64,32},{80,112},{96,0},{112,80},{1... | collective-permute-start | bytes 344072 | tf_op jit(solution)/shard_map/ppermute | solution.py:352
  66.8 15.1 %collective-permute-start.18 = (bf16[64,4096]{1,0:T(8,128)(2,1)S(1)}, bf16[64,4096]{1,0:T(8,128)(2,1)S(1)}, u32[]{:S(2)}, u32[]{:S(2)}) collective-permute-start(bf16[64,4096]{1,0:T(8,128)(2,1)S(1)} %shard_map.108.refs_2_.refs_7_), channel_id=1, source_target_pairs={{0,2},{1,3},{2,0},{3,1},{4,6},{5,7},{6,4},{7,5},{8,10},{9,11},{10,... | collective-permute-start | bytes 1572872 | tf_op jit(solution)/shard_map/ppermute | solution.py:346
  70.3 12.9 %collective-permute-start.19 = (bf16[64,4096]{1,0:T(8,128)(2,1)S(1)}, bf16[64,4096]{1,0:T(8,128)(2,1)S(1)}, u32[]{:S(2)}, u32[]{:S(2)}) collective-permute-start(bf16[64,4096]{1,0:T(8,128)(2,1)S(1)} %shard_map.108.refs_2_.refs_7_), channel_id=1, source_target_pairs={{0,1},{1,2},{2,3},{3,0},{4,5},{5,6},{6,7},{7,4},{8,9},{9,10},{10,1... | collective-permute-start | bytes 1572872 | tf_op jit(solution)/shard_map/ppermute | solution.py:346
  71.9 12.8 %collective-permute-start.20 = (bf16[64,4096]{1,0:T(8,128)(2,1)S(1)}, bf16[64,4096]{1,0:T(8,128)(2,1)S(1)}, u32[]{:S(2)}, u32[]{:S(2)}) collective-permute-start(bf16[64,4096]{1,0:T(8,128)(2,1)S(1)} %shard_map.108.refs_2_.refs_7_), channel_id=1, source_target_pairs={{0,3},{1,0},{2,1},{3,2},{4,7},{5,4},{6,5},{7,6},{8,11},{9,8},{10,9... | collective-permute-start | bytes 1572872 | tf_op jit(solution)/shard_map/ppermute | solution.py:346
  73.6 1.4 %collective-permute-start.22 = (f32[32,896]{1,0:T(8,128)S(1)}, f32[32,896]{1,0:T(8,128)S(1)}, u32[]{:S(2)}, u32[]{:S(2)}) collective-permute-start(f32[32,896]{1,0:T(8,128)S(1)} %shard_map.109.refs_1_), channel_id=1, source_target_pairs={{0,16},{16,0},{32,48},{48,32},{64,80},{80,64},{96,112},{112,96},{1... | collective-permute-start | bytes 344072 | tf_op jit(solution)/shard_map/ppermute | solution.py:355

commit v4 on v3

--- a/solution.py
+++ b/solution.py
@@ -154,7 +154,7 @@
         out[k] = block[...]
 
 
-def sum_kernel(own, a, b, c, out):
+def sum_kernel(own, a, c, b, out):
     total = (own[...].astype(F32) + b[...].astype(F32)) + (a[...].astype(F32) + c[...].astype(F32))
     out[...] = total.astype(out.dtype)
 
@@ -202,7 +202,7 @@
     )(pos, *blocks, so_far)
 
 
-def left_kernel(pos, z_t, t0, t1, t2, t3, keep, send, whole):
+def left_kernel(pos, z_t, t0, t1, t3, t2, keep, send, whole):
     half, r = keep.shape[0], keep.shape[1]
     for j, stack in enumerate((t0, t1, t2, t3)):
         for k in range(SIDE):
@@ -212,13 +212,13 @@
     send[...] = whole[pl.ds((1 - pos[2]) * half, half)].astype(send.dtype)
 
 
-def turn_kernel(pos, t0, t1, t2, t3, out):
+def turn_kernel(pos, t0, t1, t3, t2, out):
     for j, stack in enumerate((t0, t1, t2, t3)):
         for k in range(SIDE):
             out[column_block(pos, j, k)] = stack[k].T
 
 
-def right_kernel(pos, mine, other, gate, t0, t1, t2, t3, left, keep, send, gram):
+def right_kernel(pos, mine, other, gate, t0, t1, t3, t2, left, keep, send, gram):
     half, r = mine.shape[0], mine.shape[1]
     left[pl.ds(pos[2] * half, half)] = mine[...]
     left[pl.ds((1 - pos[2]) * half, half)] = other[...]
@@ -374,7 +374,7 @@
         "stack", stack_kernel, shape(SIDE, t_tok, cols), [own, got[1], got[2], got[3]]
     )
     far = {j: over_second(stack0, j) for j in shifts}
-    stacks = [stack0, far[1], far[2], far[3]]
+    stacks = [stack0, far[1], far[3], far[2]]
 
     parts = call(
         "partial", partial_kernel,
@@ -386,14 +386,15 @@
 
     part_left = shape(n // 2, r, cols)
     keep, send = call(
-        "left", left_kernel, [shape(n // 2, r, cols, dtype=F32), part_left], [z_t, *stacks],
+        "left", left_kernel, [shape(n // 2, r, cols, dtype=F32), part_left],
+        [z_t, *stacks],
         scratch=[pltpu.VMEM((n, r, cols), F32)], pos=pos, after=[parts[0]],
     )
     pair = add("pair0", keep, over_core(send), part_left)
     near = over_ring(pair, 0)
     turned = call("turn", turn_kernel, shape(n, cols, t_tok), stacks, pos=pos, after=[pair])
     sums = call(
-        "sums", sum_kernel, shape(t_tok // SIDE, d), [parts[0], got[1], got[2], got[3]],
+        "sums", sum_kernel, shape(t_tok // SIDE, d), [parts[0], got[1], got[3], got[2]],
         after=[turned],
     )
     got = {j: over_second(sums, j) for j in shifts}
@@ -417,7 +418,7 @@
     pair = add("pair3", pair, near, part_right, after=[inv])
     near = over_ring(pair, 1)
     quarter = call(
-        "quarter", sum_kernel, shape(t_tok // SIDE, d), [sums, got[1], got[2], got[3]],
+        "quarter", sum_kernel, shape(t_tok // SIDE, d), [sums, got[1], got[3], got[2]],
         after=[pair],
     )
     got = {k: over_first(quarter, k) for k in shifts}

time: 86.8 us -> 81.6 us (0.940)
  the two profiles are of different devices: /device:TPU:8 before, /device:TPU:0 now
where the time goes in v4:
time: 81.6 us; the launch traced here: 81.4 us
  starting transfers between devices  33.3 us (41%)
  Pallas kernels  29.6 us (36%)
  waiting for transfers between devices  16.4 us (20%)
  between operations  1.04 us (1%)
  local copies, waits for them, and re-layouts  1 us (1%)
    pallas_call x16, Pallas kernels, call(): pl.pallas_call(body, out_shape=outs, in_specs=[smem()] * lead + specs + [...  20.9 us
    ppermute x9, starting transfers between devices, over_first(): return lax.ppermute(a, ('dp', 'tensor'), plane(n_dp, True, k))  14.5 us
    ppermute x4, starting transfers between devices, over_ring(): return lax.ppermute(a, 'dp', ring_pairs(n_dp, step))  9.51 us
    ppermute x6, starting transfers between devices, over_second(): return lax.ppermute(a, ('dp', 'tensor'), plane(n_dp, False, j))  8.86 us
    pallas_call x1, Pallas kernels, residual(): pl.pallas_call(lambda *refs: residual_kernel(n_dp, *refs), in_specs=[smem...  7.01 us
    ppermute x9, waiting for transfers between devices, over_first(): return lax.ppermute(a, ('dp', 'tensor'), plane(n_dp, True, k))  6.89 us
    ppermute x4, waiting for transfers between devices, over_core(): return lax.ppermute(a, 'dp', [(i, i ^ 1) for i in range(n_dp)])  5.55 us
    ppermute x6, waiting for transfers between devices, over_second(): return lax.ppermute(a, ('dp', 'tensor'), plane(n_dp, False, j))  3.15 us
  transfers between devices with their start and end apart: 23, of which 10 were waited for; matrix products, arithmetic and copies ran while one was open for 0% of the time, Pallas kernels for 34%

profile of v4, /device:TPU:0, one launch (start us, length us, event | category | flops | bytes accessed | tf_op | source)
XLA Modules:
  0.0 81.4 jit_solution(58940476568576321)
XLA Ops:
  0.6 1.6 %collective-permute-start = (bf16[256,256]{1,0:T(8,128)(2,1)}, bf16[256,256]{1,0:T(8,128)(2,1)S(1)}, u32[]{:S(2)}, u32[]{:S(2)}) collective-permute-start(bf16[256,256]{1,0:T(8,128)(2,1)} %refs_4_.1), channel_id=1, source_target_pairs={{0,1},{1,2},{2,3},{3,0},{4,5},{5,6},{6,7},{7,4},{8,9},{9,10},{10,1... | collective-permute-start | bytes 393224 | tf_op jit(solution)/shard_map/ppermute | solution.py:346
  2.3 2.7 %collective-permute-start.1 = (bf16[256,256]{1,0:T(8,128)(2,1)}, bf16[256,256]{1,0:T(8,128)(2,1)S(1)}, u32[]{:S(2)}, u32[]{:S(2)}) collective-permute-start(bf16[256,256]{1,0:T(8,128)(2,1)} %refs_4_.1), channel_id=1, source_target_pairs={{0,2},{1,3},{2,0},{3,1},{4,6},{5,7},{6,4},{7,5},{8,10},{9,11},{10,... | collective-permute-start | bytes 393224 | tf_op jit(solution)/shard_map/ppermute | solution.py:346
  5.0 1.4 %collective-permute-start.2 = (bf16[256,256]{1,0:T(8,128)(2,1)}, bf16[256,256]{1,0:T(8,128)(2,1)S(1)}, u32[]{:S(2)}, u32[]{:S(2)}) collective-permute-start(bf16[256,256]{1,0:T(8,128)(2,1)} %refs_4_.1), channel_id=1, source_target_pairs={{0,3},{1,0},{2,1},{3,2},{4,7},{5,4},{6,5},{7,6},{8,11},{9,8},{10,9... | collective-permute-start | bytes 393224 | tf_op jit(solution)/shard_map/ppermute | solution.py:346
  6.4 3.0 %shard_map.94 = (bf16[256,896]{1,0:T(8,128)(2,1)}, bf16[256,1792]{1,0:T(8,128)(2,1)}, bf16[128,256]{1,0:T(8,128)(2,1)}, bf16[256,256]{1,0:T(8,128)(2,1)}) custom-call(bf16[256,896]{1,0:T(8,128)(2,1)} %refs_0_.1, bf16[256,896]{1,0:T(8,128)(2,1)} %refs_1_.2, bf16[256,896]{1,0:T(8,128)(2,1)} %refs_2_.2, f32[64,896]{1,0:T(8,128)} %bitcast.5, ...), custom_call_target="tpu_custom_call" | custom-call | flops 3000000000 | tf_op jit(solution)/shard_map/pallas_call | solution.py:75
  9.5 1.0 %copy-done.3 = bf16[256,256]{1,0:T(8,128)(2,1)S(1)} copy-done((bf16[256,256]{1,0:T(8,128)(2,1)S(1)}, bf16[256,256]{1,0:T(8,128)(2,1)}, u32[]{:S(2)}) %copy-start.3) | copy-done | bytes 131096
  10.5 0.1 pad_add_fusion.refs_0_.pos
  10.7 1.6 %collective-permute-start.6 = (bf16[4,256,256]{2,1,0:T(8,128)(2,1)S(1)}, bf16[4,256,256]{2,1,0:T(8,128)(2,1)S(1)}, u32[]{:S(2)}, u32[]{:S(2)}) collective-permute-start(bf16[4,256,256]{2,1,0:T(8,128)(2,1)S(1)} %shard_map.96.refs_3_.refs_2_.refs_1_.refs_4_), channel_id=1, source_target_pairs={{0,4},{1,5},{2,6},{3,7},{4,8},{5,9},{6,10},{7,11},{8,12},{9,13},{1... | collective-permute-start | bytes 1572872 | tf_op jit(solution)/shard_map/ppermute | solution.py:349
  12.3 1.7 %collective-permute-start.7 = (bf16[4,256,256]{2,1,0:T(8,128)(2,1)S(1)}, bf16[4,256,256]{2,1,0:T(8,128)(2,1)S(1)}, u32[]{:S(2)}, u32[]{:S(2)}) collective-permute-start(bf16[4,256,256]{2,1,0:T(8,128)(2,1)S(1)} %shard_map.96.refs_3_.refs_2_.refs_1_.refs_4_), channel_id=1, source_target_pairs={{0,12},{1,13},{2,14},{3,15},{4,0},{5,1},{6,2},{7,3},{8,4},{9,5},{1... | collective-permute-start | bytes 1572872 | tf_op jit(solution)/shard_map/ppermute | solution.py:349
  14.0 2.0 %collective-permute-start.8 = (bf16[4,256,256]{2,1,0:T(8,128)(2,1)S(1)}, bf16[4,256,256]{2,1,0:T(8,128)(2,1)S(1)}, u32[]{:S(2)}, u32[]{:S(2)}) collective-permute-start(bf16[4,256,256]{2,1,0:T(8,128)(2,1)S(1)} %shard_map.96.refs_3_.refs_2_.refs_1_.refs_4_), channel_id=1, source_target_pairs={{0,8},{1,9},{2,10},{3,11},{4,12},{5,13},{6,14},{7,15},{8,0},{9,1},... | collective-permute-start | bytes 1572872 | tf_op jit(solution)/shard_map/ppermute | solution.py:349
  16.0 7.6 %shard_map.97 = (f32[64,4096]{1,0:T(8,128)S(1)}, bf16[64,4096]{1,0:T(8,128)(2,1)S(1)}, bf16[64,4096]{1,0:T(8,128)(2,1)S(1)}, bf16[64,4096]{1,0:T(8,128)(2,1)S(1)}) custom-call(bf16[256,1792]{1,0:T(8,128)(2,1)S(1)} %copy-done.2, bf16[4096,896]{1,0:T(8,128)(2,1)} %refs_1_.3, bf16[4096,896]{1,0:T(8,128)(2,1)} %refs_2_.3, ...), custom_call_target="tpu_custom_call" | custom-call | flops 7000000000 | tf_op jit(solution)/shard_map/pallas_call | solution.py:75
  23.5 0.9 %collective-permute-start.3 = (bf16[64,4096]{1,0:T(8,128)(2,1)S(1)}, bf16[64,4096]{1,0:T(8,128)(2,1)S(1)}, u32[]{:S(2)}, u32[]{:S(2)}) collective-permute-start(bf16[64,4096]{1,0:T(8,128)(2,1)S(1)} %get-tuple-element.25), channel_id=1, source_target_pairs={{0,1},{1,2},{2,3},{3,0},{4,5},{5,6},{6,7},{7,4},{8,9},{9,10},{10,1... | collective-permute-start | bytes 1572872 | tf_op jit(solution)/shard_map/ppermute | solution.py:346
  24.4 2.4 %collective-permute-start.4 = (bf16[64,4096]{1,0:T(8,128)(2,1)S(1)}, bf16[64,4096]{1,0:T(8,128)(2,1)S(1)}, u32[]{:S(2)}, u32[]{:S(2)}) collective-permute-start(bf16[64,4096]{1,0:T(8,128)(2,1)S(1)} %get-tuple-element.26), channel_id=1, source_target_pairs={{0,3},{1,0},{2,1},{3,2},{4,7},{5,4},{6,5},{7,6},{8,11},{9,8},{10,9... | collective-permute-start | bytes 1572872 | tf_op jit(solution)/shard_map/ppermute | solution.py:346
  26.8 0.7 collective-permute-start.5
  27.5 3.1 %collective-permute-done.8.refs_5_.refs_4_.refs_7_ = bf16[4,256,256]{2,1,0:T(8,128)(2,1)S(1)} collective-permute-done((bf16[4,256,256]{2,1,0:T(8,128)(2,1)S(1)}, bf16[4,256,256]{2,1,0:T(8,128)(2,1)S(1)}, u32[]{:S(2)}, u32[]{:S(2)}) %collective-permute-start.8) | collective-permute-done | bytes 524320 | tf_op jit(solution)/shard_map/ppermute | solution.py:349
  30.6 1.0 %shard_map.98 = (f32[8,64,256]{2,1,0:T(8,128)S(1)}, bf16[8,64,256]{2,1,0:T(8,128)(2,1)S(1)}) custom-call(s32[3]{0:T(128)S(1)} %pad_add_fusion.refs_0_.pos, bf16[128,256]{1,0:T(8,128)(2,1)S(1)} %copy-done.1, bf16[4,256,256]{2,1,0:T(8,128)(2,1)S(1)} %shard_map.96.refs_3_.refs_2_.refs_1_.refs_4_, ...), custom_call_target="tpu_custom_call" | custom-call | flops 1000000000 | tf_op jit(solution)/shard_map/pallas_call | solution.py:75
  31.7 0.1 collective-permute-start.9
  31.8 1.5 %collective-permute-done.9.refs_1_ = bf16[8,64,256]{2,1,0:T(8,128)(2,1)S(1)} collective-permute-done((bf16[8,64,256]{2,1,0:T(8,128)(2,1)S(1)}, bf16[8,64,256]{2,1,0:T(8,128)(2,1)S(1)}, u32[]{:S(2)}, u32[]{:S(2)}) %collective-permute-start.9) | collective-permute-done | bytes 262176 | tf_op jit(solution)/shard_map/ppermute | solution.py:355
  33.3 0.1 shard_map.99.refs_5_.refs_0_
  33.4 2.0 %collective-permute-start.13 = (bf16[8,64,256]{2,1,0:T(8,128)(2,1)S(1)}, bf16[8,64,256]{2,1,0:T(8,128)(2,1)S(1)}, u32[]{:S(2)}, u32[]{:S(2)}) collective-permute-start(bf16[8,64,256]{2,1,0:T(8,128)(2,1)S(1)} %shard_map.99.refs_5_.refs_0_), channel_id=1, source_target_pairs={{0,32},{16,112},{32,0},{48,80},{64,96},{80,48},{96,64},{112,16},{1... | collective-permute-start | bytes 786440 | tf_op jit(solution)/shard_map/ppermute | solution.py:352
  35.4 1.1 %shard_map.100.refs_4_.refs_6_ = bf16[16,256,256]{2,1,0:T(8,128)(2,1)S(1)} custom-call(s32[3]{0:T(128)S(1)} %pad_add_fusion.refs_0_.pos, bf16[4,256,256]{2,1,0:T(8,128)(2,1)S(1)} %shard_map.96.refs_3_.refs_2_.refs_1_.refs_4_, bf16[4,256,256]{2,1,0:T(8,128)(2,1)S(1)} %collective-permute-done.6.refs_3_.refs_2_.refs_5_, ...), custom_call_target="tpu_custom_call" | custom-call | flops 1000000000 | tf_op jit(solution)/shard_map/pallas_call | solution.py:75
  36.5 2.6 %collective-permute-done.4.refs_2_ = bf16[64,4096]{1,0:T(8,128)(2,1)S(1)} collective-permute-done((bf16[64,4096]{1,0:T(8,128)(2,1)S(1)}, bf16[64,4096]{1,0:T(8,128)(2,1)S(1)}, u32[]{:S(2)}, u32[]{:S(2)}) %collective-permute-start.4) | collective-permute-done | bytes 524320 | tf_op jit(solution)/shard_map/ppermute | solution.py:346
  39.2 0.9 %collective-permute-done.5.refs_3_ = bf16[64,4096]{1,0:T(8,128)(2,1)S(1)} collective-permute-done((bf16[64,4096]{1,0:T(8,128)(2,1)S(1)}, bf16[64,4096]{1,0:T(8,128)(2,1)S(1)}, u32[]{:S(2)}, u32[]{:S(2)}) %collective-permute-start.5) | collective-permute-done | bytes 524320 | tf_op jit(solution)/shard_map/ppermute | solution.py:346
  40.0 0.3 shard_map.101.refs_2_.refs_0_
  40.3 0.1 shard_map.102.refs_0_
  40.4 4.1 %collective-permute-start.14 = (bf16[8,64,256]{2,1,0:T(8,128)(2,1)S(1)}, bf16[8,64,256]{2,1,0:T(8,128)(2,1)S(1)}, u32[]{:S(2)}, u32[]{:S(2)}) collective-permute-start(bf16[8,64,256]{2,1,0:T(8,128)(2,1)S(1)} %shard_map.102.refs_0_), channel_id=1, source_target_pairs={{0,96},{16,48},{32,64},{48,16},{64,32},{80,112},{96,0},{112,80},{1... | collective-permute-start | bytes 786440 | tf_op jit(solution)/shard_map/ppermute | solution.py:352
  44.5 1.2 %collective-permute-start.10 = (bf16[64,4096]{1,0:T(8,128)(2,1)S(1)}, bf16[64,4096]{1,0:T(8,128)(2,1)S(1)}, u32[]{:S(2)}, u32[]{:S(2)}) collective-permute-start(bf16[64,4096]{1,0:T(8,128)(2,1)S(1)} %shard_map.101.refs_2_.refs_0_), channel_id=1, source_target_pairs={{0,4},{1,5},{2,6},{3,7},{4,8},{5,9},{6,10},{7,11},{8,12},{9,13},{1... | collective-permute-start | bytes 1572872 | tf_op jit(solution)/shard_map/ppermute | solution.py:349
  45.7 2.0 %collective-permute-start.11 = (bf16[64,4096]{1,0:T(8,128)(2,1)S(1)}, bf16[64,4096]{1,0:T(8,128)(2,1)S(1)}, u32[]{:S(2)}, u32[]{:S(2)}) collective-permute-start(bf16[64,4096]{1,0:T(8,128)(2,1)S(1)} %shard_map.101.refs_2_.refs_0_), channel_id=1, source_target_pairs={{0,12},{1,13},{2,14},{3,15},{4,0},{5,1},{6,2},{7,3},{8,4},{9,5},{1... | collective-permute-start | bytes 1572872 | tf_op jit(solution)/shard_map/ppermute | solution.py:349
  47.7 0.3 collective-permute-start.12
  48.1 0.8 collective-permute-done.14.refs_1_
  48.9 0.1 shard_map.103.refs_1_
  48.9 0.1 collective-permute-start.15
  49.0 1.5 %collective-permute-done.15.refs_2_ = bf16[8,64,256]{2,1,0:T(8,128)(2,1)S(1)} collective-permute-done((bf16[8,64,256]{2,1,0:T(8,128)(2,1)S(1)}, bf16[8,64,256]{2,1,0:T(8,128)(2,1)S(1)}, u32[]{:S(2)}, u32[]{:S(2)}) %collective-permute-start.15) | collective-permute-done | bytes 262176 | tf_op jit(solution)/shard_map/ppermute | solution.py:355
  50.5 1.9 %shard_map.104 = (bf16[16,64,256]{2,1,0:T(8,128)(2,1)S(1)}, f32[32,896]{1,0:T(8,128)S(1)}, f32[32,896]{1,0:T(8,128)S(1)}, f32[64,64]{1,0:T(8,128)S(1)}) custom-call(s32[3]{0:T(128)S(1)} %pad_add_fusion.refs_0_.pos, bf16[8,64,256]{2,1,0:T(8,128)(2,1)S(1)} %shard_map.103.refs_1_, bf16[8,64,256]{2,1,0:T(8,128)(2,1)S(1)} %collective-permute-done.15.refs_2_, ...), custom_call_target="tpu_custom_call" | custom-call | flops 100000000 | tf_op jit(solution)/shard_map/pallas_call | solution.py:75
  52.4 0.2 collective-permute-start.16
  52.6 1.2 %collective-permute-done.16.refs_1_ = f32[32,896]{1,0:T(8,128)S(1)} collective-permute-done((f32[32,896]{1,0:T(8,128)S(1)}, f32[32,896]{1,0:T(8,128)S(1)}, u32[]{:S(2)}, u32[]{:S(2)}) %collective-permute-start.16) | collective-permute-done | bytes 114720 | tf_op jit(solution)/shard_map/ppermute | solution.py:355
  53.8 0.1 collective-permute-start.17
  53.9 5.4 %shard_map.106 = (f32[64,64]{1,0:T(8,128)S(1)}, bf16[16,256,128]{2,1,0:T(8,128)(2,1)S(1)}) custom-call(f32[64,64]{1,0:T(8,128)S(1)} %get-tuple-element.34.refs_0_, bf16[16,64,256]{2,1,0:T(8,128)(2,1)S(1)} %get-tuple-element.35.refs_1_, f32[32,896]{1,0:T(8,128)S(1)} %shard_map.105.refs_2_.refs_0_), custom_call_target="tpu_custom_call" | custom-call | flops 500000000 | tf_op jit(solution)/shard_map/pallas_call | solution.py:75
  59.4 3.3 %collective-permute-start.21 = (f32[32,896]{1,0:T(8,128)S(1)}, f32[32,896]{1,0:T(8,128)S(1)}, u32[]{:S(2)}, u32[]{:S(2)}) collective-permute-start(f32[32,896]{1,0:T(8,128)S(1)} %shard_map.107.refs_4_.refs_0_), channel_id=1, source_target_pairs={{0,96},{16,48},{32,64},{48,16},{64,32},{80,112},{96,0},{112,80},{1... | collective-permute-start | bytes 344072 | tf_op jit(solution)/shard_map/ppermute | solution.py:352
  62.7 0.3 shard_map.108.refs_2_.refs_7_
  63.0 1.5 %collective-permute-start.18 = (bf16[64,4096]{1,0:T(8,128)(2,1)S(1)}, bf16[64,4096]{1,0:T(8,128)(2,1)S(1)}, u32[]{:S(2)}, u32[]{:S(2)}) collective-permute-start(bf16[64,4096]{1,0:T(8,128)(2,1)S(1)} %shard_map.108.refs_2_.refs_7_), channel_id=1, source_target_pairs={{0,2},{1,3},{2,0},{3,1},{4,6},{5,7},{6,4},{7,5},{8,10},{9,11},{10,... | collective-permute-start | bytes 1572872 | tf_op jit(solution)/shard_map/ppermute | solution.py:346
  64.5 2.3 %collective-permute-start.19 = (bf16[64,4096]{1,0:T(8,128)(2,1)S(1)}, bf16[64,4096]{1,0:T(8,128)(2,1)S(1)}, u32[]{:S(2)}, u32[]{:S(2)}) collective-permute-start(bf16[64,4096]{1,0:T(8,128)(2,1)S(1)} %shard_map.108.refs_2_.refs_7_), channel_id=1, source_target_pairs={{0,1},{1,2},{2,3},{3,0},{4,5},{5,6},{6,7},{7,4},{8,9},{9,10},{10,1... | collective-permute-start | bytes 1572872 | tf_op jit(solution)/shard_map/ppermute | solution.py:346
  66.7 1.0 %collective-permute-start.20 = (bf16[64,4096]{1,0:T(8,128)(2,1)S(1)}, bf16[64,4096]{1,0:T(8,128)(2,1)S(1)}, u32[]{:S(2)}, u32[]{:S(2)}) collective-permute-start(bf16[64,4096]{1,0:T(8,128)(2,1)S(1)} %shard_map.108.refs_2_.refs_7_), channel_id=1, source_target_pairs={{0,3},{1,0},{2,1},{3,2},{4,7},{5,4},{6,5},{7,6},{8,11},{9,8},{10,9... | collective-permute-start | bytes 1572872 | tf_op jit(solution)/shard_map/ppermute | solution.py:346
  67.7 0.1 collective-permute-start.22
  67.8 1.3 %collective-permute-done.22.refs_2_ = f32[32,896]{1,0:T(8,128)S(1)} collective-permute-done((f32[32,896]{1,0:T(8,128)S(1)}, f32[32,896]{1,0:T(8,128)S(1)}, u32[]{:S(2)}, u32[]{:S(2)}) %collective-permute-start.22) | collective-permute-done | bytes 114720 | tf_op jit(solution)/shard_map/ppermute | solution.py:355
  69.1 7.0 %shard_map.110 = (f32[64,896]{1,0:T(8,128)}, bf16[4096,896]{1,0:T(8,128)(2,1)}, bf16[256,4096]{1,0:T(8,128)(2,1)}) custom-call(s32[3]{0:T(128)S(1)} %pad_add_fusion.refs_0_.pos, f32[32,896]{1,0:T(8,128)S(1)} %shard_map.109.refs_1_, f32[32,896]{1,0:T(8,128)S(1)} %collective-permute-done.22.refs_2_, f32[64,64]{1,0:T(8,128)S(1)} %get-tuple-element.36.refs_2_.refs_3_, ...), custom_call_target="tpu_custom_call" | custom-call | flops 3600000000 | tf_op jit(solution)/shard_map/pallas_call | solution.py:295
  76.2 3.2 %collective-permute-done.19.refs_1_ = bf16[64,4096]{1,0:T(8,128)(2,1)S(1)} collective-permute-done((bf16[64,4096]{1,0:T(8,128)(2,1)S(1)}, bf16[64,4096]{1,0:T(8,128)(2,1)S(1)}, u32[]{:S(2)}, u32[]{:S(2)}) %collective-permute-start.19) | collective-permute-done | bytes 524320 | tf_op jit(solution)/shard_map/ppermute | solution.py:346
  79.4 0.2 collective-permute-done.20.refs_2_
  79.6 1.7 %shard_map.111 = bf16[256,4096]{1,0:T(8,128)(2,1)} custom-call(s32[3]{0:T(128)S(1)} %pad_add_fusion.refs_0_.pos, bf16[64,4096]{1,0:T(8,128)(2,1)S(1)} %collective-permute-done.18.refs_0_, bf16[64,4096]{1,0:T(8,128)(2,1)S(1)} %collective-permute-done.19.refs_1_, bf16[64,4096]{1,0:T(8,128)(2,1)S(1)} %collective-permute-done.20.refs_2_, ...), custom_call_target="tpu_custom_call", output_to_operand_aliasing={{}: (4, {})} | custom-call | flops 500000000 | tf_op jit(solution)/shard_map/pallas_call | solution.py:193
  (25 shorter events, 0.1 us)
Async XLA Ops:
  0.6 10.0 %collective-permute-start = (bf16[256,256]{1,0:T(8,128)(2,1)}, bf16[256,256]{1,0:T(8,128)(2,1)S(1)}, u32[]{:S(2)}, u32[]{:S(2)}) collective-permute-start(bf16[256,256]{1,0:T(8,128)(2,1)} %refs_4_.1), channel_id=1, source_target_pairs={{0,1},{1,2},{2,3},{3,0},{4,5},{5,6},{6,7},{7,4},{8,9},{9,10},{10,1... | collective-permute-start | bytes 393224 | tf_op jit(solution)/shard_map/ppermute | solution.py:346
  2.3 8.3 %collective-permute-start.1 = (bf16[256,256]{1,0:T(8,128)(2,1)}, bf16[256,256]{1,0:T(8,128)(2,1)S(1)}, u32[]{:S(2)}, u32[]{:S(2)}) collective-permute-start(bf16[256,256]{1,0:T(8,128)(2,1)} %refs_4_.1), channel_id=1, source_target_pairs={{0,2},{1,3},{2,0},{3,1},{4,6},{5,7},{6,4},{7,5},{8,10},{9,11},{10,... | collective-permute-start | bytes 393224 | tf_op jit(solution)/shard_map/ppermute | solution.py:346
  5.0 5.6 %collective-permute-start.2 = (bf16[256,256]{1,0:T(8,128)(2,1)}, bf16[256,256]{1,0:T(8,128)(2,1)S(1)}, u32[]{:S(2)}, u32[]{:S(2)}) collective-permute-start(bf16[256,256]{1,0:T(8,128)(2,1)} %refs_4_.1), channel_id=1, source_target_pairs={{0,3},{1,0},{2,1},{3,2},{4,7},{5,4},{6,5},{7,6},{8,11},{9,8},{10,9... | collective-permute-start | bytes 393224 | tf_op jit(solution)/shard_map/ppermute | solution.py:346
  9.5 6.5 %copy-start.2 = (bf16[256,1792]{1,0:T(8,128)(2,1)S(1)}, bf16[256,1792]{1,0:T(8,128)(2,1)}, u32[]{:S(2)}) copy-start(bf16[256,1792]{1,0:T(8,128)(2,1)} %get-tuple-element.22.refs_0_) | copy-start | bytes 2752516
  9.5 1.0 %copy-start.3 = (bf16[256,256]{1,0:T(8,128)(2,1)S(1)}, bf16[256,256]{1,0:T(8,128)(2,1)}, u32[]{:S(2)}) copy-start(bf16[256,256]{1,0:T(8,128)(2,1)} %get-tuple-element.23.refs_0_) | copy-start | bytes 393220
  10.7 16.2 %collective-permute-start.6 = (bf16[4,256,256]{2,1,0:T(8,128)(2,1)S(1)}, bf16[4,256,256]{2,1,0:T(8,128)(2,1)S(1)}, u32[]{:S(2)}, u32[]{:S(2)}) collective-permute-start(bf16[4,256,256]{2,1,0:T(8,128)(2,1)S(1)} %shard_map.96.refs_3_.refs_2_.refs_1_.refs_4_), channel_id=1, source_target_pairs={{0,4},{1,5},{2,6},{3,7},{4,8},{5,9},{6,10},{7,11},{8,12},{9,13},{1... | collective-permute-start | bytes 1572872 | tf_op jit(solution)/shard_map/ppermute | solution.py:349
  12.3 15.2 %collective-permute-start.7 = (bf16[4,256,256]{2,1,0:T(8,128)(2,1)S(1)}, bf16[4,256,256]{2,1,0:T(8,128)(2,1)S(1)}, u32[]{:S(2)}, u32[]{:S(2)}) collective-permute-start(bf16[4,256,256]{2,1,0:T(8,128)(2,1)S(1)} %shard_map.96.refs_3_.refs_2_.refs_1_.refs_4_), channel_id=1, source_target_pairs={{0,12},{1,13},{2,14},{3,15},{4,0},{5,1},{6,2},{7,3},{8,4},{9,5},{1... | collective-permute-start | bytes 1572872 | tf_op jit(solution)/shard_map/ppermute | solution.py:349
  14.0 16.7 %collective-permute-start.8 = (bf16[4,256,256]{2,1,0:T(8,128)(2,1)S(1)}, bf16[4,256,256]{2,1,0:T(8,128)(2,1)S(1)}, u32[]{:S(2)}, u32[]{:S(2)}) collective-permute-start(bf16[4,256,256]{2,1,0:T(8,128)(2,1)S(1)} %shard_map.96.refs_3_.refs_2_.refs_1_.refs_4_), channel_id=1, source_target_pairs={{0,8},{1,9},{2,10},{3,11},{4,12},{5,13},{6,14},{7,15},{8,0},{9,1},... | collective-permute-start | bytes 1572872 | tf_op jit(solution)/shard_map/ppermute | solution.py:349
  16.0 14.7 %copy-start.1 = (bf16[128,256]{1,0:T(8,128)(2,1)S(1)}, bf16[128,256]{1,0:T(8,128)(2,1)}, u32[]{:S(2)}) copy-start(bf16[128,256]{1,0:T(8,128)(2,1)} %get-tuple-element.28.refs_1_) | copy-start | bytes 196612
  23.5 13.0 %collective-permute-start.3 = (bf16[64,4096]{1,0:T(8,128)(2,1)S(1)}, bf16[64,4096]{1,0:T(8,128)(2,1)S(1)}, u32[]{:S(2)}, u32[]{:S(2)}) collective-permute-start(bf16[64,4096]{1,0:T(8,128)(2,1)S(1)} %get-tuple-element.25), channel_id=1, source_target_pairs={{0,1},{1,2},{2,3},{3,0},{4,5},{5,6},{6,7},{7,4},{8,9},{9,10},{10,1... | collective-permute-start | bytes 1572872 | tf_op jit(solution)/shard_map/ppermute | solution.py:346
  24.4 14.8 %collective-permute-start.4 = (bf16[64,4096]{1,0:T(8,128)(2,1)S(1)}, bf16[64,4096]{1,0:T(8,128)(2,1)S(1)}, u32[]{:S(2)}, u32[]{:S(2)}) collective-permute-start(bf16[64,4096]{1,0:T(8,128)(2,1)S(1)} %get-tuple-element.26), channel_id=1, source_target_pairs={{0,3},{1,0},{2,1},{3,2},{4,7},{5,4},{6,5},{7,6},{8,11},{9,8},{10,9... | collective-permute-start | bytes 1572872 | tf_op jit(solution)/shard_map/ppermute | solution.py:346
  26.8 13.2 %collective-permute-start.5 = (bf16[64,4096]{1,0:T(8,128)(2,1)S(1)}, bf16[64,4096]{1,0:T(8,128)(2,1)S(1)}, u32[]{:S(2)}, u32[]{:S(2)}) collective-permute-start(bf16[64,4096]{1,0:T(8,128)(2,1)S(1)} %get-tuple-element.27), channel_id=1, source_target_pairs={{0,2},{1,3},{2,0},{3,1},{4,6},{5,7},{6,4},{7,5},{8,10},{9,11},{10,... | collective-permute-start | bytes 1572872 | tf_op jit(solution)/shard_map/ppermute | solution.py:346
  31.7 18.8 %copy-start = (bf16[256,896]{1,0:T(8,128)(2,1)S(1)}, bf16[256,896]{1,0:T(8,128)(2,1)}, u32[]{:S(2)}) copy-start(bf16[256,896]{1,0:T(8,128)(2,1)} %get-tuple-element.31.refs_3_.refs_4_) | copy-start | bytes 1376260
  31.7 1.6 %collective-permute-start.9 = (bf16[8,64,256]{2,1,0:T(8,128)(2,1)S(1)}, bf16[8,64,256]{2,1,0:T(8,128)(2,1)S(1)}, u32[]{:S(2)}, u32[]{:S(2)}) collective-permute-start(bf16[8,64,256]{2,1,0:T(8,128)(2,1)S(1)} %get-tuple-element.30), channel_id=1, source_target_pairs={{0,16},{16,0},{32,48},{48,32},{64,80},{80,64},{96,112},{112,96},{1... | collective-permute-start | bytes 786440 | tf_op jit(solution)/shard_map/ppermute | solution.py:355
  33.4 6.9 %collective-permute-start.13 = (bf16[8,64,256]{2,1,0:T(8,128)(2,1)S(1)}, bf16[8,64,256]{2,1,0:T(8,128)(2,1)S(1)}, u32[]{:S(2)}, u32[]{:S(2)}) collective-permute-start(bf16[8,64,256]{2,1,0:T(8,128)(2,1)S(1)} %shard_map.99.refs_5_.refs_0_), channel_id=1, source_target_pairs={{0,32},{16,112},{32,0},{48,80},{64,96},{80,48},{96,64},{112,16},{1... | collective-permute-start | bytes 786440 | tf_op jit(solution)/shard_map/ppermute | solution.py:352
  40.4 8.5 %collective-permute-start.14 = (bf16[8,64,256]{2,1,0:T(8,128)(2,1)S(1)}, bf16[8,64,256]{2,1,0:T(8,128)(2,1)S(1)}, u32[]{:S(2)}, u32[]{:S(2)}) collective-permute-start(bf16[8,64,256]{2,1,0:T(8,128)(2,1)S(1)} %shard_map.102.refs_0_), channel_id=1, source_target_pairs={{0,96},{16,48},{32,64},{48,16},{64,32},{80,112},{96,0},{112,80},{1... | collective-permute-start | bytes 786440 | tf_op jit(solution)/shard_map/ppermute | solution.py:352
  44.5 18.2 %collective-permute-start.10 = (bf16[64,4096]{1,0:T(8,128)(2,1)S(1)}, bf16[64,4096]{1,0:T(8,128)(2,1)S(1)}, u32[]{:S(2)}, u32[]{:S(2)}) collective-permute-start(bf16[64,4096]{1,0:T(8,128)(2,1)S(1)} %shard_map.101.refs_2_.refs_0_), channel_id=1, source_target_pairs={{0,4},{1,5},{2,6},{3,7},{4,8},{5,9},{6,10},{7,11},{8,12},{9,13},{1... | collective-permute-start | bytes 1572872 | tf_op jit(solution)/shard_map/ppermute | solution.py:349
  45.7 17.0 %collective-permute-start.11 = (bf16[64,4096]{1,0:T(8,128)(2,1)S(1)}, bf16[64,4096]{1,0:T(8,128)(2,1)S(1)}, u32[]{:S(2)}, u32[]{:S(2)}) collective-permute-start(bf16[64,4096]{1,0:T(8,128)(2,1)S(1)} %shard_map.101.refs_2_.refs_0_), channel_id=1, source_target_pairs={{0,12},{1,13},{2,14},{3,15},{4,0},{5,1},{6,2},{7,3},{8,4},{9,5},{1... | collective-permute-start | bytes 1572872 | tf_op jit(solution)/shard_map/ppermute | solution.py:349
  47.7 14.9 %collective-permute-start.12 = (bf16[64,4096]{1,0:T(8,128)(2,1)S(1)}, bf16[64,4096]{1,0:T(8,128)(2,1)S(1)}, u32[]{:S(2)}, u32[]{:S(2)}) collective-permute-start(bf16[64,4096]{1,0:T(8,128)(2,1)S(1)} %shard_map.101.refs_2_.refs_0_), channel_id=1, source_target_pairs={{0,8},{1,9},{2,10},{3,11},{4,12},{5,13},{6,14},{7,15},{8,0},{9,1},... | collective-permute-start | bytes 1572872 | tf_op jit(solution)/shard_map/ppermute | solution.py:349
  48.9 1.6 %collective-permute-start.15 = (bf16[8,64,256]{2,1,0:T(8,128)(2,1)S(1)}, bf16[8,64,256]{2,1,0:T(8,128)(2,1)S(1)}, u32[]{:S(2)}, u32[]{:S(2)}) collective-permute-start(bf16[8,64,256]{2,1,0:T(8,128)(2,1)S(1)} %shard_map.103.refs_1_), channel_id=1, source_target_pairs={{0,16},{16,0},{32,48},{48,32},{64,80},{80,64},{96,112},{112,96},{1... | collective-permute-start | bytes 786440 | tf_op jit(solution)/shard_map/ppermute | solution.py:355
  52.4 1.4 %collective-permute-start.16 = (f32[32,896]{1,0:T(8,128)S(1)}, f32[32,896]{1,0:T(8,128)S(1)}, u32[]{:S(2)}, u32[]{:S(2)}) collective-permute-start(f32[32,896]{1,0:T(8,128)S(1)} %get-tuple-element.33), channel_id=1, source_target_pairs={{0,16},{16,0},{32,48},{48,32},{64,80},{80,64},{96,112},{112,96},{1... | collective-permute-start | bytes 344072 | tf_op jit(solution)/shard_map/ppermute | solution.py:355
  53.8 5.5 %collective-permute-start.17 = (f32[32,896]{1,0:T(8,128)S(1)}, f32[32,896]{1,0:T(8,128)S(1)}, u32[]{:S(2)}, u32[]{:S(2)}) collective-permute-start(f32[32,896]{1,0:T(8,128)S(1)} %shard_map.105.refs_2_.refs_0_), channel_id=1, source_target_pairs={{0,32},{16,112},{32,0},{48,80},{64,96},{80,48},{96,64},{112,16},{1... | collective-permute-start | bytes 344072 | tf_op jit(solution)/shard_map/ppermute | solution.py:352
  59.4 8.3 %collective-permute-start.21 = (f32[32,896]{1,0:T(8,128)S(1)}, f32[32,896]{1,0:T(8,128)S(1)}, u32[]{:S(2)}, u32[]{:S(2)}) collective-permute-start(f32[32,896]{1,0:T(8,128)S(1)} %shard_map.107.refs_4_.refs_0_), channel_id=1, source_target_pairs={{0,96},{16,48},{32,64},{48,16},{64,32},{80,112},{96,0},{112,80},{1... | collective-permute-start | bytes 344072 | tf_op jit(solution)/shard_map/ppermute | solution.py:352
  63.0 13.2 %collective-permute-start.18 = (bf16[64,4096]{1,0:T(8,128)(2,1)S(1)}, bf16[64,4096]{1,0:T(8,128)(2,1)S(1)}, u32[]{:S(2)}, u32[]{:S(2)}) collective-permute-start(bf16[64,4096]{1,0:T(8,128)(2,1)S(1)} %shard_map.108.refs_2_.refs_7_), channel_id=1, source_target_pairs={{0,2},{1,3},{2,0},{3,1},{4,6},{5,7},{6,4},{7,5},{8,10},{9,11},{10,... | collective-permute-start | bytes 1572872 | tf_op jit(solution)/shard_map/ppermute | solution.py:346
  64.5 14.9 %collective-permute-start.19 = (bf16[64,4096]{1,0:T(8,128)(2,1)S(1)}, bf16[64,4096]{1,0:T(8,128)(2,1)S(1)}, u32[]{:S(2)}, u32[]{:S(2)}) collective-permute-start(bf16[64,4096]{1,0:T(8,128)(2,1)S(1)} %shard_map.108.refs_2_.refs_7_), channel_id=1, source_target_pairs={{0,1},{1,2},{2,3},{3,0},{4,5},{5,6},{6,7},{7,4},{8,9},{9,10},{10,1... | collective-permute-start | bytes 1572872 | tf_op jit(solution)/shard_map/ppermute | solution.py:346
  66.7 12.8 %collective-permute-start.20 = (bf16[64,4096]{1,0:T(8,128)(2,1)S(1)}, bf16[64,4096]{1,0:T(8,128)(2,1)S(1)}, u32[]{:S(2)}, u32[]{:S(2)}) collective-permute-start(bf16[64,4096]{1,0:T(8,128)(2,1)S(1)} %shard_map.108.refs_2_.refs_7_), channel_id=1, source_target_pairs={{0,3},{1,0},{2,1},{3,2},{4,7},{5,4},{6,5},{7,6},{8,11},{9,8},{10,9... | collective-permute-start | bytes 1572872 | tf_op jit(solution)/shard_map/ppermute | solution.py:346
  67.7 1.4 %collective-permute-start.22 = (f32[32,896]{1,0:T(8,128)S(1)}, f32[32,896]{1,0:T(8,128)S(1)}, u32[]{:S(2)}, u32[]{:S(2)}) collective-permute-start(f32[32,896]{1,0:T(8,128)S(1)} %shard_map.109.refs_1_), channel_id=1, source_target_pairs={{0,16},{16,0},{32,48},{48,32},{64,80},{80,64},{96,112},{112,96},{1... | collective-permute-start | bytes 344072 | tf_op jit(solution)/shard_map/ppermute | solution.py:355

commit v5 on v4

--- a/solution.py
+++ b/solution.py
@@ -20,7 +20,7 @@
     "mine": 0.1,
     "right": 0.1,
     "pair2": 0.1,
-    "cholesky": 0.5,
+    "cholesky": 0.3,
     "pair3": 0.1,
     "turn": 1,
     "quarter": 0.6,
@@ -28,6 +28,7 @@
     "residual": 3.6,
     "rows": 0.5,
     "own": 3,
+    "inverse": 0.2,
 }
 
 
@@ -238,19 +239,31 @@
     send[...] = jnp.where(pos[2] == 0, high, low)
 
 
-def cholesky_kernel(gram, left, out, left_n):
+def eliminate(a, steps):
+    row_id = lax.broadcasted_iota(jnp.int32, (a.shape[0], 1), 0)
+    for k in steps:
+        row = a[k:k + 1, :]
+        scale = jnp.where(row_id > k, a[:, k:k + 1] / a[k:k + 1, k:k + 1], 0.0)
+        a = a - scale * row
+    return a
+
+
+def diagonal(r, shift):
+    row_id = lax.broadcasted_iota(jnp.int32, (r, 2 * r), 0)
+    return row_id + shift == lax.broadcasted_iota(jnp.int32, (r, 2 * r), 1)
+
+
+def cholesky_kernel(gram, out):
     r = gram.shape[0]
-    row_id = lax.broadcasted_iota(jnp.int32, (r, 2 * r), 0)
-    lane_id = lax.broadcasted_iota(jnp.int32, (r, 2 * r), 1)
-    eye = jnp.where(row_id + r == lane_id, 1.0, 0.0).astype(F32)
+    eye = jnp.where(diagonal(r, r), 1.0, 0.0).astype(F32)
     a = jnp.concatenate([gram[...], jnp.zeros((r, r), F32)], 1) + eye
-    for k in range(r):
-        row = a[k:k + 1, :]
-        col = a[:, k:k + 1]
-        pivot = a[k:k + 1, k:k + 1]
-        scale = jnp.where(row_id[:, :1] > k, col / pivot, 0.0)
-        a = a - scale * row
-    diag = jnp.sum(jnp.where(row_id == lane_id, a, 0.0), axis=1, keepdims=True)
+    out[...] = eliminate(a, range(r * 11 // 16))
+
+
+def inverse_kernel(half, left, out, left_n):
+    r = half.shape[0]
+    a = eliminate(half[...], range(r * 11 // 16, r))
+    diag = jnp.sum(jnp.where(diagonal(r, 0), a, 0.0), axis=1, keepdims=True)
     out[...] = a[:, r:] / jnp.sqrt(diag)
     for s in range(left.shape[0]):
         left_n[s] = jnp.concatenate([left[s], left[s]], 0).T
@@ -411,18 +424,19 @@
     part_right = shape(r // 2, width, dtype=F32)
     pair = add("pair2", keep, over_core(send), part_right)
     near = over_ring(pair, 0)
-    inv, left_n = call(
-        "cholesky", cholesky_kernel, [shape(r, r, dtype=F32), shape(n, cols, 2 * r)], [gram, left],
-        after=[pair],
-    )
-    pair = add("pair3", pair, near, part_right, after=[inv])
+    half = call("cholesky", cholesky_kernel, shape(r, 2 * r, dtype=F32), [gram], after=[pair])
+    pair = add("pair3", pair, near, part_right, after=[half])
     near = over_ring(pair, 1)
     quarter = call(
         "quarter", sum_kernel, shape(t_tok // SIDE, d), [sums, got[1], got[3], got[2]],
         after=[pair],
     )
     got = {k: over_first(quarter, k) for k in shifts}
-    mine = add("mine2", pair, near, part_right, after=[quarter])
+    inv, left_n = call(
+        "inverse", inverse_kernel, [shape(r, r, dtype=F32), shape(n, cols, 2 * r)], [half, left],
+        after=[quarter],
+    )
+    mine = add("mine2", pair, near, part_right, after=[inv])
     other = over_core(mine)
     gate_q_t, error, rows = residual(pos, mine, other, inv, gate, left_n, turned, quarter, n_dp)
     grad_input = put_rows((2, 1, 3), pos, [got[k] for k in (2, 1, 3)], rows)

time: 81.6 us -> 80.9 us (level)
    ppermute x9, waiting for transfers between devices: 6.89 us -> 5.14 us  [over_first(): return lax.ppermute(a, ('dp', 'tensor'), plane(n_dp, True, k))]
    ppermute x4, waiting for transfers between devices: 0.79 us -> 1.9 us  [over_ring(): return lax.ppermute(a, 'dp', ring_pairs(n_dp, step))]
    pallas_call x16 -> x17, Pallas kernels: 20.9 us -> 20.8 us  [call(): pl.pallas_call(body, out_shape=outs, in_specs=[smem()] * lead + specs + [...]
  transfers between devices with their start and end apart: 23 -> 23, of which waited for: 10 -> 11; matrix products, arithmetic and copies ran while one was open for 0% -> 0% of each run, Pallas kernels for 34% -> 34%
where the time goes in v5:
time: 80.9 us; the launch traced here: 80.7 us
  starting transfers between devices  33.3 us (41%)
  Pallas kernels  29.5 us (36%)
  waiting for transfers between devices  15.7 us (19%)
  between operations  1.04 us (1%)
  local copies, waits for them, and re-layouts  1 us (1%)
    pallas_call x17, Pallas kernels, call(): pl.pallas_call(body, out_shape=outs, in_specs=[smem()] * lead + specs + [...  20.8 us
    ppermute x9, starting transfers between devices, over_first(): return lax.ppermute(a, ('dp', 'tensor'), plane(n_dp, True, k))  14.5 us
    ppermute x4, starting transfers between devices, over_ring(): return lax.ppermute(a, 'dp', ring_pairs(n_dp, step))  9.51 us
    ppermute x6, starting transfers between devices, over_second(): return lax.ppermute(a, ('dp', 'tensor'), plane(n_dp, False, j))  8.86 us
    pallas_call x1, Pallas kernels, residual(): pl.pallas_call(lambda *refs: residual_kernel(n_dp, *refs), in_specs=[smem...  7.03 us
    ppermute x4, waiting for transfers between devices, over_core(): return lax.ppermute(a, 'dp', [(i, i ^ 1) for i in range(n_dp)])  5.55 us
    ppermute x9, waiting for transfers between devices, over_first(): return lax.ppermute(a, ('dp', 'tensor'), plane(n_dp, True, k))  5.14 us
    ppermute x6, waiting for transfers between devices, over_second(): return lax.ppermute(a, ('dp', 'tensor'), plane(n_dp, False, j))  3.15 us
  transfers between devices with their start and end apart: 23, of which 11 were waited for; matrix products, arithmetic and copies ran while one was open for 0% of the time, Pallas kernels for 34%

profile of v5, /device:TPU:0, one launch (start us, length us, event | category | flops | bytes accessed | tf_op | source)
XLA Modules:
  0.0 80.7 jit_solution(369970168781706177)
XLA Ops:
  0.6 1.6 %collective-permute-start = (bf16[256,256]{1,0:T(8,128)(2,1)}, bf16[256,256]{1,0:T(8,128)(2,1)S(1)}, u32[]{:S(2)}, u32[]{:S(2)}) collective-permute-start(bf16[256,256]{1,0:T(8,128)(2,1)} %refs_4_.1), channel_id=1, source_target_pairs={{0,1},{1,2},{2,3},{3,0},{4,5},{5,6},{6,7},{7,4},{8,9},{9,10},{10,1... | collective-permute-start | bytes 393224 | tf_op jit(solution)/shard_map/ppermute | solution.py:359
  2.3 2.7 %collective-permute-start.1 = (bf16[256,256]{1,0:T(8,128)(2,1)}, bf16[256,256]{1,0:T(8,128)(2,1)S(1)}, u32[]{:S(2)}, u32[]{:S(2)}) collective-permute-start(bf16[256,256]{1,0:T(8,128)(2,1)} %refs_4_.1), channel_id=1, source_target_pairs={{0,2},{1,3},{2,0},{3,1},{4,6},{5,7},{6,4},{7,5},{8,10},{9,11},{10,... | collective-permute-start | bytes 393224 | tf_op jit(solution)/shard_map/ppermute | solution.py:359
  5.0 1.4 %collective-permute-start.2 = (bf16[256,256]{1,0:T(8,128)(2,1)}, bf16[256,256]{1,0:T(8,128)(2,1)S(1)}, u32[]{:S(2)}, u32[]{:S(2)}) collective-permute-start(bf16[256,256]{1,0:T(8,128)(2,1)} %refs_4_.1), channel_id=1, source_target_pairs={{0,3},{1,0},{2,1},{3,2},{4,7},{5,4},{6,5},{7,6},{8,11},{9,8},{10,9... | collective-permute-start | bytes 393224 | tf_op jit(solution)/shard_map/ppermute | solution.py:359
  6.4 3.0 %shard_map.94 = (bf16[256,896]{1,0:T(8,128)(2,1)}, bf16[256,1792]{1,0:T(8,128)(2,1)}, bf16[128,256]{1,0:T(8,128)(2,1)}, bf16[256,256]{1,0:T(8,128)(2,1)}) custom-call(bf16[256,896]{1,0:T(8,128)(2,1)} %refs_0_.1, bf16[256,896]{1,0:T(8,128)(2,1)} %refs_1_.2, bf16[256,896]{1,0:T(8,128)(2,1)} %refs_2_.2, f32[64,896]{1,0:T(8,128)} %bitcast.5, ...), custom_call_target="tpu_custom_call" | custom-call | flops 3000000000 | tf_op jit(solution)/shard_map/pallas_call | solution.py:76
  9.5 1.0 %copy-done.3 = bf16[256,256]{1,0:T(8,128)(2,1)S(1)} copy-done((bf16[256,256]{1,0:T(8,128)(2,1)S(1)}, bf16[256,256]{1,0:T(8,128)(2,1)}, u32[]{:S(2)}) %copy-start.3) | copy-done | bytes 131096
  10.5 0.1 pad_add_fusion.refs_0_.pos
  10.7 1.6 %collective-permute-start.6 = (bf16[4,256,256]{2,1,0:T(8,128)(2,1)S(1)}, bf16[4,256,256]{2,1,0:T(8,128)(2,1)S(1)}, u32[]{:S(2)}, u32[]{:S(2)}) collective-permute-start(bf16[4,256,256]{2,1,0:T(8,128)(2,1)S(1)} %shard_map.96.refs_3_.refs_2_.refs_1_.refs_4_), channel_id=1, source_target_pairs={{0,4},{1,5},{2,6},{3,7},{4,8},{5,9},{6,10},{7,11},{8,12},{9,13},{1... | collective-permute-start | bytes 1572872 | tf_op jit(solution)/shard_map/ppermute | solution.py:362
  12.3 1.7 %collective-permute-start.7 = (bf16[4,256,256]{2,1,0:T(8,128)(2,1)S(1)}, bf16[4,256,256]{2,1,0:T(8,128)(2,1)S(1)}, u32[]{:S(2)}, u32[]{:S(2)}) collective-permute-start(bf16[4,256,256]{2,1,0:T(8,128)(2,1)S(1)} %shard_map.96.refs_3_.refs_2_.refs_1_.refs_4_), channel_id=1, source_target_pairs={{0,12},{1,13},{2,14},{3,15},{4,0},{5,1},{6,2},{7,3},{8,4},{9,5},{1... | collective-permute-start | bytes 1572872 | tf_op jit(solution)/shard_map/ppermute | solution.py:362
  14.0 2.0 %collective-permute-start.8 = (bf16[4,256,256]{2,1,0:T(8,128)(2,1)S(1)}, bf16[4,256,256]{2,1,0:T(8,128)(2,1)S(1)}, u32[]{:S(2)}, u32[]{:S(2)}) collective-permute-start(bf16[4,256,256]{2,1,0:T(8,128)(2,1)S(1)} %shard_map.96.refs_3_.refs_2_.refs_1_.refs_4_), channel_id=1, source_target_pairs={{0,8},{1,9},{2,10},{3,11},{4,12},{5,13},{6,14},{7,15},{8,0},{9,1},... | collective-permute-start | bytes 1572872 | tf_op jit(solution)/shard_map/ppermute | solution.py:362
  16.0 7.6 %shard_map.97 = (f32[64,4096]{1,0:T(8,128)S(1)}, bf16[64,4096]{1,0:T(8,128)(2,1)S(1)}, bf16[64,4096]{1,0:T(8,128)(2,1)S(1)}, bf16[64,4096]{1,0:T(8,128)(2,1)S(1)}) custom-call(bf16[256,1792]{1,0:T(8,128)(2,1)S(1)} %copy-done.2, bf16[4096,896]{1,0:T(8,128)(2,1)} %refs_1_.3, bf16[4096,896]{1,0:T(8,128)(2,1)} %refs_2_.3, ...), custom_call_target="tpu_custom_call" | custom-call | flops 7000000000 | tf_op jit(solution)/shard_map/pallas_call | solution.py:76
  23.5 0.9 %collective-permute-start.3 = (bf16[64,4096]{1,0:T(8,128)(2,1)S(1)}, bf16[64,4096]{1,0:T(8,128)(2,1)S(1)}, u32[]{:S(2)}, u32[]{:S(2)}) collective-permute-start(bf16[64,4096]{1,0:T(8,128)(2,1)S(1)} %get-tuple-element.25), channel_id=1, source_target_pairs={{0,1},{1,2},{2,3},{3,0},{4,5},{5,6},{6,7},{7,4},{8,9},{9,10},{10,1... | collective-permute-start | bytes 1572872 | tf_op jit(solution)/shard_map/ppermute | solution.py:359
  24.4 2.4 %collective-permute-start.4 = (bf16[64,4096]{1,0:T(8,128)(2,1)S(1)}, bf16[64,4096]{1,0:T(8,128)(2,1)S(1)}, u32[]{:S(2)}, u32[]{:S(2)}) collective-permute-start(bf16[64,4096]{1,0:T(8,128)(2,1)S(1)} %get-tuple-element.26), channel_id=1, source_target_pairs={{0,3},{1,0},{2,1},{3,2},{4,7},{5,4},{6,5},{7,6},{8,11},{9,8},{10,9... | collective-permute-start | bytes 1572872 | tf_op jit(solution)/shard_map/ppermute | solution.py:359
  26.8 0.7 collective-permute-start.5
  27.5 3.1 %collective-permute-done.8.refs_5_.refs_4_.refs_7_ = bf16[4,256,256]{2,1,0:T(8,128)(2,1)S(1)} collective-permute-done((bf16[4,256,256]{2,1,0:T(8,128)(2,1)S(1)}, bf16[4,256,256]{2,1,0:T(8,128)(2,1)S(1)}, u32[]{:S(2)}, u32[]{:S(2)}) %collective-permute-start.8) | collective-permute-done | bytes 524320 | tf_op jit(solution)/shard_map/ppermute | solution.py:362
  30.6 1.0 %shard_map.98 = (f32[8,64,256]{2,1,0:T(8,128)S(1)}, bf16[8,64,256]{2,1,0:T(8,128)(2,1)S(1)}) custom-call(s32[3]{0:T(128)S(1)} %pad_add_fusion.refs_0_.pos, bf16[128,256]{1,0:T(8,128)(2,1)S(1)} %copy-done.1, bf16[4,256,256]{2,1,0:T(8,128)(2,1)S(1)} %shard_map.96.refs_3_.refs_2_.refs_1_.refs_4_, ...), custom_call_target="tpu_custom_call" | custom-call | flops 1000000000 | tf_op jit(solution)/shard_map/pallas_call | solution.py:76
  31.7 0.1 collective-permute-start.9
  31.8 1.5 %collective-permute-done.9.refs_1_ = bf16[8,64,256]{2,1,0:T(8,128)(2,1)S(1)} collective-permute-done((bf16[8,64,256]{2,1,0:T(8,128)(2,1)S(1)}, bf16[8,64,256]{2,1,0:T(8,128)(2,1)S(1)}, u32[]{:S(2)}, u32[]{:S(2)}) %collective-permute-start.9) | collective-permute-done | bytes 262176 | tf_op jit(solution)/shard_map/ppermute | solution.py:368
  33.4 2.0 %collective-permute-start.13 = (bf16[8,64,256]{2,1,0:T(8,128)(2,1)S(1)}, bf16[8,64,256]{2,1,0:T(8,128)(2,1)S(1)}, u32[]{:S(2)}, u32[]{:S(2)}) collective-permute-start(bf16[8,64,256]{2,1,0:T(8,128)(2,1)S(1)} %shard_map.99.refs_5_.refs_0_), channel_id=1, source_target_pairs={{0,32},{16,112},{32,0},{48,80},{64,96},{80,48},{96,64},{112,16},{1... | collective-permute-start | bytes 786440 | tf_op jit(solution)/shard_map/ppermute | solution.py:365
  35.4 1.1 %shard_map.100.refs_4_.refs_6_ = bf16[16,256,256]{2,1,0:T(8,128)(2,1)S(1)} custom-call(s32[3]{0:T(128)S(1)} %pad_add_fusion.refs_0_.pos, bf16[4,256,256]{2,1,0:T(8,128)(2,1)S(1)} %shard_map.96.refs_3_.refs_2_.refs_1_.refs_4_, bf16[4,256,256]{2,1,0:T(8,128)(2,1)S(1)} %collective-permute-done.6.refs_3_.refs_2_.refs_5_, ...), custom_call_target="tpu_custom_call" | custom-call | flops 1000000000 | tf_op jit(solution)/shard_map/pallas_call | solution.py:76
  36.5 2.6 %collective-permute-done.4.refs_2_ = bf16[64,4096]{1,0:T(8,128)(2,1)S(1)} collective-permute-done((bf16[64,4096]{1,0:T(8,128)(2,1)S(1)}, bf16[64,4096]{1,0:T(8,128)(2,1)S(1)}, u32[]{:S(2)}, u32[]{:S(2)}) %collective-permute-start.4) | collective-permute-done | bytes 524320 | tf_op jit(solution)/shard_map/ppermute | solution.py:359
  39.2 0.9 %collective-permute-done.5.refs_3_ = bf16[64,4096]{1,0:T(8,128)(2,1)S(1)} collective-permute-done((bf16[64,4096]{1,0:T(8,128)(2,1)S(1)}, bf16[64,4096]{1,0:T(8,128)(2,1)S(1)}, u32[]{:S(2)}, u32[]{:S(2)}) %collective-permute-start.5) | collective-permute-done | bytes 524320 | tf_op jit(solution)/shard_map/ppermute | solution.py:359
  40.0 0.3 shard_map.101.refs_2_.refs_0_
  40.3 0.1 shard_map.102.refs_0_
  40.4 4.1 %collective-permute-start.14 = (bf16[8,64,256]{2,1,0:T(8,128)(2,1)S(1)}, bf16[8,64,256]{2,1,0:T(8,128)(2,1)S(1)}, u32[]{:S(2)}, u32[]{:S(2)}) collective-permute-start(bf16[8,64,256]{2,1,0:T(8,128)(2,1)S(1)} %shard_map.102.refs_0_), channel_id=1, source_target_pairs={{0,96},{16,48},{32,64},{48,16},{64,32},{80,112},{96,0},{112,80},{1... | collective-permute-start | bytes 786440 | tf_op jit(solution)/shard_map/ppermute | solution.py:365
  44.5 1.2 %collective-permute-start.10 = (bf16[64,4096]{1,0:T(8,128)(2,1)S(1)}, bf16[64,4096]{1,0:T(8,128)(2,1)S(1)}, u32[]{:S(2)}, u32[]{:S(2)}) collective-permute-start(bf16[64,4096]{1,0:T(8,128)(2,1)S(1)} %shard_map.101.refs_2_.refs_0_), channel_id=1, source_target_pairs={{0,4},{1,5},{2,6},{3,7},{4,8},{5,9},{6,10},{7,11},{8,12},{9,13},{1... | collective-permute-start | bytes 1572872 | tf_op jit(solution)/shard_map/ppermute | solution.py:362
  45.7 2.0 %collective-permute-start.11 = (bf16[64,4096]{1,0:T(8,128)(2,1)S(1)}, bf16[64,4096]{1,0:T(8,128)(2,1)S(1)}, u32[]{:S(2)}, u32[]{:S(2)}) collective-permute-start(bf16[64,4096]{1,0:T(8,128)(2,1)S(1)} %shard_map.101.refs_2_.refs_0_), channel_id=1, source_target_pairs={{0,12},{1,13},{2,14},{3,15},{4,0},{5,1},{6,2},{7,3},{8,4},{9,5},{1... | collective-permute-start | bytes 1572872 | tf_op jit(solution)/shard_map/ppermute | solution.py:362
  47.7 0.3 collective-permute-start.12
  48.1 0.8 collective-permute-done.14.refs_1_
  48.9 0.1 collective-permute-start.15
  49.0 1.5 %collective-permute-done.15.refs_2_ = bf16[8,64,256]{2,1,0:T(8,128)(2,1)S(1)} collective-permute-done((bf16[8,64,256]{2,1,0:T(8,128)(2,1)S(1)}, bf16[8,64,256]{2,1,0:T(8,128)(2,1)S(1)}, u32[]{:S(2)}, u32[]{:S(2)}) %collective-permute-start.15) | collective-permute-done | bytes 262176 | tf_op jit(solution)/shard_map/ppermute | solution.py:368
  50.5 1.9 %shard_map.104 = (bf16[16,64,256]{2,1,0:T(8,128)(2,1)S(1)}, f32[32,896]{1,0:T(8,128)S(1)}, f32[32,896]{1,0:T(8,128)S(1)}, f32[64,64]{1,0:T(8,128)S(1)}) custom-call(s32[3]{0:T(128)S(1)} %pad_add_fusion.refs_0_.pos, bf16[8,64,256]{2,1,0:T(8,128)(2,1)S(1)} %shard_map.103.refs_1_, bf16[8,64,256]{2,1,0:T(8,128)(2,1)S(1)} %collective-permute-done.15.refs_2_, ...), custom_call_target="tpu_custom_call" | custom-call | flops 100000000 | tf_op jit(solution)/shard_map/pallas_call | solution.py:76
  52.4 0.2 collective-permute-start.16
  52.6 1.2 %collective-permute-done.16.refs_1_ = f32[32,896]{1,0:T(8,128)S(1)} collective-permute-done((f32[32,896]{1,0:T(8,128)S(1)}, f32[32,896]{1,0:T(8,128)S(1)}, u32[]{:S(2)}, u32[]{:S(2)}) %collective-permute-start.16) | collective-permute-done | bytes 114720 | tf_op jit(solution)/shard_map/ppermute | solution.py:368
  53.8 0.1 collective-permute-start.17
  53.9 3.7 %shard_map.106.refs_2_.refs_0_ = f32[64,128]{1,0:T(8,128)S(1)} custom-call(f32[64,64]{1,0:T(8,128)S(1)} %get-tuple-element.34.refs_0_, f32[32,896]{1,0:T(8,128)S(1)} %shard_map.105.refs_1_.refs_0_), custom_call_target="tpu_custom_call" | custom-call | flops 300000000 | tf_op jit(solution)/shard_map/pallas_call | solution.py:76
  57.6 1.1 %collective-permute-done.17.refs_1_ = f32[32,896]{1,0:T(8,128)S(1)} collective-permute-done((f32[32,896]{1,0:T(8,128)S(1)}, f32[32,896]{1,0:T(8,128)S(1)}, u32[]{:S(2)}, u32[]{:S(2)}) %collective-permute-start.17) | collective-permute-done | bytes 114720 | tf_op jit(solution)/shard_map/ppermute | solution.py:365
  58.7 3.3 %collective-permute-start.21 = (f32[32,896]{1,0:T(8,128)S(1)}, f32[32,896]{1,0:T(8,128)S(1)}, u32[]{:S(2)}, u32[]{:S(2)}) collective-permute-start(f32[32,896]{1,0:T(8,128)S(1)} %shard_map.107.refs_4_.refs_0_), channel_id=1, source_target_pairs={{0,96},{16,48},{32,64},{48,16},{64,32},{80,112},{96,0},{112,80},{1... | collective-permute-start | bytes 344072 | tf_op jit(solution)/shard_map/ppermute | solution.py:365
  62.0 0.3 shard_map.108.refs_2_.refs_7_
  62.3 1.5 %collective-permute-start.18 = (bf16[64,4096]{1,0:T(8,128)(2,1)S(1)}, bf16[64,4096]{1,0:T(8,128)(2,1)S(1)}, u32[]{:S(2)}, u32[]{:S(2)}) collective-permute-start(bf16[64,4096]{1,0:T(8,128)(2,1)S(1)} %shard_map.108.refs_2_.refs_7_), channel_id=1, source_target_pairs={{0,2},{1,3},{2,0},{3,1},{4,6},{5,7},{6,4},{7,5},{8,10},{9,11},{10,... | collective-permute-start | bytes 1572872 | tf_op jit(solution)/shard_map/ppermute | solution.py:359
  63.8 2.3 %collective-permute-start.19 = (bf16[64,4096]{1,0:T(8,128)(2,1)S(1)}, bf16[64,4096]{1,0:T(8,128)(2,1)S(1)}, u32[]{:S(2)}, u32[]{:S(2)}) collective-permute-start(bf16[64,4096]{1,0:T(8,128)(2,1)S(1)} %shard_map.108.refs_2_.refs_7_), channel_id=1, source_target_pairs={{0,1},{1,2},{2,3},{3,0},{4,5},{5,6},{6,7},{7,4},{8,9},{9,10},{10,1... | collective-permute-start | bytes 1572872 | tf_op jit(solution)/shard_map/ppermute | solution.py:359
  66.0 1.0 %collective-permute-start.20 = (bf16[64,4096]{1,0:T(8,128)(2,1)S(1)}, bf16[64,4096]{1,0:T(8,128)(2,1)S(1)}, u32[]{:S(2)}, u32[]{:S(2)}) collective-permute-start(bf16[64,4096]{1,0:T(8,128)(2,1)S(1)} %shard_map.108.refs_2_.refs_7_), channel_id=1, source_target_pairs={{0,3},{1,0},{2,1},{3,2},{4,7},{5,4},{6,5},{7,6},{8,11},{9,8},{10,9... | collective-permute-start | bytes 1572872 | tf_op jit(solution)/shard_map/ppermute | solution.py:359
  67.0 1.7 %shard_map.109 = (f32[64,64]{1,0:T(8,128)S(1)}, bf16[16,256,128]{2,1,0:T(8,128)(2,1)S(1)}) custom-call(f32[64,128]{1,0:T(8,128)S(1)} %shard_map.106.refs_2_.refs_0_, bf16[16,64,256]{2,1,0:T(8,128)(2,1)S(1)} %get-tuple-element.35.refs_1_, bf16[64,4096]{1,0:T(8,128)(2,1)S(1)} %shard_map.108.refs_2_.refs_7_), custom_call_target="tpu_custom_call" | custom-call | flops 200000000 | tf_op jit(solution)/shard_map/pallas_call | solution.py:76
  68.8 0.1 collective-permute-start.22
  68.9 1.3 %collective-permute-done.22.refs_2_ = f32[32,896]{1,0:T(8,128)S(1)} collective-permute-done((f32[32,896]{1,0:T(8,128)S(1)}, f32[32,896]{1,0:T(8,128)S(1)}, u32[]{:S(2)}, u32[]{:S(2)}) %collective-permute-start.22) | collective-permute-done | bytes 114720 | tf_op jit(solution)/shard_map/ppermute | solution.py:368
  70.2 7.0 %shard_map.111 = (f32[64,896]{1,0:T(8,128)}, bf16[4096,896]{1,0:T(8,128)(2,1)}, bf16[256,4096]{1,0:T(8,128)(2,1)}) custom-call(s32[3]{0:T(128)S(1)} %pad_add_fusion.refs_0_.pos, f32[32,896]{1,0:T(8,128)S(1)} %shard_map.110.refs_1_, f32[32,896]{1,0:T(8,128)S(1)} %collective-permute-done.22.refs_2_, f32[64,64]{1,0:T(8,128)S(1)} %get-tuple-element.36.refs_2_.refs_3_, ...), custom_call_target="tpu_custom_call" | custom-call | flops 3600000000 | tf_op jit(solution)/shard_map/pallas_call | solution.py:308
  77.2 1.5 %collective-permute-done.19.refs_1_ = bf16[64,4096]{1,0:T(8,128)(2,1)S(1)} collective-permute-done((bf16[64,4096]{1,0:T(8,128)(2,1)S(1)}, bf16[64,4096]{1,0:T(8,128)(2,1)S(1)}, u32[]{:S(2)}, u32[]{:S(2)}) %collective-permute-start.19) | collective-permute-done | bytes 524320 | tf_op jit(solution)/shard_map/ppermute | solution.py:359
  78.7 0.2 collective-permute-done.20.refs_2_
  78.9 1.7 %shard_map.112 = bf16[256,4096]{1,0:T(8,128)(2,1)} custom-call(s32[3]{0:T(128)S(1)} %pad_add_fusion.refs_0_.pos, bf16[64,4096]{1,0:T(8,128)(2,1)S(1)} %collective-permute-done.18.refs_0_, bf16[64,4096]{1,0:T(8,128)(2,1)S(1)} %collective-permute-done.19.refs_1_, bf16[64,4096]{1,0:T(8,128)(2,1)S(1)} %collective-permute-done.20.refs_2_, ...), custom_call_target="tpu_custom_call", output_to_operand_aliasing={{}: (4, {})} | custom-call | flops 500000000 | tf_op jit(solution)/shard_map/pallas_call | solution.py:194
  (26 shorter events, 0.3 us)
Async XLA Ops:
  0.6 10.0 %collective-permute-start = (bf16[256,256]{1,0:T(8,128)(2,1)}, bf16[256,256]{1,0:T(8,128)(2,1)S(1)}, u32[]{:S(2)}, u32[]{:S(2)}) collective-permute-start(bf16[256,256]{1,0:T(8,128)(2,1)} %refs_4_.1), channel_id=1, source_target_pairs={{0,1},{1,2},{2,3},{3,0},{4,5},{5,6},{6,7},{7,4},{8,9},{9,10},{10,1... | collective-permute-start | bytes 393224 | tf_op jit(solution)/shard_map/ppermute | solution.py:359
  2.3 8.3 %collective-permute-start.1 = (bf16[256,256]{1,0:T(8,128)(2,1)}, bf16[256,256]{1,0:T(8,128)(2,1)S(1)}, u32[]{:S(2)}, u32[]{:S(2)}) collective-permute-start(bf16[256,256]{1,0:T(8,128)(2,1)} %refs_4_.1), channel_id=1, source_target_pairs={{0,2},{1,3},{2,0},{3,1},{4,6},{5,7},{6,4},{7,5},{8,10},{9,11},{10,... | collective-permute-start | bytes 393224 | tf_op jit(solution)/shard_map/ppermute | solution.py:359
  5.0 5.6 %collective-permute-start.2 = (bf16[256,256]{1,0:T(8,128)(2,1)}, bf16[256,256]{1,0:T(8,128)(2,1)S(1)}, u32[]{:S(2)}, u32[]{:S(2)}) collective-permute-start(bf16[256,256]{1,0:T(8,128)(2,1)} %refs_4_.1), channel_id=1, source_target_pairs={{0,3},{1,0},{2,1},{3,2},{4,7},{5,4},{6,5},{7,6},{8,11},{9,8},{10,9... | collective-permute-start | bytes 393224 | tf_op jit(solution)/shard_map/ppermute | solution.py:359
  9.5 6.5 %copy-start.2 = (bf16[256,1792]{1,0:T(8,128)(2,1)S(1)}, bf16[256,1792]{1,0:T(8,128)(2,1)}, u32[]{:S(2)}) copy-start(bf16[256,1792]{1,0:T(8,128)(2,1)} %get-tuple-element.22.refs_0_) | copy-start | bytes 2752516
  9.5 1.0 %copy-start.3 = (bf16[256,256]{1,0:T(8,128)(2,1)S(1)}, bf16[256,256]{1,0:T(8,128)(2,1)}, u32[]{:S(2)}) copy-start(bf16[256,256]{1,0:T(8,128)(2,1)} %get-tuple-element.23.refs_0_) | copy-start | bytes 393220
  10.7 16.2 %collective-permute-start.6 = (bf16[4,256,256]{2,1,0:T(8,128)(2,1)S(1)}, bf16[4,256,256]{2,1,0:T(8,128)(2,1)S(1)}, u32[]{:S(2)}, u32[]{:S(2)}) collective-permute-start(bf16[4,256,256]{2,1,0:T(8,128)(2,1)S(1)} %shard_map.96.refs_3_.refs_2_.refs_1_.refs_4_), channel_id=1, source_target_pairs={{0,4},{1,5},{2,6},{3,7},{4,8},{5,9},{6,10},{7,11},{8,12},{9,13},{1... | collective-permute-start | bytes 1572872 | tf_op jit(solution)/shard_map/ppermute | solution.py:362
  12.3 15.2 %collective-permute-start.7 = (bf16[4,256,256]{2,1,0:T(8,128)(2,1)S(1)}, bf16[4,256,256]{2,1,0:T(8,128)(2,1)S(1)}, u32[]{:S(2)}, u32[]{:S(2)}) collective-permute-start(bf16[4,256,256]{2,1,0:T(8,128)(2,1)S(1)} %shard_map.96.refs_3_.refs_2_.refs_1_.refs_4_), channel_id=1, source_target_pairs={{0,12},{1,13},{2,14},{3,15},{4,0},{5,1},{6,2},{7,3},{8,4},{9,5},{1... | collective-permute-start | bytes 1572872 | tf_op jit(solution)/shard_map/ppermute | solution.py:362
  14.0 16.7 %collective-permute-start.8 = (bf16[4,256,256]{2,1,0:T(8,128)(2,1)S(1)}, bf16[4,256,256]{2,1,0:T(8,128)(2,1)S(1)}, u32[]{:S(2)}, u32[]{:S(2)}) collective-permute-start(bf16[4,256,256]{2,1,0:T(8,128)(2,1)S(1)} %shard_map.96.refs_3_.refs_2_.refs_1_.refs_4_), channel_id=1, source_target_pairs={{0,8},{1,9},{2,10},{3,11},{4,12},{5,13},{6,14},{7,15},{8,0},{9,1},... | collective-permute-start | bytes 1572872 | tf_op jit(solution)/shard_map/ppermute | solution.py:362
  16.0 14.7 %copy-start.1 = (bf16[128,256]{1,0:T(8,128)(2,1)S(1)}, bf16[128,256]{1,0:T(8,128)(2,1)}, u32[]{:S(2)}) copy-start(bf16[128,256]{1,0:T(8,128)(2,1)} %get-tuple-element.28.refs_1_) | copy-start | bytes 196612
  23.5 13.0 %collective-permute-start.3 = (bf16[64,4096]{1,0:T(8,128)(2,1)S(1)}, bf16[64,4096]{1,0:T(8,128)(2,1)S(1)}, u32[]{:S(2)}, u32[]{:S(2)}) collective-permute-start(bf16[64,4096]{1,0:T(8,128)(2,1)S(1)} %get-tuple-element.25), channel_id=1, source_target_pairs={{0,1},{1,2},{2,3},{3,0},{4,5},{5,6},{6,7},{7,4},{8,9},{9,10},{10,1... | collective-permute-start | bytes 1572872 | tf_op jit(solution)/shard_map/ppermute | solution.py:359
  24.4 14.8 %collective-permute-start.4 = (bf16[64,4096]{1,0:T(8,128)(2,1)S(1)}, bf16[64,4096]{1,0:T(8,128)(2,1)S(1)}, u32[]{:S(2)}, u32[]{:S(2)}) collective-permute-start(bf16[64,4096]{1,0:T(8,128)(2,1)S(1)} %get-tuple-element.26), channel_id=1, source_target_pairs={{0,3},{1,0},{2,1},{3,2},{4,7},{5,4},{6,5},{7,6},{8,11},{9,8},{10,9... | collective-permute-start | bytes 1572872 | tf_op jit(solution)/shard_map/ppermute | solution.py:359
  26.8 13.2 %collective-permute-start.5 = (bf16[64,4096]{1,0:T(8,128)(2,1)S(1)}, bf16[64,4096]{1,0:T(8,128)(2,1)S(1)}, u32[]{:S(2)}, u32[]{:S(2)}) collective-permute-start(bf16[64,4096]{1,0:T(8,128)(2,1)S(1)} %get-tuple-element.27), channel_id=1, source_target_pairs={{0,2},{1,3},{2,0},{3,1},{4,6},{5,7},{6,4},{7,5},{8,10},{9,11},{10,... | collective-permute-start | bytes 1572872 | tf_op jit(solution)/shard_map/ppermute | solution.py:359
  31.7 18.8 %copy-start = (bf16[256,896]{1,0:T(8,128)(2,1)S(1)}, bf16[256,896]{1,0:T(8,128)(2,1)}, u32[]{:S(2)}) copy-start(bf16[256,896]{1,0:T(8,128)(2,1)} %get-tuple-element.31.refs_3_.refs_4_) | copy-start | bytes 1376260
  31.7 1.6 %collective-permute-start.9 = (bf16[8,64,256]{2,1,0:T(8,128)(2,1)S(1)}, bf16[8,64,256]{2,1,0:T(8,128)(2,1)S(1)}, u32[]{:S(2)}, u32[]{:S(2)}) collective-permute-start(bf16[8,64,256]{2,1,0:T(8,128)(2,1)S(1)} %get-tuple-element.30), channel_id=1, source_target_pairs={{0,16},{16,0},{32,48},{48,32},{64,80},{80,64},{96,112},{112,96},{1... | collective-permute-start | bytes 786440 | tf_op jit(solution)/shard_map/ppermute | solution.py:368
  33.4 6.9 %collective-permute-start.13 = (bf16[8,64,256]{2,1,0:T(8,128)(2,1)S(1)}, bf16[8,64,256]{2,1,0:T(8,128)(2,1)S(1)}, u32[]{:S(2)}, u32[]{:S(2)}) collective-permute-start(bf16[8,64,256]{2,1,0:T(8,128)(2,1)S(1)} %shard_map.99.refs_5_.refs_0_), channel_id=1, source_target_pairs={{0,32},{16,112},{32,0},{48,80},{64,96},{80,48},{96,64},{112,16},{1... | collective-permute-start | bytes 786440 | tf_op jit(solution)/shard_map/ppermute | solution.py:365
  40.4 8.5 %collective-permute-start.14 = (bf16[8,64,256]{2,1,0:T(8,128)(2,1)S(1)}, bf16[8,64,256]{2,1,0:T(8,128)(2,1)S(1)}, u32[]{:S(2)}, u32[]{:S(2)}) collective-permute-start(bf16[8,64,256]{2,1,0:T(8,128)(2,1)S(1)} %shard_map.102.refs_0_), channel_id=1, source_target_pairs={{0,96},{16,48},{32,64},{48,16},{64,32},{80,112},{96,0},{112,80},{1... | collective-permute-start | bytes 786440 | tf_op jit(solution)/shard_map/ppermute | solution.py:365
  44.5 17.5 %collective-permute-start.10 = (bf16[64,4096]{1,0:T(8,128)(2,1)S(1)}, bf16[64,4096]{1,0:T(8,128)(2,1)S(1)}, u32[]{:S(2)}, u32[]{:S(2)}) collective-permute-start(bf16[64,4096]{1,0:T(8,128)(2,1)S(1)} %shard_map.101.refs_2_.refs_0_), channel_id=1, source_target_pairs={{0,4},{1,5},{2,6},{3,7},{4,8},{5,9},{6,10},{7,11},{8,12},{9,13},{1... | collective-permute-start | bytes 1572872 | tf_op jit(solution)/shard_map/ppermute | solution.py:362
  45.7 16.3 %collective-permute-start.11 = (bf16[64,4096]{1,0:T(8,128)(2,1)S(1)}, bf16[64,4096]{1,0:T(8,128)(2,1)S(1)}, u32[]{:S(2)}, u32[]{:S(2)}) collective-permute-start(bf16[64,4096]{1,0:T(8,128)(2,1)S(1)} %shard_map.101.refs_2_.refs_0_), channel_id=1, source_target_pairs={{0,12},{1,13},{2,14},{3,15},{4,0},{5,1},{6,2},{7,3},{8,4},{9,5},{1... | collective-permute-start | bytes 1572872 | tf_op jit(solution)/shard_map/ppermute | solution.py:362
  47.7 14.3 %collective-permute-start.12 = (bf16[64,4096]{1,0:T(8,128)(2,1)S(1)}, bf16[64,4096]{1,0:T(8,128)(2,1)S(1)}, u32[]{:S(2)}, u32[]{:S(2)}) collective-permute-start(bf16[64,4096]{1,0:T(8,128)(2,1)S(1)} %shard_map.101.refs_2_.refs_0_), channel_id=1, source_target_pairs={{0,8},{1,9},{2,10},{3,11},{4,12},{5,13},{6,14},{7,15},{8,0},{9,1},... | collective-permute-start | bytes 1572872 | tf_op jit(solution)/shard_map/ppermute | solution.py:362
  48.9 1.6 %collective-permute-start.15 = (bf16[8,64,256]{2,1,0:T(8,128)(2,1)S(1)}, bf16[8,64,256]{2,1,0:T(8,128)(2,1)S(1)}, u32[]{:S(2)}, u32[]{:S(2)}) collective-permute-start(bf16[8,64,256]{2,1,0:T(8,128)(2,1)S(1)} %shard_map.103.refs_1_), channel_id=1, source_target_pairs={{0,16},{16,0},{32,48},{48,32},{64,80},{80,64},{96,112},{112,96},{1... | collective-permute-start | bytes 786440 | tf_op jit(solution)/shard_map/ppermute | solution.py:368
  52.4 1.4 %collective-permute-start.16 = (f32[32,896]{1,0:T(8,128)S(1)}, f32[32,896]{1,0:T(8,128)S(1)}, u32[]{:S(2)}, u32[]{:S(2)}) collective-permute-start(f32[32,896]{1,0:T(8,128)S(1)} %get-tuple-element.33), channel_id=1, source_target_pairs={{0,16},{16,0},{32,48},{48,32},{64,80},{80,64},{96,112},{112,96},{1... | collective-permute-start | bytes 344072 | tf_op jit(solution)/shard_map/ppermute | solution.py:368
  53.8 4.9 %collective-permute-start.17 = (f32[32,896]{1,0:T(8,128)S(1)}, f32[32,896]{1,0:T(8,128)S(1)}, u32[]{:S(2)}, u32[]{:S(2)}) collective-permute-start(f32[32,896]{1,0:T(8,128)S(1)} %shard_map.105.refs_1_.refs_0_), channel_id=1, source_target_pairs={{0,32},{16,112},{32,0},{48,80},{64,96},{80,48},{96,64},{112,16},{1... | collective-permute-start | bytes 344072 | tf_op jit(solution)/shard_map/ppermute | solution.py:365
  58.7 10.0 %collective-permute-start.21 = (f32[32,896]{1,0:T(8,128)S(1)}, f32[32,896]{1,0:T(8,128)S(1)}, u32[]{:S(2)}, u32[]{:S(2)}) collective-permute-start(f32[32,896]{1,0:T(8,128)S(1)} %shard_map.107.refs_4_.refs_0_), channel_id=1, source_target_pairs={{0,96},{16,48},{32,64},{48,16},{64,32},{80,112},{96,0},{112,80},{1... | collective-permute-start | bytes 344072 | tf_op jit(solution)/shard_map/ppermute | solution.py:365
  62.3 14.9 %collective-permute-start.18 = (bf16[64,4096]{1,0:T(8,128)(2,1)S(1)}, bf16[64,4096]{1,0:T(8,128)(2,1)S(1)}, u32[]{:S(2)}, u32[]{:S(2)}) collective-permute-start(bf16[64,4096]{1,0:T(8,128)(2,1)S(1)} %shard_map.108.refs_2_.refs_7_), channel_id=1, source_target_pairs={{0,2},{1,3},{2,0},{3,1},{4,6},{5,7},{6,4},{7,5},{8,10},{9,11},{10,... | collective-permute-start | bytes 1572872 | tf_op jit(solution)/shard_map/ppermute | solution.py:359
  63.8 14.9 %collective-permute-start.19 = (bf16[64,4096]{1,0:T(8,128)(2,1)S(1)}, bf16[64,4096]{1,0:T(8,128)(2,1)S(1)}, u32[]{:S(2)}, u32[]{:S(2)}) collective-permute-start(bf16[64,4096]{1,0:T(8,128)(2,1)S(1)} %shard_map.108.refs_2_.refs_7_), channel_id=1, source_target_pairs={{0,1},{1,2},{2,3},{3,0},{4,5},{5,6},{6,7},{7,4},{8,9},{9,10},{10,1... | collective-permute-start | bytes 1572872 | tf_op jit(solution)/shard_map/ppermute | solution.py:359
  66.0 12.8 %collective-permute-start.20 = (bf16[64,4096]{1,0:T(8,128)(2,1)S(1)}, bf16[64,4096]{1,0:T(8,128)(2,1)S(1)}, u32[]{:S(2)}, u32[]{:S(2)}) collective-permute-start(bf16[64,4096]{1,0:T(8,128)(2,1)S(1)} %shard_map.108.refs_2_.refs_7_), channel_id=1, source_target_pairs={{0,3},{1,0},{2,1},{3,2},{4,7},{5,4},{6,5},{7,6},{8,11},{9,8},{10,9... | collective-permute-start | bytes 1572872 | tf_op jit(solution)/shard_map/ppermute | solution.py:359
  68.8 1.4 %collective-permute-start.22 = (f32[32,896]{1,0:T(8,128)S(1)}, f32[32,896]{1,0:T(8,128)S(1)}, u32[]{:S(2)}, u32[]{:S(2)}) collective-permute-start(f32[32,896]{1,0:T(8,128)S(1)} %shard_map.110.refs_1_), channel_id=1, source_target_pairs={{0,16},{16,0},{32,48},{48,32},{64,80},{80,64},{96,112},{112,96},{1... | collective-permute-start | bytes 344072 | tf_op jit(solution)/shard_map/ppermute | solution.py:368
